TPU v7x, 128 devices: a whole 4x4x4 slice. The times are simulated.
128 devices in a mesh: az: 16 (over x_hi, y, core), rg: 8 (over z, x_lo).
Axes of the slice: x: 4 (x_hi: 2, x_lo: 2; x = x_hi * 2 + x_lo), y: 4, z: 4, core: 2. Of those that a mesh axis runs over, the one named last changes fastest.
Arguments:
- reference_slc: bfloat16 [2, 1536, 24576], P(None, 'az', 'rg'), may hold values from -6 to 6
- secondary_slc: bfloat16 [2, 1536, 24576], P(None, 'az', 'rg'), may hold values from -6 to 6
- chip_offsets: int32 [2, 16, 768], P(None, 'az', 'rg'), may hold values from -80 to 80, as said below
- src_row: int32 [1536], replicated, may hold values from 0 to 1535, as said below
- line_owner: int32 [1536], replicated, may hold values from 0 to 127, as said below
- band_start: int32 [24576], replicated, may hold values from -64 to 24631, as said below
- band_taps: bfloat16 [8, 24576], replicated, may hold values from -2.09375 to 2.09375
Outputs:
- est_offsets: float32 [2, 16, 768], P(None, 'az', 'rg')
- resampled: bfloat16 [2, 4096, 24576], P(None, ('az', 'rg'))
Inputs may be any that keep to these rules, and one draw needn't show every extreme that they name: chip_offsets[0] lies within -80 and 80, chip_offsets[1] within -48 and 48. `src_row`: the source row of line i lies within 8 rows of i. `line_owner`: for every owner and every azimuth tile, at most 2 lines of that owner take their source rows from that tile, and an owner holds at most 32 lines; both bounds are met in every draw. band_start[j] lies within j - 64 and j + 56.
All inputs are finite; a program needn't handle non-finite values.
Results may differ from a plain program's by a relative error of at most 0.008.
Values may be sent and summed in bfloat16 or wider, within the bound.
No kernel may reach another device: no remote copies, remote signals or barrier semaphores. Data moves between devices by JAX's collectives and lax.ppermute only.
A program may use at most 128 MiB of HBM per device.

v0:
```python
import functools
import math

import jax
import jax.numpy as jnp
import ml_dtypes
import numpy as np
from jax import lax
from jax.experimental import pallas as pl
from jax.experimental.pallas import tpu as pltpu
from jax.sharding import PartitionSpec as P

CHIP_LEN = 64
OVERSAMPLE = 16
LAG_COUNT = 48
TAP_COUNT = 8
SPACING = 32
MARGIN = 64
PHASE_RATE = 2.0
EPS = 1e-06

TILES = 16
PIECES = 8
OWNERS = 128
LINES = 96
COLS = 3072
ALL_LINES = 1536
CHIPS = 96
PAIRS = CHIPS // 2
OWNER_CAP = 32
FIRST_ROW = 16
ROWS = LINES + 2 * MARGIN
WINDOWS = COLS // 128 + 2
HALF = WINDOWS // 2
WIDTH = HALF * 128
LINE_SPAN = 256
SCRATCH_BLOCKS = 27
GROUP = 4
BOTH = ("az", "rg")
BF = jnp.bfloat16
F32 = jnp.float32


def numpy_tables():
    ids = np.arange(CHIP_LEN)
    angles = -2.0 * math.pi / CHIP_LEN * (ids[:, None] * ids[None, :] % CHIP_LEN)
    scale = 1.0 / math.sqrt(CHIP_LEN)

    def low(values):
        return values.astype(np.float32).astype(ml_dtypes.bfloat16).astype(np.float32)

    four = (low(np.cos(angles) * scale), low(np.sin(angles) * scale))
    steps = np.arange(LAG_COUNT) - LAG_COUNT // 2
    freq = np.where(ids < CHIP_LEN // 2, ids, ids - CHIP_LEN)
    turns = steps[:, None] * freq[None, :] % (OVERSAMPLE * CHIP_LEN)
    lifted = 2.0 * math.pi / (OVERSAMPLE * CHIP_LEN) * turns
    lift = (low(np.cos(lifted) * scale), low(np.sin(lifted) * scale))
    return four, lift


def kernel_tables():
    four, lift = numpy_tables()

    def stacked(re, im):
        return np.block([[re, -im], [im, re]])

    def paired(re, im, starts):
        out = np.zeros((2, 128, 2, 2, 64), np.float32)
        count = re.shape[0]
        for chip, first in enumerate(starts):
            rows = slice(first, first + CHIP_LEN)
            out[0, rows, 0, chip, :count] = re.T
            out[0, rows, 1, chip, :count] = im.T
            out[1, rows, 0, chip, :count] = -im.T
            out[1, rows, 1, chip, :count] = re.T
        return out.reshape(256, 256)

    return tuple(
        jnp.asarray(t.astype(ml_dtypes.bfloat16))
        for t in (
            stacked(*four),
            paired(*four, (0, 32)),
            paired(*four, (0, 64)),
            paired(*lift, (0, 64)),
            stacked(*lift),
        )
    )


def iota(shape, dim):
    return lax.broadcasted_iota(jnp.int32, shape, dim)


def pack_kernel(
    place_ref, sec_ref, start_ref, taps_ref, src_ref, own_ref, out_ref, shift_ref, res_ref, pick_ref
):
    az = place_ref[0]
    rg = place_ref[1]

    line_first = jnp.minimum(jnp.maximum(az * LINES - 8, 0) // 128 * 128, ALL_LINES - LINE_SPAN)
    span = pl.ds(pl.multiple_of(line_first, 128), LINE_SPAN)
    local = src_ref[:, span] - az * LINES
    owner = own_ref[:, span]
    here = (local >= 0) & (local < LINES)
    tagged = jnp.where(here, owner, -1).astype(F32)
    tagged_col = jnp.transpose(jnp.broadcast_to(tagged, (128, LINE_SPAN)))
    tagged_col = jnp.concatenate([tagged_col, tagged_col], axis=1)
    square = (LINE_SPAN, LINE_SPAN)
    earlier = iota(square, 0) < iota(square, 1)
    same = (tagged_col == tagged) & earlier
    rank = jnp.sum(jnp.where(same, 1.0, 0.0), axis=0, keepdims=True)
    slot = jnp.where(here, tagged * 2.0 + rank, -1.0)
    marked = jnp.where(here, local + 1, 0).astype(F32)
    marked_col = jnp.transpose(jnp.broadcast_to(marked, (128, LINE_SPAN))).astype(BF)
    for first in range(0, 1024, 256):
        ids = iota((256, LINE_SPAN), 0) + first
        wanted = ((ids >> 3) * 2 + ((ids >> 1) & 1)).astype(F32)
        hot = jnp.where(slot == wanted, 1.0, 0.0).astype(BF)
        found = jnp.dot(hot, marked_col, preferred_element_type=F32).astype(jnp.int32)
        ids = iota((256, 128), 0) + first
        base = ((ids >> 2) & 1) * (2 * LINES) + (ids & 1) * LINES - 1
        target = jnp.where(found > 0, found + base, -1)
        for block in range(3):
            lanes = iota((256, 128), 1) + block * 128
            pick_ref[first : first + 256, block * 128 : (block + 1) * 128] = jnp.where(
                lanes == target, 1.0, 0.0
            ).astype(BF)

    lane = iota((2 * LINES, 128), 1)
    none = jnp.zeros((2 * LINES, 128), F32)
    shift_ref[:, 0:128] = none.astype(BF)
    shift_ref[:, 26 * 128 : 27 * 128] = none.astype(BF)

    def moved(left, right):
        return pltpu.roll(jnp.where(lane >= 64, left, right), 64, 1).astype(BF)

    shift_ref[:, 128:256] = moved(none, sec_ref[:, 0:128].astype(F32))
    shift_ref[:, 25 * 128 : 26 * 128] = moved(sec_ref[:, COLS - 128 : COLS].astype(F32), none)

    def move(block, carry):
        at = pl.multiple_of(block * 128, 128)
        left = sec_ref[:, pl.ds(pl.multiple_of(at - 128, 128), 128)].astype(F32)
        right = sec_ref[:, pl.ds(at, 128)].astype(F32)
        shift_ref[:, pl.ds(pl.multiple_of(at + 128, 128), 128)] = moved(left, right)
        return carry

    lax.fori_loop(1, COLS // 128, move, 0)

    tap_row = iota((256, 128), 0)
    for half in range(2):

        def window(step, carry):
            at = step + half * HALF
            block = jnp.clip(rg * (COLS // 128) + at - 1, 0, PIECES * (COLS // 128) - 1)
            start = start_ref[pl.ds(block, 1), :] - block * 128 + MARGIN
            taps = taps_ref[:, pl.ds(pl.multiple_of(block * 128, 128), 128)].astype(F32)
            offset = tap_row - start
            band = jnp.zeros((256, 128), F32)
            for tap in range(TAP_COUNT):
                band = jnp.where(offset == tap, taps[tap : tap + 1, :], band)
            lines = shift_ref[:, pl.ds(pl.multiple_of(at * 128, 128), 256)]
            summed = jnp.dot(lines, band.astype(BF), preferred_element_type=F32)
            res_ref[
                half * 2 * LINES : (half + 1) * 2 * LINES,
                pl.ds(pl.multiple_of(step * 128, 128), 128),
            ] = summed.astype(BF)
            return carry

        lax.fori_loop(0, HALF, window, 0)

    def send(step, carry):
        at = pl.ds(pl.multiple_of(step * 128, 128), 128)
        out_ref[:, at] = jnp.dot(
            pick_ref[...], res_ref[:, at], preferred_element_type=F32
        ).astype(BF)
        return carry

    lax.fori_loop(0, HALF, send, 0)


def pack_lines(place, sec, starts, taps, src, own):
    smem = pl.BlockSpec(memory_space=pltpu.SMEM)
    vmem = pl.BlockSpec(memory_space=pltpu.VMEM)
    return pl.pallas_call(
        pack_kernel,
        out_shape=jax.ShapeDtypeStruct((OWNERS * 8, WIDTH), BF),
        in_specs=[smem] + [vmem] * 5,
        out_specs=vmem,
        scratch_shapes=[
            pltpu.VMEM((2 * LINES, SCRATCH_BLOCKS * 128), BF),
            pltpu.VMEM((4 * LINES, WIDTH), BF),
            pltpu.VMEM((OWNERS * 8, 4 * LINES), BF),
        ],
        compiler_params=pltpu.CompilerParams(vmem_limit_bytes=40 * 2**20),
        cost_estimate=pl.CostEstimate(
            flops=2 * 10**9, bytes_accessed=6 * 10**6, transcendentals=0
        ),
        name="pack_lines",
    )(place, sec, starts, taps, src, own)


def estimate_kernel(
    off_ref,
    offv_ref,
    ref_ref,
    sec_ref,
    up_ref,
    down_ref,
    left_ref,
    right_ref,
    fwd_ref,
    wref_ref,
    wsec_ref,
    wlift_ref,
    lift_ref,
    est_ref,
    msg_ref,
    rcols_ref,
    scols_ref,
    chips_ref,
    half_ref,
    tot_ref,
    mom_ref,
):
    for part in range(2):
        rows = slice(part * CHIP_LEN, (part + 1) * CHIP_LEN)
        rcols_ref[rows, 0:128] = left_ref[part, 0:CHIP_LEN, :]
        rcols_ref[rows, 128 : 128 + COLS] = ref_ref[part, FIRST_ROW : FIRST_ROW + CHIP_LEN, :]
        rcols_ref[rows, 128 + COLS : 256 + COLS] = right_ref[part, 0:CHIP_LEN, :]
        rows = slice(part * ROWS, (part + 1) * ROWS)
        scols_ref[0, rows, :] = left_ref[part, CHIP_LEN:, :].astype(F32)
        scols_ref[SCRATCH_BLOCKS - 2, rows, :] = right_ref[part, CHIP_LEN:, :].astype(F32)
        scols_ref[SCRATCH_BLOCKS - 1, rows, :] = jnp.zeros((ROWS, 128), F32)

    def widen(block, carry):
        at = pl.ds(pl.multiple_of(block * 128, 128), 128)
        to = block + 1
        for part in range(2):
            base = part * ROWS
            own = base + MARGIN
            scols_ref[to, base:own, :] = up_ref[part, :, at].astype(F32)
            scols_ref[to, own : own + LINES, :] = sec_ref[part, :, at].astype(F32)
            scols_ref[to, own + LINES : base + ROWS, :] = down_ref[part, :, at].astype(F32)
        return carry

    lax.fori_loop(0, COLS // 128, widen, 0)

    lane = iota((CHIP_LEN, 128), 1)
    lane_all = iota((2 * CHIP_LEN, 128), 1)

    def cut(pair, carry):
        col = pair * 64 + 112
        at = pl.multiple_of((col >> 7) * 128, 128)
        turn = col & 127
        near = rcols_ref[:, pl.ds(at, 128)].astype(F32)
        far = rcols_ref[:, pl.ds(pl.multiple_of(at + 128, 128), 128)].astype(F32)
        both = pltpu.roll(jnp.where(lane_all >= turn, near, far), (128 - turn) & 127, 1)
        to = pl.multiple_of(pair * 128, 128)
        chips_ref[:, pl.ds(to, 128)] = both.astype(BF)
        for part in range(2):
            found = []
            for side in range(2):
                chip = pair * 2 + side
                row = off_ref[0, chip] + (FIRST_ROW + MARGIN + part * ROWS)
                col = chip * SPACING + off_ref[1, chip] + 112
                block = col >> 7
                turn = col & 127
                near = scols_ref[block, pl.ds(row, CHIP_LEN), :]
                far = scols_ref[block + 1, pl.ds(row, CHIP_LEN), :]
                found.append(
                    pltpu.roll(
                        jnp.where(lane >= turn, near, far), (128 + side * 64 - turn) & 127, 1
                    )
                )
            chips_ref[
                part * CHIP_LEN : (part + 1) * CHIP_LEN,
                pl.ds(pl.multiple_of(to + CHIPS * 64, 128), 128),
            ] = jnp.where(lane < 64, found[0], found[1]).astype(BF)
        return carry

    lax.fori_loop(0, PAIRS, cut, 0)

    def first_pass(step, carry):
        at = pl.ds(pl.multiple_of(step * 512, 512), 512)
        half_ref[:, at] = jnp.dot(
            fwd_ref[...], chips_ref[:, at], preferred_element_type=F32
        ).astype(BF)
        return carry

    lax.fori_loop(0, CHIPS * 128 // 512, first_pass, 0)

    lag_row = (iota((LAG_COUNT, 128), 0) - LAG_COUNT // 2).astype(F32) / OVERSAMPLE

    def correlate(step, carry):
        def gathered(base):
            rows = []
            for member in range(GROUP):
                at = pl.ds(pl.multiple_of(base + (step * GROUP + member) * 128, 128), 128)
                rows.append(
                    jnp.concatenate(
                        [half_ref[0:CHIP_LEN, at], half_ref[CHIP_LEN : 2 * CHIP_LEN, at]], axis=1
                    )
                )
            return jnp.concatenate(rows, axis=0)

        spec_ref = jnp.dot(gathered(0), wref_ref[...], preferred_element_type=F32)
        spec_sec = jnp.dot(gathered(CHIPS * 64), wsec_ref[...], preferred_element_type=F32)
        rr, ri = spec_ref[:, :128], spec_ref[:, 128:]
        sr, si = spec_sec[:, :128], spec_sec[:, 128:]
        cross = jnp.concatenate([rr * sr + ri * si, ri * sr - rr * si], axis=1).astype(BF)
        middle = jnp.dot(cross, wlift_ref[...], preferred_element_type=F32).astype(BF)
        columns = [
            jnp.concatenate(
                [
                    middle[m * CHIP_LEN : (m + 1) * CHIP_LEN, :128],
                    middle[m * CHIP_LEN : (m + 1) * CHIP_LEN, 128:],
                ],
                axis=0,
            )
            for m in range(GROUP)
        ]
        corr = jnp.dot(
            lift_ref[...], jnp.concatenate(columns, axis=1), preferred_element_type=F32
        )
        for m in range(GROUP):
            re = corr[:LAG_COUNT, m * 128 : (m + 1) * 128]
            im = corr[LAG_COUNT:, m * 128 : (m + 1) * 128]
            energy = re * re + im * im
            weight = energy * energy
            row = pl.ds(step * GROUP + m, 1)
            tot_ref[row, :] = jnp.sum(weight, axis=0, keepdims=True)
            mom_ref[row, :] = jnp.sum(weight * lag_row, axis=0, keepdims=True)
        return carry

    lax.fori_loop(0, PAIRS // GROUP, correlate, 0)

    wide = (PAIRS, 128)
    lanes = iota(wide, 1)
    total = tot_ref[...]
    moment = mom_ref[...]
    lag_lane = ((lanes & 63) - LAG_COUNT // 2).astype(F32) / OVERSAMPLE
    sides = []
    for side in range(2):
        mask = (lanes < 64) if side == 0 else (lanes >= 64)

        def over(values):
            return jnp.sum(jnp.where(mask, values, 0.0), axis=1, keepdims=True)

        whole = over(total) + EPS
        sides.append((over(moment) / whole, over(total * lag_lane) / whole))
    own = (lanes >> 1) == iota(wide, 0)
    even = (lanes & 1) == 0

    def spread(which):
        values = jnp.where(even, sides[0][which], sides[1][which])
        return jnp.sum(jnp.where(own, values, 0.0), axis=0, keepdims=True)

    offsets = offv_ref[...].astype(F32)
    est_az = offsets[0:1, :] + spread(0)
    est_rg = offsets[1:2, :] + spread(1)
    est_ref[0:1, :] = est_az
    est_ref[1:2, :] = est_rg
    angle = PHASE_RATE * est_az
    cosine = jnp.cos(angle)
    sine = jnp.sin(angle)
    cos_hi = cosine.astype(BF).astype(F32)
    sin_hi = sine.astype(BF).astype(F32)
    kind = iota((8, 128), 0)
    message = jnp.where(
        kind == 0,
        cos_hi,
        jnp.where(
            kind == 1,
            cosine - cos_hi,
            jnp.where(kind == 2, sin_hi, jnp.where(kind == 3, sine - sin_hi, 0.0)),
        ),
    ).astype(BF)
    for owner in range(OWNERS):
        msg_ref[owner] = message


def estimate(off, offv, ref, sec, up, down, left, right):
    smem = pl.BlockSpec(memory_space=pltpu.SMEM)
    vmem = pl.BlockSpec(memory_space=pltpu.VMEM)
    return pl.pallas_call(
        estimate_kernel,
        out_shape=(
            jax.ShapeDtypeStruct((2, 128), F32),
            jax.ShapeDtypeStruct((OWNERS, 8, 128), BF),
        ),
        in_specs=[smem] + [vmem] * 12,
        out_specs=(vmem, vmem),
        scratch_shapes=[
            pltpu.VMEM((2 * CHIP_LEN, SCRATCH_BLOCKS * 128), BF),
            pltpu.VMEM((SCRATCH_BLOCKS, 2 * ROWS, 128), F32),
            pltpu.VMEM((2 * CHIP_LEN, CHIPS * 128), BF),
            pltpu.VMEM((2 * CHIP_LEN, CHIPS * 128), BF),
            pltpu.VMEM((PAIRS, 128), F32),
            pltpu.VMEM((PAIRS, 128), F32),
        ],
        compiler_params=pltpu.CompilerParams(vmem_limit_bytes=48 * 2**20),
        cost_estimate=pl.CostEstimate(
            flops=6 * 10**9, bytes_accessed=20 * 10**6, transcendentals=0
        ),
        name="estimate",
    )(off, offv, ref, sec, up, down, left, right, *kernel_tables())


def place_kernel(pick_ref, sel_ref, msg_ref, arr_ref, prev_ref, next_ref, out_ref):
    piece = pl.program_id(0)
    pick = pick_ref[...]
    turned = jnp.dot(sel_ref[...], msg_ref[...].reshape(128, 128), preferred_element_type=F32)
    cos_all = turned[0:32] + turned[32:64]
    sin_all = turned[64:96] + turned[96:128]
    lane = iota((OWNER_CAP, 128), 1)

    def moved(block_ref, first, last):
        return jnp.dot(
            pick, block_ref[:, 0, :, first:last].reshape(128, last - first),
            preferred_element_type=F32,
        )

    def write(block, lines):
        chip = block * 4 + (lane >> 5)
        cosine = jnp.take_along_axis(cos_all, chip, axis=1)
        sine = jnp.take_along_axis(sin_all, chip, axis=1)
        re, im = lines[:OWNER_CAP], lines[OWNER_CAP:]
        at = slice(block * 128, (block + 1) * 128)
        out_ref[0, :, at] = (re * cosine + im * sine).astype(BF)
        out_ref[1, :, at] = (im * cosine - re * sine).astype(BF)

    before = jnp.where(piece > 0, moved(prev_ref, 0, 128)[64:], 0.0)
    after = jnp.where(piece < PIECES - 1, moved(next_ref, 0, 128)[:64], 0.0)
    for first in range(0, HALF, 2):
        last = min(first + 2, HALF)
        lines = moved(arr_ref, first * 128, last * 128)
        for at in range(first, last):
            cols = slice((at - first) * 128, (at - first + 1) * 128)
            if at >= 1:
                low = lines[:64, cols]
                write(at - 1, low + before if at == 1 else low)
            if at < HALF - 1:
                high = lines[64:, cols]
                write(HALF - 1 + at, high + after if at == HALF - 2 else high)


def place_lines(pick, sel, message, arrived):
    same = pl.BlockSpec((128, 128), lambda r: (0, 0))
    block = (TILES, 1, 8, 128)
    return pl.pallas_call(
        place_kernel,
        grid=(PIECES,),
        out_shape=jax.ShapeDtypeStruct((2, OWNER_CAP, COLS * PIECES), BF),
        in_specs=[
            same,
            same,
            pl.BlockSpec(block, lambda r: (0, r, 0, 0)),
            pl.BlockSpec((TILES, 1, 8, WIDTH), lambda r: (0, r, 0, 0)),
            pl.BlockSpec(block, lambda r: (0, jnp.maximum(r - 1, 0), 0, HALF - 1)),
            pl.BlockSpec(block, lambda r: (0, jnp.minimum(r + 1, PIECES - 1), 0, 0)),
        ],
        out_specs=pl.BlockSpec((2, OWNER_CAP, COLS), lambda r: (0, 0, r)),
        compiler_params=pltpu.CompilerParams(vmem_limit_bytes=40 * 2**20),
        cost_estimate=pl.CostEstimate(
            flops=10**9, bytes_accessed=8 * 10**6, transcendentals=0
        ),
        name="place_lines",
    )(pick, sel, message, arrived, arrived, arrived)


def owner_tables(src_row, line_owner, me):
    tile = src_row // LINES
    owned = line_owner == me
    ids = jnp.arange(ALL_LINES, dtype=jnp.int32)
    before = owned[None, :] & (ids[None, :] < ids[:, None])
    rank = jnp.sum(before.astype(jnp.int32), axis=1)
    rank_tile = jnp.sum((before & (tile[None, :] == tile[:, None])).astype(jnp.int32), axis=1)
    outs = jnp.arange(OWNER_CAP, dtype=jnp.int32)
    hit = owned[None, :] & (rank[None, :] == outs[:, None])
    code = jnp.sum(jnp.where(hit, (tile * 2 + rank_tile + 1)[None, :], 0), axis=1) - 1
    rows = jnp.arange(128, dtype=jnp.int32)[:, None]
    cols = jnp.arange(128, dtype=jnp.int32)[None, :]
    slot = jnp.tile(code, 4)[:, None]
    pick = (
        (slot == (cols >> 3) * 2 + ((cols >> 1) & 1))
        & ((rows >> 6) == ((cols >> 2) & 1))
        & (((rows >> 5) & 1) == (cols & 1))
    )
    sel = (slot >= 0) & ((slot >> 1) == (cols >> 3)) & ((rows >> 5) == (cols & 7))
    return pick.astype(BF), sel.astype(BF)


def neighbours(axis, first, last):
    count = lax.axis_size(axis)
    up = [(i, i + 1) for i in range(count - 1)]
    down = [(i + 1, i) for i in range(count - 1)]
    return lax.ppermute(last, axis, up), lax.ppermute(first, axis, down)


def per_device(
    reference_slc, secondary_slc, chip_offsets, src_row, line_owner, band_start, band_taps
):
    az = lax.axis_index("az")
    rg = lax.axis_index("rg")
    place = jnp.stack([az, rg]).astype(jnp.int32)
    packed = pack_lines(
        place,
        secondary_slc.reshape(2 * LINES, COLS),
        band_start.reshape(PIECES * COLS // 128, 128),
        band_taps,
        src_row.reshape(1, ALL_LINES),
        line_owner.reshape(1, ALL_LINES),
    )
    arrived = lax.all_to_all(packed, BOTH, 0, 0, tiled=True)

    up, down = neighbours(
        "az", secondary_slc[:, :MARGIN, :], secondary_slc[:, LINES - MARGIN :, :]
    )

    def edge(cols):
        return jnp.concatenate(
            [
                reference_slc[:, FIRST_ROW : FIRST_ROW + CHIP_LEN, cols],
                up[:, :, cols],
                secondary_slc[:, :, cols],
                down[:, :, cols],
            ],
            axis=1,
        )

    left, right = neighbours("rg", edge(slice(0, 128)), edge(slice(COLS - 128, COLS)))
    off = chip_offsets[:, 0, :]
    offv = jnp.pad(off, ((0, 0), (0, 128 - CHIPS)))
    est, message = estimate(off, offv, reference_slc, secondary_slc, up, down, left, right)
    told = lax.all_to_all(message.reshape(OWNERS * 8, 128), BOTH, 0, 0, tiled=True)
    pick, sel = owner_tables(src_row, line_owner, az * PIECES + rg)
    resampled = place_lines(
        pick,
        sel,
        told.reshape(TILES, PIECES, 8, 128),
        arrived.reshape(TILES, PIECES, 8, WIDTH),
    )
    return est[:, None, :CHIPS], resampled


def solution(mesh):
    return jax.shard_map(
        per_device,
        mesh=mesh,
        in_specs=(
            P(None, "az", "rg"),
            P(None, "az", "rg"),
            P(None, "az", "rg"),
            P(),
            P(),
            P(),
            P(),
        ),
        out_specs=(P(None, "az", "rg"), P(None, BOTH, None)),
        check_vma=False,
    )
```

profile of v0, /device:TPU:0, one launch (start us, length us, event | category | flops | bytes accessed | tf_op | source)
XLA Modules:
  0.0 145.1 jit_solution(5171789099973870178)
XLA Ops:
  0.6 0.0 copy-start.14
  0.6 0.0 copy-start.13
  0.7 1.6 %fusion.8 = (bf16[2,64,3072]{2,1,0:T(8,128)(2,1)S(1)}, bf16[2,64,3072]{2,1,0:T(8,128)(2,1)S(1)}) fusion(bf16[2,96,3072]{2,1,0:T(8,128)(2,1)} %sec_ref.1), kind=kLoop, calls=%fused_computation.34 | loop fusion | bytes 3145728 | tf_op jit(solution)/shard_map/slice | solution.py:517
  2.3 1.3 collective-permute-start.1
  3.6 3.1 %collective-permute-start = (bf16[2,64,3072]{2,1,0:T(8,128)(2,1)S(1)}, bf16[2,64,3072]{2,1,0:T(8,128)(2,1)S(1)}, u32[]{:S(2)}, u32[]{:S(2)}) collective-permute-start(bf16[2,64,3072]{2,1,0:T(8,128)(2,1)S(1)} %get-tuple-element.17), channel_id=1, source_target_pairs={{0,8},{8,16},{16,24},{24,32},{32,40},{40,48},{48,56},{56,64},{64,7... | collective-permute-start | bytes 2359304 | tf_op jit(solution)/shard_map/ppermute | solution.py:497
  6.7 0.8 fusion.6
  7.5 1.0 collective-permute-done.up_ref
  8.5 3.5 %collective-permute-start.2 = (bf16[2,288,128]{2,1,0:T(8,128)(2,1)S(1)}, bf16[2,288,128]{2,1,0:T(8,128)(2,1)S(1)}, u32[]{:S(2)}, u32[]{:S(2)}) collective-permute-start(bf16[2,288,128]{2,1,0:T(8,128)(2,1)S(1)} %pad_maximum_fusion), channel_id=1, source_target_pairs={{0,1},{1,2},{2,3},{3,4},{4,5},{5,6},{6,7},{8,9},{9,10},{10,11},{11... | collective-permute-start | bytes 442376 | tf_op jit(solution)/shard_map/ppermute | solution.py:497
  12.1 1.3 collective-permute-start.3
  13.4 1.3 collective-permute-done.2.left_ref
  14.7 4.4 %collective-permute-done.3.right_ref = bf16[2,288,128]{2,1,0:T(8,128)(2,1)S(1)} collective-permute-done((bf16[2,288,128]{2,1,0:T(8,128)(2,1)S(1)}, bf16[2,288,128]{2,1,0:T(8,128)(2,1)S(1)}, u32[]{:S(2)}, u32[]{:S(2)}) %collective-permute-start.3) | collective-permute-done | bytes 147488 | tf_op jit(solution)/shard_map/ppermute | solution.py:497
  19.1 0.7 copy-done.7
  19.8 1.3 copy-done.4
  21.0 0.9 copy-done.8
  21.9 0.9 copy-done.10
  22.8 0.9 copy-done.11
  23.8 0.9 copy-done.12
  24.7 17.8 %estimate.1 = (f32[2,128]{1,0:T(2,128)}, bf16[128,8,128]{2,1,0:T(8,128)(2,1)}) custom-call(s32[2,96]{1,0:T(2,128)S(1)} %bitcast.19, s32[2,128]{1,0:T(2,128)S(1)} %pad.4.offv_ref, bf16[2,96,3072]{2,1,0:T(8,128)(2,1)S(1)} %copy-done.4, bf16[2,96,3072]{2,1,0:T(8,128)(2,1)S(1)} %copy-done.1, bf16[2,64,3072]{2,1,0:T(8,128)(2,1)S(1)} %collective-permute-done.up_ref, ...), custom_call_target="tpu_custom_call" | custom-call | flops 6000000000 | bytes 20000000 | tf_op jit(solution)/shard_map/estimate/pallas_call | solution.py:385
  42.5 24.3 %all-to-all-start = ((bf16[128,8,128]{2,1,0:T(8,128)(2,1)}), bf16[128,8,128]{2,1,0:T(8,128)(2,1)S(1)}, u32[]{:S(2)}, u32[]{:S(2)}) async-start(bf16[128,8,128]{2,1,0:T(8,128)(2,1)} %get-tuple-element.5), calls=%async_computation | async-start | bytes 524288 | tf_op jit(solution)/shard_map/all_to_all | solution.py:535
  66.8 0.1 pad_add_fusion.place_ref
  66.9 14.5 %pack_lines.1 = bf16[1024,1664]{1,0:T(8,128)(2,1)S(1)} custom-call(s32[2]{0:T(128)S(1)} %pad_add_fusion.place_ref, bf16[192,3072]{1,0:T(8,128)(2,1)S(1)} %bitcast.16, s32[192,128]{1,0:T(8,128)S(1)} %bitcast.20, bf16[8,24576]{1,0:T(8,128)(2,1)S(1)} %copy-done.6, s32[1,1536]{1,0:T(1,128)S(1)} %reshape.102.src_ref, s32[1,1536]{1,0:T(1,128)S(1)} %reshape.103.own_ref), custom_call_target="tpu_custom_call" | custom-call | flops 2000000000 | bytes 6000000 | tf_op jit(solution)/shard_map/pack_lines/pallas_call | solution.py:184
  81.4 1.7 %copy-done = bf16[1024,1664]{1,0:T(8,128)(2,1)} copy-done((bf16[1024,1664]{1,0:T(8,128)(2,1)}, bf16[1024,1664]{1,0:T(8,128)(2,1)S(1)}, u32[]{:S(2)}) %copy-start) | copy-done | bytes 3407896
  83.2 0.7 copy-done.2
  83.9 9.8 %all-to-all-start.1 = ((bf16[128,8,1664]{2,1,0:T(8,128)(2,1)}), bf16[128,8,1664]{2,1,0:T(8,128)(2,1)S(1)}, u32[]{:S(2)}, u32[]{:S(2)}) async-start(bf16[128,8,1664]{2,1,0:T(8,128)(2,1)} %bitcast.15), calls=%async_computation.1 | async-start | bytes 6815744 | tf_op jit(solution)/shard_map/all_to_all | solution.py:514
  93.7 4.1 %convert_reduce_fusion.1 = (s32[1536]{0:T(1024)S(1)}, s32[1536]{0:T(1024)S(1)}) fusion(pred[1536]{0:T(1024)(128)(4,1)S(1)} %broadcast_compare_fusion, s32[1536]{0:T(1024)S(1)} %add_select_fusion), kind=kLoop, calls=%fused_computation.1 | loop fusion | flops 18871296 | bytes 19968 | tf_op jit(solution)/shard_map/reduce_sum | solution.py:476
  97.8 0.2 select_reduce_fusion
  97.9 0.1 eq.107
  98.1 0.1 and_convert_fusion.sel_ref
  98.2 0.1 and_convert_fusion.1.pick_ref
  98.3 39.3 %all-to-all-done.1 = bf16[128,8,1664]{2,1,0:T(8,128)(2,1)S(1)} async-done(((bf16[128,8,1664]{2,1,0:T(8,128)(2,1)}), bf16[128,8,1664]{2,1,0:T(8,128)(2,1)S(1)}, u32[]{:S(2)}, u32[]{:S(2)}) %all-to-all-start.1) | async-done | bytes 3407904 | tf_op jit(solution)/shard_map/all_to_all | solution.py:514
  137.6 0.9 copy-done.3
  138.6 6.5 %place_lines.1 = bf16[2,32,24576]{2,1,0:T(8,128)(2,1)} custom-call(bf16[128,128]{1,0:T(8,128)(2,1)S(1)} %and_convert_fusion.1.pick_ref, bf16[128,128]{1,0:T(8,128)(2,1)S(1)} %and_convert_fusion.sel_ref, bf16[16,8,8,128]{3,2,1,0:T(8,128)(2,1)S(1)} %bitcast.17, bf16[16,8,8,1664]{3,2,1,0:T(8,128)(2,1)S(1)} %bitcast.12, bf16[16,8,8,1664]{3,2,1,0:T(8,128)(2,1)S(1)} %bitcast.13, ...), custom_call_target="tpu_custom_call" | custom-call | flops 1000000000 | bytes 8000000 | tf_op jit(solution)/shard_map/place_lines/pallas_call | solution.py:450
  (44 shorter events, 0.2 us)
Async XLA Ops:
  0.6 19.1 %copy-start.14 = (bf16[96,128]{1,0:T(8,128)(2,1)S(1)}, bf16[96,128]{1,0:T(8,128)(2,1)}, u32[]{:S(2)}) copy-start(bf16[96,128]{1,0:T(8,128)(2,1)} %constant.54.clone.lift_ref) | copy-start | bytes 73732
  0.6 19.1 %copy-start.13 = (bf16[128,128]{1,0:T(8,128)(2,1)S(1)}, bf16[128,128]{1,0:T(8,128)(2,1)}, u32[]{:S(2)}) copy-start(bf16[128,128]{1,0:T(8,128)(2,1)} %constant.50.clone.fwd_ref) | copy-start | bytes 98308
  0.7 6.8 %copy-start.1 = (bf16[2,96,3072]{2,1,0:T(8,128)(2,1)S(1)}, bf16[2,96,3072]{2,1,0:T(8,128)(2,1)}, u32[]{:S(2)}) copy-start(bf16[2,96,3072]{2,1,0:T(8,128)(2,1)} %sec_ref.1) | copy-start | bytes 3538948
  0.7 12.7 %copy-start.16 = (s32[1536]{0:T(1024)S(1)}, s32[1536]{0:T(1024)}, u32[]{:S(2)}) copy-start(s32[1536]{0:T(1024)} %param.16) | copy-start | bytes 18436
  0.7 12.7 %copy-start.15 = (s32[1536]{0:T(1024)S(1)}, s32[1536]{0:T(1024)}, u32[]{:S(2)}) copy-start(s32[1536]{0:T(1024)} %param.15) | copy-start | bytes 18436
  0.7 12.7 %copy-start.5 = (s32[2,1,96]{2,1,0:T(1,128)S(1)}, s32[2,1,96]{2,1,0:T(1,128)}, u32[]{:S(2)}) copy-start(s32[2,1,96]{2,1,0:T(1,128)} %param.14) | copy-start | bytes 2308
  2.3 5.2 %collective-permute-start.1 = (bf16[2,64,3072]{2,1,0:T(8,128)(2,1)S(1)}, bf16[2,64,3072]{2,1,0:T(8,128)(2,1)S(1)}, u32[]{:S(2)}, u32[]{:S(2)}) collective-permute-start(bf16[2,64,3072]{2,1,0:T(8,128)(2,1)S(1)} %get-tuple-element.16), channel_id=1, source_target_pairs={{8,0},{16,8},{24,16},{32,24},{40,32},{48,40},{56,48},{64,56},{72,6... | collective-permute-start | bytes 2359304 | tf_op jit(solution)/shard_map/ppermute | solution.py:497
  3.6 4.9 %collective-permute-start = (bf16[2,64,3072]{2,1,0:T(8,128)(2,1)S(1)}, bf16[2,64,3072]{2,1,0:T(8,128)(2,1)S(1)}, u32[]{:S(2)}, u32[]{:S(2)}) collective-permute-start(bf16[2,64,3072]{2,1,0:T(8,128)(2,1)S(1)} %get-tuple-element.17), channel_id=1, source_target_pairs={{0,8},{8,16},{16,24},{24,32},{32,40},{40,48},{48,56},{56,64},{64,7... | collective-permute-start | bytes 2359304 | tf_op jit(solution)/shard_map/ppermute | solution.py:497
  8.5 6.1 %collective-permute-start.2 = (bf16[2,288,128]{2,1,0:T(8,128)(2,1)S(1)}, bf16[2,288,128]{2,1,0:T(8,128)(2,1)S(1)}, u32[]{:S(2)}, u32[]{:S(2)}) collective-permute-start(bf16[2,288,128]{2,1,0:T(8,128)(2,1)S(1)} %pad_maximum_fusion), channel_id=1, source_target_pairs={{0,1},{1,2},{2,3},{3,4},{4,5},{5,6},{6,7},{8,9},{9,10},{10,11},{11... | collective-permute-start | bytes 442376 | tf_op jit(solution)/shard_map/ppermute | solution.py:497
  12.1 7.0 %collective-permute-start.3 = (bf16[2,288,128]{2,1,0:T(8,128)(2,1)S(1)}, bf16[2,288,128]{2,1,0:T(8,128)(2,1)S(1)}, u32[]{:S(2)}, u32[]{:S(2)}) collective-permute-start(bf16[2,288,128]{2,1,0:T(8,128)(2,1)S(1)} %pad_maximum_fusion.1), channel_id=1, source_target_pairs={{1,0},{2,1},{3,2},{4,3},{5,4},{6,5},{7,6},{9,8},{10,9},{11,10},{12... | collective-permute-start | bytes 442376 | tf_op jit(solution)/shard_map/ppermute | solution.py:497
  19.1 0.7 copy-start.7
  19.8 1.3 copy-start.4
  21.0 0.9 copy-start.8
  21.9 0.9 copy-start.10
  22.8 0.9 copy-start.11
  23.7 0.9 copy-start.12
  24.7 42.2 %copy-start.6 = (bf16[8,24576]{1,0:T(8,128)(2,1)S(1)}, bf16[8,24576]{1,0:T(8,128)(2,1)}, u32[]{:S(2)}) copy-start(bf16[8,24576]{1,0:T(8,128)(2,1)} %taps_ref.1) | copy-start | bytes 1179652
  24.7 42.2 %copy-start.9 = (s32[24576]{0:T(1024)S(1)}, s32[24576]{0:T(1024)}, u32[]{:S(2)}) copy-start(s32[24576]{0:T(1024)} %param.17) | copy-start | bytes 294916
  42.5 40.7 %all-to-all-start = ((bf16[128,8,128]{2,1,0:T(8,128)(2,1)}), bf16[128,8,128]{2,1,0:T(8,128)(2,1)S(1)}, u32[]{:S(2)}, u32[]{:S(2)}) async-start(bf16[128,8,128]{2,1,0:T(8,128)(2,1)} %get-tuple-element.5), calls=%async_computation | async-start | bytes 524288 | tf_op jit(solution)/shard_map/all_to_all | solution.py:535
  81.4 1.7 %copy-start = (bf16[1024,1664]{1,0:T(8,128)(2,1)}, bf16[1024,1664]{1,0:T(8,128)(2,1)S(1)}, u32[]{:S(2)}) copy-start(bf16[1024,1664]{1,0:T(8,128)(2,1)S(1)} %pack_lines.1) | copy-start | bytes 10223620
  83.2 0.7 copy-start.2
  83.9 53.7 %all-to-all-start.1 = ((bf16[128,8,1664]{2,1,0:T(8,128)(2,1)}), bf16[128,8,1664]{2,1,0:T(8,128)(2,1)S(1)}, u32[]{:S(2)}, u32[]{:S(2)}) async-start(bf16[128,8,1664]{2,1,0:T(8,128)(2,1)} %bitcast.15), calls=%async_computation.1 | async-start | bytes 6815744 | tf_op jit(solution)/shard_map/all_to_all | solution.py:514
  137.6 1.0 copy-start.3
where the time goes:
time: 146 us; the launch traced here: 145 us
  waiting for transfers between devices  45.9 us (31%)
  starting transfers between devices  43.2 us (30%)
  Pallas kernels  38.9 us (27%)
  local copies, waits for them, and re-layouts  11.5 us (8%)
  other arithmetic  4.65 us (3%)
    all_to_all x1, waiting for transfers between devices, per_device(): arrived = lax.all_to_all(packed, BOTH, 0, 0, tiled=True)  39.3 us
    all_to_all x1, starting transfers between devices, per_device(): lax.all_to_all(message.reshape(OWNERS * 8, 128), BOTH, 0, 0, tiled=True)  24.3 us
    pallas_call x1, Pallas kernels, estimate(): pl.pallas_call(estimate_kernel, out_shape=(jax.ShapeDtypeStruct((2, 128),...  17.8 us
    pallas_call x1, Pallas kernels, pack_lines(): pl.pallas_call(pack_kernel, out_shape=jax.ShapeDtypeStruct((OWNERS * 8, W...  14.5 us
    all_to_all x1, starting transfers between devices, per_device(): arrived = lax.all_to_all(packed, BOTH, 0, 0, tiled=True)  9.75 us
    ppermute x4, starting transfers between devices, neighbours(): return (lax.ppermute(last, axis, up), lax.ppermute(first, axis, down))  9.15 us
    unnamed x34, local copies, waits for them, and re-layouts  8.96 us
    ppermute x4, waiting for transfers between devices, neighbours(): return (lax.ppermute(last, axis, up), lax.ppermute(first, axis, down))  6.66 us
  transfers between devices with their start and end apart: 6, of which 4 were waited for; matrix products, arithmetic and copies ran while one was open for 4% of the time, Pallas kernels for 10%

commit v1 on v0

--- a/solution.py
+++ b/solution.py
@@ -191,7 +191,7 @@
             pltpu.VMEM((4 * LINES, WIDTH), BF),
             pltpu.VMEM((OWNERS * 8, 4 * LINES), BF),
         ],
-        compiler_params=pltpu.CompilerParams(vmem_limit_bytes=40 * 2**20),
+        compiler_params=pltpu.CompilerParams(vmem_limit_bytes=20 * 2**20),
         cost_estimate=pl.CostEstimate(
             flops=2 * 10**9, bytes_accessed=6 * 10**6, transcendentals=0
         ),
@@ -375,8 +375,7 @@
             jnp.where(kind == 2, sin_hi, jnp.where(kind == 3, sine - sin_hi, 0.0)),
         ),
     ).astype(BF)
-    for owner in range(OWNERS):
-        msg_ref[owner] = message
+    msg_ref[...] = message
 
 
 def estimate(off, offv, ref, sec, up, down, left, right):
@@ -386,7 +385,7 @@
         estimate_kernel,
         out_shape=(
             jax.ShapeDtypeStruct((2, 128), F32),
-            jax.ShapeDtypeStruct((OWNERS, 8, 128), BF),
+            jax.ShapeDtypeStruct((8, 128), BF),
         ),
         in_specs=[smem] + [vmem] * 12,
         out_specs=(vmem, vmem),
@@ -398,7 +397,7 @@
             pltpu.VMEM((PAIRS, 128), F32),
             pltpu.VMEM((PAIRS, 128), F32),
         ],
-        compiler_params=pltpu.CompilerParams(vmem_limit_bytes=48 * 2**20),
+        compiler_params=pltpu.CompilerParams(vmem_limit_bytes=26 * 2**20),
         cost_estimate=pl.CostEstimate(
             flops=6 * 10**9, bytes_accessed=20 * 10**6, transcendentals=0
         ),
@@ -406,7 +405,7 @@
     )(off, offv, ref, sec, up, down, left, right, *kernel_tables())
 
 
-def place_kernel(pick_ref, sel_ref, msg_ref, arr_ref, prev_ref, next_ref, out_ref):
+def place_kernel(at_ref, pick_ref, sel_ref, msg_ref, arr_ref, prev_ref, next_ref, out_ref):
     piece = pl.program_id(0)
     pick = pick_ref[...]
     turned = jnp.dot(sel_ref[...], msg_ref[...].reshape(128, 128), preferred_element_type=F32)
@@ -444,31 +443,34 @@
                 write(HALF - 1 + at, high + after if at == HALF - 2 else high)
 
 
-def place_lines(pick, sel, message, arrived):
-    same = pl.BlockSpec((128, 128), lambda r: (0, 0))
+def place_lines(place, pick, sel, message, arrived):
+    same = pl.BlockSpec((128, 128), lambda r, at: (0, 0))
     block = (TILES, 1, 8, 128)
     return pl.pallas_call(
         place_kernel,
-        grid=(PIECES,),
+        grid_spec=pltpu.PrefetchScalarGridSpec(
+            num_scalar_prefetch=1,
+            grid=(PIECES,),
+            in_specs=[
+                same,
+                same,
+                pl.BlockSpec(block, lambda r, at: (0, r ^ at[1], 0, 0)),
+                pl.BlockSpec((TILES, 1, 8, WIDTH), lambda r, at: (0, r, 0, 0)),
+                pl.BlockSpec(block, lambda r, at: (0, jnp.maximum(r - 1, 0), 0, HALF - 1)),
+                pl.BlockSpec(block, lambda r, at: (0, jnp.minimum(r + 1, PIECES - 1), 0, 0)),
+            ],
+            out_specs=pl.BlockSpec((2, OWNER_CAP, COLS), lambda r, at: (0, 0, r)),
+        ),
         out_shape=jax.ShapeDtypeStruct((2, OWNER_CAP, COLS * PIECES), BF),
-        in_specs=[
-            same,
-            same,
-            pl.BlockSpec(block, lambda r: (0, r, 0, 0)),
-            pl.BlockSpec((TILES, 1, 8, WIDTH), lambda r: (0, r, 0, 0)),
-            pl.BlockSpec(block, lambda r: (0, jnp.maximum(r - 1, 0), 0, HALF - 1)),
-            pl.BlockSpec(block, lambda r: (0, jnp.minimum(r + 1, PIECES - 1), 0, 0)),
-        ],
-        out_specs=pl.BlockSpec((2, OWNER_CAP, COLS), lambda r: (0, 0, r)),
-        compiler_params=pltpu.CompilerParams(vmem_limit_bytes=40 * 2**20),
+        compiler_params=pltpu.CompilerParams(vmem_limit_bytes=20 * 2**20),
         cost_estimate=pl.CostEstimate(
             flops=10**9, bytes_accessed=8 * 10**6, transcendentals=0
         ),
         name="place_lines",
-    )(pick, sel, message, arrived, arrived, arrived)
-
-
-def owner_tables(src_row, line_owner, me):
+    )(place, pick, sel, message, arrived, arrived, arrived)
+
+
+def owner_tables(src_row, line_owner, az, me):
     tile = src_row // LINES
     owned = line_owner == me
     ids = jnp.arange(ALL_LINES, dtype=jnp.int32)
@@ -486,7 +488,7 @@
         & ((rows >> 6) == ((cols >> 2) & 1))
         & (((rows >> 5) & 1) == (cols & 1))
     )
-    sel = (slot >= 0) & ((slot >> 1) == (cols >> 3)) & ((rows >> 5) == (cols & 7))
+    sel = (slot >= 0) & ((slot >> 1) == ((cols >> 3) ^ az)) & ((rows >> 5) == (cols & 7))
     return pick.astype(BF), sel.astype(BF)
 
 
@@ -495,6 +497,23 @@
     up = [(i, i + 1) for i in range(count - 1)]
     down = [(i + 1, i) for i in range(count - 1)]
     return lax.ppermute(last, axis, up), lax.ppermute(first, axis, down)
+
+
+def exchanged(block):
+    block = block[None]
+    held = 1
+    while held < OWNERS:
+        radix = min(4, OWNERS // held)
+        block = jnp.concatenate(
+            [block]
+            + [
+                lax.ppermute(block, BOTH, [(d, d ^ (held * k)) for d in range(OWNERS)])
+                for k in range(1, radix)
+            ],
+            axis=0,
+        )
+        held *= radix
+    return block
 
 
 def per_device(
@@ -512,6 +531,7 @@
         line_owner.reshape(1, ALL_LINES),
     )
     arrived = lax.all_to_all(packed, BOTH, 0, 0, tiled=True)
+    chip_offsets, _ = lax.optimization_barrier((chip_offsets, packed))
 
     up, down = neighbours(
         "az", secondary_slc[:, :MARGIN, :], secondary_slc[:, LINES - MARGIN :, :]
@@ -532,9 +552,10 @@
     off = chip_offsets[:, 0, :]
     offv = jnp.pad(off, ((0, 0), (0, 128 - CHIPS)))
     est, message = estimate(off, offv, reference_slc, secondary_slc, up, down, left, right)
-    told = lax.all_to_all(message.reshape(OWNERS * 8, 128), BOTH, 0, 0, tiled=True)
-    pick, sel = owner_tables(src_row, line_owner, az * PIECES + rg)
+    told = exchanged(message)
+    pick, sel = owner_tables(src_row, line_owner, az, az * PIECES + rg)
     resampled = place_lines(
+        place,
         pick,
         sel,
         told.reshape(TILES, PIECES, 8, 128),

time: 146 us -> 149 us (1.021)
  local copies, waits for them, and re-layouts: 11.5 us -> 17.8 us
  starting transfers between devices: 43.2 us -> 37 us
  waiting for transfers between devices: 45.9 us -> 48.1 us
    all_to_all x1, waiting for transfers between devices: 39.3 us -> 0.01 us  [per_device(): arrived = lax.all_to_all(packed, BOTH, 0, 0, tiled=True)]
    ppermute x4, waiting for transfers between devices: 6.66 us -> 33.4 us  [neighbours(): return (lax.ppermute(last, axis, up), lax.ppermute(first, axis, down))]
    all_to_all x1 -> x0, starting transfers between devices: 24.3 us -> none  [per_device(): lax.all_to_all(message.reshape(OWNERS * 8, 128), BOTH, 0, 0, tiled=True)]
    ppermute x0 -> x10, waiting for transfers between devices: none -> 14.8 us  [exchanged(): lax.ppermute(block, BOTH, [(d, d ^ held * k) for d in range(OWNERS)])]
    ppermute x0 -> x10, starting transfers between devices: none -> 14.7 us  [exchanged(): lax.ppermute(block, BOTH, [(d, d ^ held * k) for d in range(OWNERS)])]
    all_to_all x1, starting transfers between devices: 9.75 us -> 12.8 us  [per_device(): arrived = lax.all_to_all(packed, BOTH, 0, 0, tiled=True)]
    unnamed x34 -> x41, local copies, waits for them, and re-layouts: 8.96 us -> 11.9 us
  transfers between devices with their start and end apart: 6 -> 15, of which waited for: 4 -> 7; matrix products, arithmetic and copies ran while one was open for 4% -> 5% of each run, Pallas kernels for 10% -> 22%
where the time goes in v1:
time: 149 us
  waiting for transfers between devices  48.1 us (32%)
  Pallas kernels  40.1 us (27%)
  starting transfers between devices  37 us (25%)
  local copies, waits for them, and re-layouts  17.8 us (12%)
  other arithmetic  4.67 us (3%)
    ppermute x4, waiting for transfers between devices, neighbours(): return (lax.ppermute(last, axis, up), lax.ppermute(first, axis, down))  33.4 us
    pallas_call x1, Pallas kernels, estimate(): pl.pallas_call(estimate_kernel, out_shape=(jax.ShapeDtypeStruct((2, 128),...  18.5 us
    ppermute x10, waiting for transfers between devices, exchanged(): lax.ppermute(block, BOTH, [(d, d ^ held * k) for d in range(OWNERS)])  14.8 us
    ppermute x10, starting transfers between devices, exchanged(): lax.ppermute(block, BOTH, [(d, d ^ held * k) for d in range(OWNERS)])  14.7 us
    pallas_call x1, Pallas kernels, pack_lines(): pl.pallas_call(pack_kernel, out_shape=jax.ShapeDtypeStruct((OWNERS * 8, W...  14.5 us
    all_to_all x1, starting transfers between devices, per_device(): arrived = lax.all_to_all(packed, BOTH, 0, 0, tiled=True)  12.8 us
    unnamed x41, local copies, waits for them, and re-layouts  11.9 us
    ppermute x4, starting transfers between devices, neighbours(): return (lax.ppermute(last, axis, up), lax.ppermute(first, axis, down))  9.4 us
  transfers between devices with their start and end apart: 15, of which 7 were waited for; matrix products, arithmetic and copies ran while one was open for 5% of the time, Pallas kernels for 22%

profile of v1, /device:TPU:0, one launch (start us, length us, event | category | flops | bytes accessed | tf_op | source)
XLA Modules:
  0.0 148.6 jit_solution(531382647020799537)
XLA Ops:
  0.6 2.6 %fusion.10 = (bf16[2,64,3072]{2,1,0:T(8,128)(2,1)}, bf16[2,64,3072]{2,1,0:T(8,128)(2,1)}) fusion(bf16[2,96,3072]{2,1,0:T(8,128)(2,1)} %sec_ref.1), kind=kLoop, calls=%fused_computation.65 | loop fusion | bytes 3145728 | tf_op jit(solution)/shard_map/slice | solution.py:537
  3.3 1.3 collective-permute-start.1
  4.6 4.0 %collective-permute-start = (bf16[2,64,3072]{2,1,0:T(8,128)(2,1)}, bf16[2,64,3072]{2,1,0:T(8,128)(2,1)}, u32[]{:S(2)}, u32[]{:S(2)}) collective-permute-start(bf16[2,64,3072]{2,1,0:T(8,128)(2,1)} %get-tuple-element.19), channel_id=1, source_target_pairs={{0,8},{8,16},{16,24},{24,32},{32,40},{40,48},{48,56},{56,64},{64,7... | collective-permute-start | bytes 2359304 | tf_op jit(solution)/shard_map/ppermute | solution.py:499
  8.6 1.3 copy-done.1
  9.9 1.0 copy-done.7
  11.8 14.5 %pack_lines.1 = bf16[1024,1664]{1,0:T(8,128)(2,1)S(1)} custom-call(s32[2]{0:T(128)S(1)} %pad_add_fusion.place_ref.at_ref, bf16[192,3072]{1,0:T(8,128)(2,1)S(1)} %bitcast.20, s32[192,128]{1,0:T(8,128)S(1)} %bitcast.28, bf16[8,24576]{1,0:T(8,128)(2,1)S(1)} %copy-done.7, s32[1,1536]{1,0:T(1,128)S(1)} %reshape.98.src_ref, s32[1,1536]{1,0:T(1,128)S(1)} %reshape.99.own_ref), custom_call_target="tpu_custom_call" | custom-call | flops 2000000000 | bytes 6000000 | tf_op jit(solution)/shard_map/pack_lines/pallas_call | solution.py:184
  26.3 1.7 %copy-done = bf16[1024,1664]{1,0:T(8,128)(2,1)} copy-done((bf16[1024,1664]{1,0:T(8,128)(2,1)}, bf16[1024,1664]{1,0:T(8,128)(2,1)S(1)}, u32[]{:S(2)}) %copy-start) | copy-done | bytes 3407896
  28.0 12.8 %all-to-all-start = ((bf16[128,8,1664]{2,1,0:T(8,128)(2,1)}), bf16[128,8,1664]{2,1,0:T(8,128)(2,1)S(1)}, u32[]{:S(2)}, u32[]{:S(2)}) async-start(bf16[128,8,1664]{2,1,0:T(8,128)(2,1)} %bitcast.19), calls=%async_computation | async-start | bytes 6815744 | tf_op jit(solution)/shard_map/all_to_all | solution.py:533
  40.9 4.1 %convert_reduce_fusion.1 = (s32[1536]{0:T(1024)S(1)}, s32[1536]{0:T(1024)S(1)}) fusion(pred[1536]{0:T(1024)(128)(4,1)S(1)} %broadcast_compare_fusion, s32[1536]{0:T(1024)S(1)} %add_select_fusion), kind=kLoop, calls=%fused_computation.1 | loop fusion | flops 18871296 | bytes 19968 | tf_op jit(solution)/shard_map/reduce_sum | solution.py:478
  48.7 2.9 %collective-permute-start.2 = (bf16[2,288,128]{2,1,0:T(8,128)(2,1)S(1)}, bf16[2,288,128]{2,1,0:T(8,128)(2,1)S(1)}, u32[]{:S(2)}, u32[]{:S(2)}) collective-permute-start(bf16[2,288,128]{2,1,0:T(8,128)(2,1)S(1)} %pad_maximum_fusion), channel_id=1, source_target_pairs={{0,1},{1,2},{2,3},{3,4},{4,5},{5,6},{6,7},{8,9},{9,10},{10,11},{11... | collective-permute-start | bytes 442376 | tf_op jit(solution)/shard_map/ppermute | solution.py:499
  51.6 1.3 collective-permute-start.3
  52.9 27.1 %collective-permute-done.2.left_ref = bf16[2,288,128]{2,1,0:T(8,128)(2,1)S(1)} collective-permute-done((bf16[2,288,128]{2,1,0:T(8,128)(2,1)S(1)}, bf16[2,288,128]{2,1,0:T(8,128)(2,1)S(1)}, u32[]{:S(2)}, u32[]{:S(2)}) %collective-permute-start.2) | collective-permute-done | bytes 147488 | tf_op jit(solution)/shard_map/ppermute | solution.py:499
  80.0 6.3 %collective-permute-done.3.right_ref = bf16[2,288,128]{2,1,0:T(8,128)(2,1)S(1)} collective-permute-done((bf16[2,288,128]{2,1,0:T(8,128)(2,1)S(1)}, bf16[2,288,128]{2,1,0:T(8,128)(2,1)S(1)}, u32[]{:S(2)}, u32[]{:S(2)}) %collective-permute-start.3) | collective-permute-done | bytes 147488 | tf_op jit(solution)/shard_map/ppermute | solution.py:499
  86.3 1.3 copy-done.2
  87.5 1.3 copy-done.5
  88.8 0.9 copy-done.9
  89.7 0.9 copy-done.10
  91.5 18.5 %estimate.1 = (f32[2,128]{1,0:T(2,128)}, bf16[8,128]{1,0:T(8,128)(2,1)S(1)}) custom-call(s32[2,96]{1,0:T(2,128)S(1)} %bitcast.27, s32[2,128]{1,0:T(2,128)S(1)} %pad.4.offv_ref, bf16[2,96,3072]{2,1,0:T(8,128)(2,1)S(1)} %copy-done.5, bf16[2,96,3072]{2,1,0:T(8,128)(2,1)S(1)} %copy-done.2, bf16[2,64,3072]{2,1,0:T(8,128)(2,1)} %collective-permute-done.up_ref, ...), custom_call_target="tpu_custom_call" | custom-call | flops 6000000000 | bytes 20000000 | tf_op jit(solution)/shard_map/estimate/pallas_call | solution.py:384
  110.0 1.8 %collective-permute-start.6 = (bf16[1,8,128]{2,1,0:T(8,128)(2,1)S(1)}, bf16[1,8,128]{2,1,0:T(8,128)(2,1)S(1)}, u32[]{:S(2)}, u32[]{:S(2)}) collective-permute-start(bf16[1,8,128]{2,1,0:T(8,128)(2,1)S(1)} %bitcast.22), channel_id=1, source_target_pairs={{0,3},{1,2},{2,1},{3,0},{4,7},{5,6},{6,5},{7,4},{8,11},{9,10},{10,... | collective-permute-start | bytes 6152 | tf_op jit(solution)/shard_map/ppermute | solution.py:510
  111.8 1.7 %collective-permute-start.4 = (bf16[1,8,128]{2,1,0:T(8,128)(2,1)S(1)}, bf16[1,8,128]{2,1,0:T(8,128)(2,1)S(1)}, u32[]{:S(2)}, u32[]{:S(2)}) collective-permute-start(bf16[1,8,128]{2,1,0:T(8,128)(2,1)S(1)} %bitcast.24), channel_id=1, source_target_pairs={{0,1},{1,0},{2,3},{3,2},{4,5},{5,4},{6,7},{7,6},{8,9},{9,8},{10,11... | collective-permute-start | bytes 6152 | tf_op jit(solution)/shard_map/ppermute | solution.py:510
  113.5 1.0 collective-permute-done.6
  115.4 1.6 %collective-permute-start.9 = (bf16[4,8,128]{2,1,0:T(8,128)(2,1)S(1)}, bf16[4,8,128]{2,1,0:T(8,128)(2,1)S(1)}, u32[]{:S(2)}, u32[]{:S(2)}) collective-permute-start(bf16[4,8,128]{2,1,0:T(8,128)(2,1)S(1)} %pad_maximum_fusion.2), channel_id=1, source_target_pairs={{0,12},{1,13},{2,14},{3,15},{4,8},{5,9},{6,10},{7,11},{8,4},{9,5},... | collective-permute-start | bytes 24584 | tf_op jit(solution)/shard_map/ppermute | solution.py:510
  117.0 2.3 %collective-permute-start.8 = (bf16[4,8,128]{2,1,0:T(8,128)(2,1)S(1)}, bf16[4,8,128]{2,1,0:T(8,128)(2,1)S(1)}, u32[]{:S(2)}, u32[]{:S(2)}) collective-permute-start(bf16[4,8,128]{2,1,0:T(8,128)(2,1)S(1)} %pad_maximum_fusion.2), channel_id=1, source_target_pairs={{0,8},{1,9},{2,10},{3,11},{4,12},{5,13},{6,14},{7,15},{8,0},{9,1},... | collective-permute-start | bytes 24584 | tf_op jit(solution)/shard_map/ppermute | solution.py:510
  119.4 5.1 %collective-permute-done.7 = bf16[4,8,128]{2,1,0:T(8,128)(2,1)S(1)} collective-permute-done((bf16[4,8,128]{2,1,0:T(8,128)(2,1)S(1)}, bf16[4,8,128]{2,1,0:T(8,128)(2,1)S(1)}, u32[]{:S(2)}, u32[]{:S(2)}) %collective-permute-start.7) | collective-permute-done | bytes 8224 | tf_op jit(solution)/shard_map/ppermute | solution.py:510
  124.5 1.1 collective-permute-start.10
  125.6 2.1 %collective-permute-start.12 = (bf16[16,8,128]{2,1,0:T(8,128)(2,1)S(1)}, bf16[16,8,128]{2,1,0:T(8,128)(2,1)S(1)}, u32[]{:S(2)}, u32[]{:S(2)}) collective-permute-start(bf16[16,8,128]{2,1,0:T(8,128)(2,1)S(1)} %get-tuple-element.32), channel_id=1, source_target_pairs={{0,48},{1,49},{2,50},{3,51},{4,52},{5,53},{6,54},{7,55},{8,56},{9,... | collective-permute-start | bytes 98312 | tf_op jit(solution)/shard_map/ppermute | solution.py:510
  127.8 1.0 collective-permute-start.11
  128.7 4.4 %collective-permute-done.11 = bf16[16,8,128]{2,1,0:T(8,128)(2,1)S(1)} collective-permute-done((bf16[16,8,128]{2,1,0:T(8,128)(2,1)S(1)}, bf16[16,8,128]{2,1,0:T(8,128)(2,1)S(1)}, u32[]{:S(2)}, u32[]{:S(2)}) %collective-permute-start.11) | collective-permute-done | bytes 32800 | tf_op jit(solution)/shard_map/ppermute | solution.py:510
  133.2 3.1 %collective-permute-start.13 = (bf16[64,8,128]{2,1,0:T(8,128)(2,1)S(1)}, bf16[64,8,128]{2,1,0:T(8,128)(2,1)S(1)}, u32[]{:S(2)}, u32[]{:S(2)}) collective-permute-start(bf16[64,8,128]{2,1,0:T(8,128)(2,1)S(1)} %get-tuple-element.24), channel_id=1, source_target_pairs={{0,64},{1,65},{2,66},{3,67},{4,68},{5,69},{6,70},{7,71},{8,72},{9,... | collective-permute-start | bytes 393224 | tf_op jit(solution)/shard_map/ppermute | solution.py:510
  136.4 3.3 %collective-permute-done.13 = bf16[64,8,128]{2,1,0:T(8,128)(2,1)S(1)} collective-permute-done((bf16[64,8,128]{2,1,0:T(8,128)(2,1)S(1)}, bf16[64,8,128]{2,1,0:T(8,128)(2,1)S(1)}, u32[]{:S(2)}, u32[]{:S(2)}) %collective-permute-start.13) | collective-permute-done | bytes 131104 | tf_op jit(solution)/shard_map/ppermute | solution.py:510
  140.5 0.9 copy-done.4
  141.5 7.1 %place_lines.1 = bf16[2,32,24576]{2,1,0:T(8,128)(2,1)} custom-call(s32[2]{0:T(128)S(1)} %pad_add_fusion.place_ref.at_ref, bf16[128,128]{1,0:T(8,128)(2,1)S(1)} %and_convert_fusion.1.pick_ref, bf16[128,128]{1,0:T(8,128)(2,1)S(1)} %and_convert_fusion.sel_ref, bf16[16,8,8,128]{3,2,1,0:T(8,128)(2,1)S(1)} %bitcast.21, bf16[16,8,8,1664]{3,2,1,0:T(8,128)(2,1)S(1)} %bitcast.16, ...), custom_call_target="tpu_custom_call" | custom-call | flops 1000000000 | bytes 8000000 | tf_op jit(solution)/shard_map/place_lines/pallas_call | solution.py:449
  (72 shorter events, 7.5 us)
Async XLA Ops:
  0.6 7.9 %copy-start.15 = (s32[1536]{0:T(1024)S(1)}, s32[1536]{0:T(1024)}, u32[]{:S(2)}) copy-start(s32[1536]{0:T(1024)} %param.16) | copy-start | bytes 18436
  0.6 7.9 %copy-start.14 = (s32[1536]{0:T(1024)S(1)}, s32[1536]{0:T(1024)}, u32[]{:S(2)}) copy-start(s32[1536]{0:T(1024)} %param.15) | copy-start | bytes 18436
  3.3 43.8 %collective-permute-start.1 = (bf16[2,64,3072]{2,1,0:T(8,128)(2,1)}, bf16[2,64,3072]{2,1,0:T(8,128)(2,1)}, u32[]{:S(2)}, u32[]{:S(2)}) collective-permute-start(bf16[2,64,3072]{2,1,0:T(8,128)(2,1)} %get-tuple-element.18), channel_id=1, source_target_pairs={{8,0},{16,8},{24,16},{32,24},{40,32},{48,40},{56,48},{64,56},{72,6... | collective-permute-start | bytes 2359304 | tf_op jit(solution)/shard_map/ppermute | solution.py:499
  4.6 43.3 %collective-permute-start = (bf16[2,64,3072]{2,1,0:T(8,128)(2,1)}, bf16[2,64,3072]{2,1,0:T(8,128)(2,1)}, u32[]{:S(2)}, u32[]{:S(2)}) collective-permute-start(bf16[2,64,3072]{2,1,0:T(8,128)(2,1)} %get-tuple-element.19), channel_id=1, source_target_pairs={{0,8},{8,16},{16,24},{24,32},{32,40},{40,48},{48,56},{56,64},{64,7... | collective-permute-start | bytes 2359304 | tf_op jit(solution)/shard_map/ppermute | solution.py:499
  8.6 1.3 copy-start.1
  9.9 1.0 copy-start.7
  10.9 0.9 copy-start.8
  26.3 1.7 %copy-start = (bf16[1024,1664]{1,0:T(8,128)(2,1)}, bf16[1024,1664]{1,0:T(8,128)(2,1)S(1)}, u32[]{:S(2)}) copy-start(bf16[1024,1664]{1,0:T(8,128)(2,1)S(1)} %pack_lines.1) | copy-start | bytes 10223620
  28.0 19.0 %copy-start.6 = (s32[2,1,96]{2,1,0:T(1,128)S(1)}, s32[2,1,96]{2,1,0:T(1,128)}, u32[]{:S(2)}) copy-start(s32[2,1,96]{2,1,0:T(1,128)} %param.14) | copy-start | bytes 2308
  28.0 58.2 %copy-start.12 = (bf16[128,128]{1,0:T(8,128)(2,1)S(1)}, bf16[128,128]{1,0:T(8,128)(2,1)}, u32[]{:S(2)}) copy-start(bf16[128,128]{1,0:T(8,128)(2,1)} %constant.50.clone.fwd_ref) | copy-start | bytes 98308
  28.0 58.2 %copy-start.13 = (bf16[96,128]{1,0:T(8,128)(2,1)S(1)}, bf16[96,128]{1,0:T(8,128)(2,1)}, u32[]{:S(2)}) copy-start(bf16[96,128]{1,0:T(8,128)(2,1)} %constant.54.clone.lift_ref) | copy-start | bytes 73732
  28.0 112.5 %all-to-all-start = ((bf16[128,8,1664]{2,1,0:T(8,128)(2,1)}), bf16[128,8,1664]{2,1,0:T(8,128)(2,1)S(1)}, u32[]{:S(2)}, u32[]{:S(2)}) async-start(bf16[128,8,1664]{2,1,0:T(8,128)(2,1)} %bitcast.19), calls=%async_computation | async-start | bytes 6815744 | tf_op jit(solution)/shard_map/all_to_all | solution.py:533
  48.7 31.3 %collective-permute-start.2 = (bf16[2,288,128]{2,1,0:T(8,128)(2,1)S(1)}, bf16[2,288,128]{2,1,0:T(8,128)(2,1)S(1)}, u32[]{:S(2)}, u32[]{:S(2)}) collective-permute-start(bf16[2,288,128]{2,1,0:T(8,128)(2,1)S(1)} %pad_maximum_fusion), channel_id=1, source_target_pairs={{0,1},{1,2},{2,3},{3,4},{4,5},{5,6},{6,7},{8,9},{9,10},{10,11},{11... | collective-permute-start | bytes 442376 | tf_op jit(solution)/shard_map/ppermute | solution.py:499
  51.6 34.7 %collective-permute-start.3 = (bf16[2,288,128]{2,1,0:T(8,128)(2,1)S(1)}, bf16[2,288,128]{2,1,0:T(8,128)(2,1)S(1)}, u32[]{:S(2)}, u32[]{:S(2)}) collective-permute-start(bf16[2,288,128]{2,1,0:T(8,128)(2,1)S(1)} %pad_maximum_fusion.1), channel_id=1, source_target_pairs={{1,0},{2,1},{3,2},{4,3},{5,4},{6,5},{7,6},{9,8},{10,9},{11,10},{12... | collective-permute-start | bytes 442376 | tf_op jit(solution)/shard_map/ppermute | solution.py:499
  86.3 1.3 copy-start.2
  87.5 1.3 copy-start.5
  88.8 0.9 copy-start.9
  89.7 0.9 copy-start.10
  90.6 0.9 copy-start.11
  110.0 4.5 %collective-permute-start.6 = (bf16[1,8,128]{2,1,0:T(8,128)(2,1)S(1)}, bf16[1,8,128]{2,1,0:T(8,128)(2,1)S(1)}, u32[]{:S(2)}, u32[]{:S(2)}) collective-permute-start(bf16[1,8,128]{2,1,0:T(8,128)(2,1)S(1)} %bitcast.22), channel_id=1, source_target_pairs={{0,3},{1,2},{2,1},{3,0},{4,7},{5,6},{6,5},{7,4},{8,11},{9,10},{10,... | collective-permute-start | bytes 6152 | tf_op jit(solution)/shard_map/ppermute | solution.py:510
  111.8 3.6 %collective-permute-start.5 = (bf16[1,8,128]{2,1,0:T(8,128)(2,1)S(1)}, bf16[1,8,128]{2,1,0:T(8,128)(2,1)S(1)}, u32[]{:S(2)}, u32[]{:S(2)}) collective-permute-start(bf16[1,8,128]{2,1,0:T(8,128)(2,1)S(1)} %bitcast.23), channel_id=1, source_target_pairs={{0,2},{1,3},{2,0},{3,1},{4,6},{5,7},{6,4},{7,5},{8,10},{9,11},{10,... | collective-permute-start | bytes 6152 | tf_op jit(solution)/shard_map/ppermute | solution.py:510
  111.8 3.6 %collective-permute-start.4 = (bf16[1,8,128]{2,1,0:T(8,128)(2,1)S(1)}, bf16[1,8,128]{2,1,0:T(8,128)(2,1)S(1)}, u32[]{:S(2)}, u32[]{:S(2)}) collective-permute-start(bf16[1,8,128]{2,1,0:T(8,128)(2,1)S(1)} %bitcast.24), channel_id=1, source_target_pairs={{0,1},{1,0},{2,3},{3,2},{4,5},{5,4},{6,7},{7,6},{8,9},{9,8},{10,11... | collective-permute-start | bytes 6152 | tf_op jit(solution)/shard_map/ppermute | solution.py:510
  115.4 9.1 %collective-permute-start.9 = (bf16[4,8,128]{2,1,0:T(8,128)(2,1)S(1)}, bf16[4,8,128]{2,1,0:T(8,128)(2,1)S(1)}, u32[]{:S(2)}, u32[]{:S(2)}) collective-permute-start(bf16[4,8,128]{2,1,0:T(8,128)(2,1)S(1)} %pad_maximum_fusion.2), channel_id=1, source_target_pairs={{0,12},{1,13},{2,14},{3,15},{4,8},{5,9},{6,10},{7,11},{8,4},{9,5},... | collective-permute-start | bytes 24584 | tf_op jit(solution)/shard_map/ppermute | solution.py:510
  117.0 7.5 %collective-permute-start.8 = (bf16[4,8,128]{2,1,0:T(8,128)(2,1)S(1)}, bf16[4,8,128]{2,1,0:T(8,128)(2,1)S(1)}, u32[]{:S(2)}, u32[]{:S(2)}) collective-permute-start(bf16[4,8,128]{2,1,0:T(8,128)(2,1)S(1)} %pad_maximum_fusion.2), channel_id=1, source_target_pairs={{0,8},{1,9},{2,10},{3,11},{4,12},{5,13},{6,14},{7,15},{8,0},{9,1},... | collective-permute-start | bytes 24584 | tf_op jit(solution)/shard_map/ppermute | solution.py:510
  119.3 5.2 %collective-permute-start.7 = (bf16[4,8,128]{2,1,0:T(8,128)(2,1)S(1)}, bf16[4,8,128]{2,1,0:T(8,128)(2,1)S(1)}, u32[]{:S(2)}, u32[]{:S(2)}) collective-permute-start(bf16[4,8,128]{2,1,0:T(8,128)(2,1)S(1)} %pad_maximum_fusion.2), channel_id=1, source_target_pairs={{0,4},{1,5},{2,6},{3,7},{4,0},{5,1},{6,2},{7,3},{8,12},{9,13},{10,... | collective-permute-start | bytes 24584 | tf_op jit(solution)/shard_map/ppermute | solution.py:510
  124.5 4.2 %collective-permute-start.10 = (bf16[16,8,128]{2,1,0:T(8,128)(2,1)S(1)}, bf16[16,8,128]{2,1,0:T(8,128)(2,1)S(1)}, u32[]{:S(2)}, u32[]{:S(2)}) collective-permute-start(bf16[16,8,128]{2,1,0:T(8,128)(2,1)S(1)} %get-tuple-element.32), channel_id=1, source_target_pairs={{0,16},{1,17},{2,18},{3,19},{4,20},{5,21},{6,22},{7,23},{8,24},{9,... | collective-permute-start | bytes 98312 | tf_op jit(solution)/shard_map/ppermute | solution.py:510
  125.6 7.6 %collective-permute-start.12 = (bf16[16,8,128]{2,1,0:T(8,128)(2,1)S(1)}, bf16[16,8,128]{2,1,0:T(8,128)(2,1)S(1)}, u32[]{:S(2)}, u32[]{:S(2)}) collective-permute-start(bf16[16,8,128]{2,1,0:T(8,128)(2,1)S(1)} %get-tuple-element.32), channel_id=1, source_target_pairs={{0,48},{1,49},{2,50},{3,51},{4,52},{5,53},{6,54},{7,55},{8,56},{9,... | collective-permute-start | bytes 98312 | tf_op jit(solution)/shard_map/ppermute | solution.py:510
  127.8 5.4 %collective-permute-start.11 = (bf16[16,8,128]{2,1,0:T(8,128)(2,1)S(1)}, bf16[16,8,128]{2,1,0:T(8,128)(2,1)S(1)}, u32[]{:S(2)}, u32[]{:S(2)}) collective-permute-start(bf16[16,8,128]{2,1,0:T(8,128)(2,1)S(1)} %get-tuple-element.32), channel_id=1, source_target_pairs={{0,32},{1,33},{2,34},{3,35},{4,36},{5,37},{6,38},{7,39},{8,40},{9,... | collective-permute-start | bytes 98312 | tf_op jit(solution)/shard_map/ppermute | solution.py:510
  133.2 6.6 %collective-permute-start.13 = (bf16[64,8,128]{2,1,0:T(8,128)(2,1)S(1)}, bf16[64,8,128]{2,1,0:T(8,128)(2,1)S(1)}, u32[]{:S(2)}, u32[]{:S(2)}) collective-permute-start(bf16[64,8,128]{2,1,0:T(8,128)(2,1)S(1)} %get-tuple-element.24), channel_id=1, source_target_pairs={{0,64},{1,65},{2,66},{3,67},{4,68},{5,69},{6,70},{7,71},{8,72},{9,... | collective-permute-start | bytes 393224 | tf_op jit(solution)/shard_map/ppermute | solution.py:510
  139.8 0.7 copy-start.3
  140.5 1.0 copy-start.4

commit v2 on v0

v2 whole, which is shorter than its diff:
```python
import math

import jax
import jax.numpy as jnp
import ml_dtypes
import numpy as np
from jax import lax
from jax.experimental import pallas as pl
from jax.experimental.pallas import tpu as pltpu
from jax.sharding import PartitionSpec as P

CHIP_LEN = 64
OVERSAMPLE = 16
LAG_COUNT = 48
TAP_COUNT = 8
SPACING = 32
MARGIN = 64
PHASE_RATE = 2.0
EPS = 1e-06

TILES = 16
PIECES = 8
OWNERS = 128
LINES = 96
COLS = 3072
BLOCKS = COLS // 128
ALL_LINES = 1536
CHIPS = 96
PAIRS = CHIPS // 2
OWNER_CAP = 32
FIRST_ROW = 16
ROWS = LINES + 2 * MARGIN
HALF = BLOCKS // 2
WIDTH = HALF * 128
LINE_SPAN = 256
SCRATCH_BLOCKS = BLOCKS + 3
GROUP = 8
BOTH = ("az", "rg")
BF = jnp.bfloat16
F32 = jnp.float32


def numpy_tables():
    ids = np.arange(CHIP_LEN)
    angles = -2.0 * math.pi / CHIP_LEN * (ids[:, None] * ids[None, :] % CHIP_LEN)
    scale = 1.0 / math.sqrt(CHIP_LEN)

    def low(values):
        return values.astype(np.float32).astype(ml_dtypes.bfloat16).astype(np.float32)

    four = (low(np.cos(angles) * scale), low(np.sin(angles) * scale))
    steps = np.arange(LAG_COUNT) - LAG_COUNT // 2
    freq = np.where(ids < CHIP_LEN // 2, ids, ids - CHIP_LEN)
    turns = steps[:, None] * freq[None, :] % (OVERSAMPLE * CHIP_LEN)
    lifted = 2.0 * math.pi / (OVERSAMPLE * CHIP_LEN) * turns
    lift = (low(np.cos(lifted) * scale), low(np.sin(lifted) * scale))
    return four, lift


def kernel_table():
    four, lift = numpy_tables()

    def stacked(re, im):
        out = np.zeros((2 * re.shape[0], 256), np.float32)
        out[:, :128] = np.block([[re, -im], [im, re]])
        return out

    def paired(re, im, starts):
        out = np.zeros((2, 128, 2, 2, 64), np.float32)
        count = re.shape[0]
        for chip, first in enumerate(starts):
            rows = slice(first, first + CHIP_LEN)
            out[0, rows, 0, chip, :count] = re.T
            out[0, rows, 1, chip, :count] = im.T
            out[1, rows, 0, chip, :count] = -im.T
            out[1, rows, 1, chip, :count] = re.T
        return out.reshape(256, 256)

    whole = np.concatenate(
        [
            paired(*four, (0, 32)),
            paired(*four, (0, 64)),
            paired(*lift, (0, 64)),
            stacked(*lift),
            stacked(*four),
        ]
    )
    return jnp.asarray(whole.astype(ml_dtypes.bfloat16))


def iota(shape, dim):
    return lax.broadcasted_iota(jnp.int32, shape, dim)


def half_turned(left, right):
    lane = iota(left.shape, 1)
    return pltpu.roll(jnp.where(lane >= 64, left.astype(F32), right.astype(F32)), 64, 1).astype(BF)


def sinc_band(start_ref, taps_ref, block):
    start = start_ref[pl.ds(block, 1), :] - block * 128 + MARGIN
    taps = taps_ref[:, pl.ds(pl.multiple_of(block * 128, 128), 128)].astype(F32)
    offset = iota((256, 128), 0) - start
    band = jnp.zeros((256, 128), F32)
    for tap in range(TAP_COUNT):
        band = jnp.where(offset == tap, taps[tap : tap + 1, :], band)
    return band.astype(BF)


def resample_kernel(
    place_ref, sec_ref, start_ref, taps_ref, src_ref, own_ref, sum_ref, pick_ref, shift_ref
):
    az = place_ref[0]
    rg = place_ref[1]

    line_first = jnp.minimum(jnp.maximum(az * LINES - 8, 0) // 128 * 128, ALL_LINES - LINE_SPAN)
    span = pl.ds(pl.multiple_of(line_first, 128), LINE_SPAN)
    local = src_ref[:, span] - az * LINES
    owner = own_ref[:, span]
    here = (local >= 0) & (local < LINES)
    tagged = jnp.where(here, owner, -1).astype(F32)
    tagged_col = jnp.transpose(jnp.broadcast_to(tagged, (128, LINE_SPAN)))
    tagged_col = jnp.concatenate([tagged_col, tagged_col], axis=1)
    square = (LINE_SPAN, LINE_SPAN)
    earlier = iota(square, 0) < iota(square, 1)
    same = (tagged_col == tagged) & earlier
    rank = jnp.sum(jnp.where(same, 1.0, 0.0), axis=0, keepdims=True)
    slot = jnp.where(here, tagged * 2.0 + rank, -1.0)
    marked = jnp.where(here, local + 1, 0).astype(F32)
    marked_col = jnp.transpose(jnp.broadcast_to(marked, (128, LINE_SPAN))).astype(BF)
    for first in range(0, 1024, 256):
        ids = iota((256, LINE_SPAN), 0) + first
        wanted = ((ids >> 3) * 2 + ((ids >> 1) & 1)).astype(F32)
        hot = jnp.where(slot == wanted, 1.0, 0.0).astype(BF)
        found = jnp.dot(hot, marked_col, preferred_element_type=F32).astype(jnp.int32)
        ids = iota((256, 128), 0) + first
        base = ((ids >> 2) & 1) * (2 * LINES) + (ids & 1) * LINES - 1
        target = jnp.where(found > 0, found + base, -1)
        for block in range(3):
            lanes = iota((256, 128), 1) + block * 128
            pick_ref[first : first + 256, block * 128 : (block + 1) * 128] = jnp.where(
                lanes == target, 1.0, 0.0
            ).astype(BF)

    def move(step, carry):
        at = pl.multiple_of(step * 128, 128)
        shift_ref[:, pl.ds(at, 128)] = half_turned(
            sec_ref[:, pl.ds(pl.multiple_of(at - 128, 128), 128)], sec_ref[:, pl.ds(at, 128)]
        )
        return carry

    lax.fori_loop(1, BLOCKS, move, 0)

    def window(step, carry):
        for member in range(2):
            block = step * 2 + member + 1
            at = pl.multiple_of(block * 128, 128)
            sum_ref[:, pl.ds(at, 128)] = jnp.dot(
                shift_ref[:, pl.ds(at, 256)],
                sinc_band(start_ref, taps_ref, rg * BLOCKS + block),
                preferred_element_type=F32,
            )
        return carry

    lax.fori_loop(0, (BLOCKS - 2) // 2, window, 0)


def resample_inner(place, sec, starts, taps, src, own):
    smem = pl.BlockSpec(memory_space=pltpu.SMEM)
    vmem = pl.BlockSpec(memory_space=pltpu.VMEM)
    return pl.pallas_call(
        resample_kernel,
        out_shape=(
            jax.ShapeDtypeStruct((2 * LINES, COLS), F32),
            jax.ShapeDtypeStruct((OWNERS * 8, 4 * LINES), BF),
        ),
        in_specs=[smem] + [vmem] * 5,
        out_specs=(vmem, vmem),
        scratch_shapes=[pltpu.VMEM((2 * LINES, COLS), BF)],
        compiler_params=pltpu.CompilerParams(vmem_limit_bytes=14 * 2**20),
        cost_estimate=pl.CostEstimate(
            flops=2 * 10**9, bytes_accessed=6 * 10**6, transcendentals=0
        ),
        name="resample_inner",
    )(place, sec, starts, taps, src, own)


def estimate_kernel(
    place_ref,
    off_ref,
    offv_ref,
    ref_ref,
    sec_ref,
    up_ref,
    down_ref,
    left_ref,
    right_ref,
    table_ref,
    start_ref,
    taps_ref,
    sum_ref,
    pick_ref,
    est_ref,
    out_ref,
    rcols_ref,
    scols_ref,
    chips_ref,
    half_ref,
    tot_ref,
    mom_ref,
    lines_ref,
):
    for part in range(2):
        rows = slice(part * CHIP_LEN, (part + 1) * CHIP_LEN)
        rcols_ref[rows, 0:128] = left_ref[part, 0:CHIP_LEN, :]
        rcols_ref[rows, 128 : 128 + COLS] = ref_ref[part, FIRST_ROW : FIRST_ROW + CHIP_LEN, :]
        rcols_ref[rows, 128 + COLS : 256 + COLS] = right_ref[part, 0:CHIP_LEN, :]
        rows = slice(part * ROWS, (part + 1) * ROWS)
        scols_ref[0, rows, :] = left_ref[part, CHIP_LEN:, :].astype(F32)
        scols_ref[SCRATCH_BLOCKS - 2, rows, :] = right_ref[part, CHIP_LEN:, :].astype(F32)
        scols_ref[SCRATCH_BLOCKS - 1, rows, :] = jnp.zeros((ROWS, 128), F32)

    def widen(step, carry):
        for member in range(2):
            block = step * 2 + member
            at = pl.ds(pl.multiple_of(block * 128, 128), 128)
            to = block + 1
            for part in range(2):
                base = part * ROWS
                own = base + MARGIN
                scols_ref[to, base:own, :] = up_ref[part, :, at].astype(F32)
                scols_ref[to, own : own + LINES, :] = sec_ref[part, :, at].astype(F32)
                scols_ref[to, own + LINES : base + ROWS, :] = down_ref[part, :, at].astype(F32)
        return carry

    lax.fori_loop(0, BLOCKS // 2, widen, 0)

    lane = iota((CHIP_LEN, 128), 1)
    lane_all = iota((2 * CHIP_LEN, 128), 1)

    def cut_pair(pair):
        col = pair * 64 + 112
        at = pl.multiple_of((col >> 7) * 128, 128)
        turn = col & 127
        near = rcols_ref[:, pl.ds(at, 128)].astype(F32)
        far = rcols_ref[:, pl.ds(pl.multiple_of(at + 128, 128), 128)].astype(F32)
        both = pltpu.roll(jnp.where(lane_all >= turn, near, far), (128 - turn) & 127, 1)
        to = pl.multiple_of(pair * 128, 128)
        chips_ref[:, pl.ds(to, 128)] = both.astype(BF)
        for part in range(2):
            found = []
            for side in range(2):
                chip = pair * 2 + side
                row = off_ref[0, chip] + (FIRST_ROW + MARGIN + part * ROWS)
                col = chip * SPACING + off_ref[1, chip] + 112
                block = col >> 7
                turn = col & 127
                near = scols_ref[block, pl.ds(row, CHIP_LEN), :]
                far = scols_ref[block + 1, pl.ds(row, CHIP_LEN), :]
                found.append(
                    pltpu.roll(
                        jnp.where(lane >= turn, near, far), (128 + side * 64 - turn) & 127, 1
                    )
                )
            chips_ref[
                part * CHIP_LEN : (part + 1) * CHIP_LEN,
                pl.ds(pl.multiple_of(to + CHIPS * 64, 128), 128),
            ] = jnp.where(lane < 64, found[0], found[1]).astype(BF)

    def cut(step, carry):
        for member in range(2):
            cut_pair(step * 2 + member)
        return carry

    lax.fori_loop(0, PAIRS // 2, cut, 0)

    fwd = table_ref[864:992, 0:128]
    for first in range(0, CHIPS * 128, 1024):
        half_ref[:, first : first + 1024] = jnp.dot(
            fwd, chips_ref[:, first : first + 1024], preferred_element_type=F32
        ).astype(BF)

    lag_row = (iota((LAG_COUNT, 128), 0) - LAG_COUNT // 2).astype(F32) / OVERSAMPLE

    def correlate(step, carry):
        def gathered(base):
            rows = []
            for member in range(GROUP):
                at = pl.ds(pl.multiple_of(base + (step * GROUP + member) * 128, 128), 128)
                rows.append(
                    jnp.concatenate(
                        [half_ref[0:CHIP_LEN, at], half_ref[CHIP_LEN : 2 * CHIP_LEN, at]], axis=1
                    )
                )
            return jnp.concatenate(rows, axis=0)

        spec_ref = jnp.dot(gathered(0), table_ref[0:256, :], preferred_element_type=F32)
        spec_sec = jnp.dot(gathered(CHIPS * 64), table_ref[256:512, :], preferred_element_type=F32)
        rr, ri = spec_ref[:, :128], spec_ref[:, 128:]
        sr, si = spec_sec[:, :128], spec_sec[:, 128:]
        cross = jnp.concatenate([rr * sr + ri * si, ri * sr - rr * si], axis=1).astype(BF)
        middle = jnp.dot(cross, table_ref[512:768, :], preferred_element_type=F32).astype(BF)
        columns = [
            jnp.concatenate(
                [
                    middle[m * CHIP_LEN : (m + 1) * CHIP_LEN, :128],
                    middle[m * CHIP_LEN : (m + 1) * CHIP_LEN, 128:],
                ],
                axis=0,
            )
            for m in range(GROUP)
        ]
        corr = jnp.dot(
            table_ref[768:864, 0:128],
            jnp.concatenate(columns, axis=1),
            preferred_element_type=F32,
        )
        for m in range(GROUP):
            re = corr[:LAG_COUNT, m * 128 : (m + 1) * 128]
            im = corr[LAG_COUNT:, m * 128 : (m + 1) * 128]
            energy = re * re + im * im
            weight = energy * energy
            row = pl.ds(step * GROUP + m, 1)
            tot_ref[row, :] = jnp.sum(weight, axis=0, keepdims=True)
            mom_ref[row, :] = jnp.sum(weight * lag_row, axis=0, keepdims=True)
        return carry

    lax.fori_loop(0, PAIRS // GROUP, correlate, 0)

    wide = (PAIRS, 128)
    lanes = iota(wide, 1)
    total = tot_ref[...]
    moment = mom_ref[...]
    lag_lane = ((lanes & 63) - LAG_COUNT // 2).astype(F32) / OVERSAMPLE
    sides = []
    for side in range(2):
        mask = (lanes < 64) if side == 0 else (lanes >= 64)

        def over(values):
            return jnp.sum(jnp.where(mask, values, 0.0), axis=1, keepdims=True)

        whole = over(total) + EPS
        sides.append((over(moment) / whole, over(total * lag_lane) / whole))
    own = (lanes >> 1) == iota(wide, 0)
    even = (lanes & 1) == 0

    def spread(which):
        values = jnp.where(even, sides[0][which], sides[1][which])
        return jnp.sum(jnp.where(own, values, 0.0), axis=0, keepdims=True)

    offsets = offv_ref[...].astype(F32)
    est_az = offsets[0:1, :] + spread(0)
    est_rg = offsets[1:2, :] + spread(1)
    est_ref[0:1, :] = est_az
    est_ref[1:2, :] = est_rg
    angle = PHASE_RATE * est_az
    cos_all = jnp.broadcast_to(jnp.cos(angle), (8, 128))
    sin_all = jnp.broadcast_to(jnp.sin(angle), (8, 128))

    def turned(block, summed):
        chip = block * 4 + (iota((8, 128), 1) >> 5)
        cosine = jnp.take_along_axis(cos_all, chip, axis=1)[0:1, :]
        sine = jnp.take_along_axis(sin_all, chip, axis=1)[0:1, :]
        re, im = summed[:LINES], summed[LINES:]
        half = block // HALF
        at = slice((block - half * HALF) * 128, (block - half * HALF + 1) * 128)
        base = half * 2 * LINES
        lines_ref[base : base + LINES, at] = (re * cosine + im * sine).astype(BF)
        lines_ref[base + LINES : base + 2 * LINES, at] = (im * cosine - re * sine).astype(BF)

    first_own = CHIP_LEN + MARGIN
    rg = place_ref[1]

    def joined(ref, rows, cols):
        return jnp.concatenate([ref[0, rows, cols], ref[1, rows, cols]], axis=0)

    every = slice(0, LINES)
    rim = slice(first_own, first_own + LINES)
    for block in (0, BLOCKS - 1):
        cols = []
        for at in range(block - 1, block + 2):
            if at < 0:
                cols.append(joined(left_ref, rim, slice(0, 128)))
            elif at >= BLOCKS:
                cols.append(joined(right_ref, rim, slice(0, 128)))
            else:
                cols.append(joined(sec_ref, every, slice(at * 128, (at + 1) * 128)))
        near = jnp.concatenate(
            [half_turned(cols[0], cols[1]), half_turned(cols[1], cols[2])], axis=1
        )
        turned(
            block,
            jnp.dot(
                near,
                sinc_band(start_ref, taps_ref, rg * BLOCKS + block),
                preferred_element_type=F32,
            ),
        )
    for block in range(1, BLOCKS - 1):
        turned(block, sum_ref[:, block * 128 : (block + 1) * 128])
    for first in range(0, WIDTH, 256):
        out_ref[:, first : first + 256] = jnp.dot(
            pick_ref[...], lines_ref[:, first : first + 256], preferred_element_type=F32
        ).astype(BF)


def estimate(place, off, offv, *arrays):
    smem = pl.BlockSpec(memory_space=pltpu.SMEM)
    vmem = pl.BlockSpec(memory_space=pltpu.VMEM)
    return pl.pallas_call(
        estimate_kernel,
        out_shape=(
            jax.ShapeDtypeStruct((2, 128), F32),
            jax.ShapeDtypeStruct((OWNERS * 8, WIDTH), BF),
        ),
        in_specs=[smem] * 2 + [vmem] * 12,
        out_specs=(vmem, vmem),
        scratch_shapes=[
            pltpu.VMEM((2 * CHIP_LEN, SCRATCH_BLOCKS * 128), BF),
            pltpu.VMEM((SCRATCH_BLOCKS, 2 * ROWS, 128), F32),
            pltpu.VMEM((2 * CHIP_LEN, CHIPS * 128), BF),
            pltpu.VMEM((2 * CHIP_LEN, CHIPS * 128), BF),
            pltpu.VMEM((PAIRS, 128), F32),
            pltpu.VMEM((PAIRS, 128), F32),
            pltpu.VMEM((4 * LINES, WIDTH), BF),
        ],
        compiler_params=pltpu.CompilerParams(vmem_limit_bytes=36 * 2**20),
        cost_estimate=pl.CostEstimate(
            flops=6 * 10**9, bytes_accessed=20 * 10**6, transcendentals=0
        ),
        name="estimate",
    )(place, off, offv, *arrays)


def place_kernel(pick_ref, arr_ref, out_ref):
    pick = pick_ref[...]
    for first in range(0, WIDTH, 256):
        lines = jnp.dot(
            pick,
            arr_ref[:, 0, :, first : first + 256].reshape(128, 256),
            preferred_element_type=F32,
        ).astype(BF)
        for half in range(2):
            at = slice(half * WIDTH + first, half * WIDTH + first + 256)
            for part in range(2):
                base = half * 64 + part * OWNER_CAP
                out_ref[part, :, at] = lines[base : base + OWNER_CAP, :]


def place_lines(pick, arrived):
    return pl.pallas_call(
        place_kernel,
        grid=(PIECES,),
        out_shape=jax.ShapeDtypeStruct((2, OWNER_CAP, COLS * PIECES), BF),
        in_specs=[
            pl.BlockSpec((128, 128), lambda r: (0, 0)),
            pl.BlockSpec((TILES, 1, 8, WIDTH), lambda r: (0, r, 0, 0)),
        ],
        out_specs=pl.BlockSpec((2, OWNER_CAP, COLS), lambda r: (0, 0, r)),
        compiler_params=pltpu.CompilerParams(vmem_limit_bytes=20 * 2**20),
        cost_estimate=pl.CostEstimate(
            flops=10**9, bytes_accessed=8 * 10**6, transcendentals=0
        ),
        name="place_lines",
    )(pick, arrived)


def owner_table(src_row, line_owner, me):
    tile = src_row // LINES
    owned = line_owner == me
    ids = jnp.arange(ALL_LINES, dtype=jnp.int32)
    before = owned[None, :] & (ids[None, :] < ids[:, None])
    rank = jnp.sum(before.astype(jnp.int32), axis=1)
    rank_tile = jnp.sum((before & (tile[None, :] == tile[:, None])).astype(jnp.int32), axis=1)
    outs = jnp.arange(OWNER_CAP, dtype=jnp.int32)
    hit = owned[None, :] & (rank[None, :] == outs[:, None])
    code = jnp.sum(jnp.where(hit, (tile * 2 + rank_tile + 1)[None, :], 0), axis=1) - 1
    rows = jnp.arange(128, dtype=jnp.int32)[:, None]
    cols = jnp.arange(128, dtype=jnp.int32)[None, :]
    slot = jnp.tile(code, 4)[:, None]
    pick = (
        (slot == (cols >> 3) * 2 + ((cols >> 1) & 1))
        & ((rows >> 6) == ((cols >> 2) & 1))
        & (((rows >> 5) & 1) == (cols & 1))
    )
    return pick.astype(BF)


def neighbours(axis, first, last):
    count = lax.axis_size(axis)
    up = [(i, i + 1) for i in range(count - 1)]
    down = [(i + 1, i) for i in range(count - 1)]
    return lax.ppermute(last, axis, up), lax.ppermute(first, axis, down)


def per_device(
    reference_slc, secondary_slc, chip_offsets, src_row, line_owner, band_start, band_taps
):
    az = lax.axis_index("az")
    rg = lax.axis_index("rg")
    place = jnp.stack([az, rg]).astype(jnp.int32)
    starts = band_start.reshape(PIECES * BLOCKS, 128)
    up, down = neighbours(
        "az", secondary_slc[:, :MARGIN, :], secondary_slc[:, LINES - MARGIN :, :]
    )

    def edge(cols):
        return jnp.concatenate(
            [
                reference_slc[:, FIRST_ROW : FIRST_ROW + CHIP_LEN, cols],
                up[:, :, cols],
                secondary_slc[:, :, cols],
                down[:, :, cols],
            ],
            axis=1,
        )

    left, right = neighbours("rg", edge(slice(0, 128)), edge(slice(COLS - 128, COLS)))
    summed, pick_sent = resample_inner(
        place,
        secondary_slc.reshape(2 * LINES, COLS),
        starts,
        band_taps,
        src_row.reshape(1, ALL_LINES),
        line_owner.reshape(1, ALL_LINES),
    )
    off = chip_offsets[:, 0, :]
    offv = jnp.pad(off, ((0, 0), (0, 128 - CHIPS)))
    est, packed = estimate(
        place,
        off,
        offv,
        reference_slc,
        secondary_slc,
        up,
        down,
        left,
        right,
        kernel_table(),
        starts,
        band_taps,
        summed,
        pick_sent,
    )
    arrived = lax.all_to_all(packed, BOTH, 0, 0, tiled=True)
    pick = owner_table(src_row, line_owner, az * PIECES + rg)
    resampled = place_lines(pick, arrived.reshape(TILES, PIECES, 8, WIDTH))
    return est[:, None, :CHIPS], resampled


def solution(mesh):
    return jax.shard_map(
        per_device,
        mesh=mesh,
        in_specs=(
            P(None, "az", "rg"),
            P(None, "az", "rg"),
            P(None, "az", "rg"),
            P(),
            P(),
            P(),
            P(),
        ),
        out_specs=(P(None, "az", "rg"), P(None, BOTH, None)),
        check_vma=False,
    )
```

time: 146 us -> 106 us (0.73)
  Pallas kernels: 38.9 us -> 23.3 us
  starting transfers between devices: 43.2 us -> 31 us
  local copies, waits for them, and re-layouts: 11.5 us -> 5.44 us
  waiting for transfers between devices: 45.9 us -> 40.6 us
    all_to_all x1 -> x0, starting transfers between devices: 24.3 us -> none  [per_device(): lax.all_to_all(message.reshape(OWNERS * 8, 128), BOTH, 0, 0, tiled=True)]
    all_to_all x1, starting transfers between devices: 9.75 us -> 22.6 us  [per_device(): arrived = lax.all_to_all(packed, BOTH, 0, 0, tiled=True)]
    unnamed x34 -> x18, local copies, waits for them, and re-layouts: 8.96 us -> 1.7 us
    pallas_call x1, Pallas kernels: 14.5 us -> 7.47 us  [resample_inner(): pl.pallas_call(resample_kernel, out_shape=(jax.ShapeDtypeStruct((2 * LINE...]
    pallas_call x1, Pallas kernels: 17.8 us -> 11.4 us  [estimate(): pl.pallas_call(estimate_kernel, out_shape=(jax.ShapeDtypeStruct((2, 128),...]
    ppermute x4, waiting for transfers between devices: 6.66 us -> 3.95 us  [neighbours(): return (lax.ppermute(last, axis, up), lax.ppermute(first, axis, down))]
    all_to_all x1, waiting for transfers between devices: 39.3 us -> 36.6 us  [per_device(): arrived = lax.all_to_all(packed, BOTH, 0, 0, tiled=True)]
    pallas_call x1, Pallas kernels: 6.51 us -> 4.39 us  [place_lines(): pl.pallas_call(place_kernel, grid=(PIECES,), out_shape=jax.ShapeDtypeStru...]
  transfers between devices with their start and end apart: 6 -> 5, of which waited for: 4 -> 2; matrix products, arithmetic and copies ran while one was open for 4% -> 5% of each run, Pallas kernels for 10% -> 7%
where the time goes in v2:
time: 106 us
  waiting for transfers between devices  40.6 us (38%)
  starting transfers between devices  31 us (29%)
  Pallas kernels  23.3 us (22%)
  local copies, waits for them, and re-layouts  5.44 us (5%)
  other arithmetic  4.52 us (4%)
    all_to_all x1, waiting for transfers between devices, per_device(): arrived = lax.all_to_all(packed, BOTH, 0, 0, tiled=True)  36.6 us
    all_to_all x1, starting transfers between devices, per_device(): arrived = lax.all_to_all(packed, BOTH, 0, 0, tiled=True)  22.6 us
    pallas_call x1, Pallas kernels, estimate(): pl.pallas_call(estimate_kernel, out_shape=(jax.ShapeDtypeStruct((2, 128),...  11.4 us
    ppermute x4, starting transfers between devices, neighbours(): return (lax.ppermute(last, axis, up), lax.ppermute(first, axis, down))  8.47 us
    pallas_call x1, Pallas kernels, resample_inner(): pl.pallas_call(resample_kernel, out_shape=(jax.ShapeDtypeStruct((2 * LINE...  7.47 us
    pallas_call x1, Pallas kernels, place_lines(): pl.pallas_call(place_kernel, grid=(PIECES,), out_shape=jax.ShapeDtypeStru...  4.39 us
    reduce_sum x1, other arithmetic, owner_table(): rank = jnp.sum(before.astype(jnp.int32), axis=1)  4.09 us
    ppermute x4, waiting for transfers between devices, neighbours(): return (lax.ppermute(last, axis, up), lax.ppermute(first, axis, down))  3.95 us
  transfers between devices with their start and end apart: 5, of which 2 were waited for; matrix products, arithmetic and copies ran while one was open for 5% of the time, Pallas kernels for 7%

profile of v2, /device:TPU:0, one launch (start us, length us, event | category | flops | bytes accessed | tf_op | source)
XLA Modules:
  0.0 105.8 jit_solution(14043776568815570074)
XLA Ops:
  0.6 0.0 copy-start.1
  0.6 0.0 copy-start.7
  0.7 0.0 copy-start.8
  0.7 0.0 copy-start.3
  0.7 0.0 copy-start.5
  0.7 0.0 copy-start.4
  0.7 2.8 %fusion.9 = (bf16[2,64,3072]{2,1,0:T(8,128)(2,1)}, bf16[2,64,3072]{2,1,0:T(8,128)(2,1)}) fusion(bf16[2,96,3072]{2,1,0:T(8,128)(2,1)} %sec_ref.1), kind=kLoop, calls=%fused_computation.30 | loop fusion | bytes 3145728 | tf_op jit(solution)/shard_map/slice | solution.py:504
  3.5 1.3 %collective-permute-start = (bf16[2,64,3072]{2,1,0:T(8,128)(2,1)}, bf16[2,64,3072]{2,1,0:T(8,128)(2,1)S(1)}, u32[]{:S(2)}, u32[]{:S(2)}) collective-permute-start(bf16[2,64,3072]{2,1,0:T(8,128)(2,1)} %get-tuple-element.21), channel_id=1, source_target_pairs={{0,8},{8,16},{16,24},{24,32},{32,40},{40,48},{48,56},{56,64},{64,7... | collective-permute-start | bytes 2359304 | tf_op jit(solution)/shard_map/ppermute | solution.py:493
  4.8 1.3 %collective-permute-start.1 = (bf16[2,64,3072]{2,1,0:T(8,128)(2,1)}, bf16[2,64,3072]{2,1,0:T(8,128)(2,1)S(1)}, u32[]{:S(2)}, u32[]{:S(2)}) collective-permute-start(bf16[2,64,3072]{2,1,0:T(8,128)(2,1)} %get-tuple-element.20), channel_id=1, source_target_pairs={{8,0},{16,8},{24,16},{32,24},{40,32},{48,40},{56,48},{64,56},{72,6... | collective-permute-start | bytes 2359304 | tf_op jit(solution)/shard_map/ppermute | solution.py:493
  6.1 0.0 copy-done.7
  6.2 0.0 copy-done.8
  6.2 0.1 pad_add_fusion.place_ref
  6.3 0.8 fusion.7
  7.1 0.0 collective-permute-done.up_ref
  7.1 3.9 %collective-permute-done.1.down_ref = bf16[2,64,3072]{2,1,0:T(8,128)(2,1)S(1)} collective-permute-done((bf16[2,64,3072]{2,1,0:T(8,128)(2,1)}, bf16[2,64,3072]{2,1,0:T(8,128)(2,1)S(1)}, u32[]{:S(2)}, u32[]{:S(2)}) %collective-permute-start.1) | collective-permute-done | bytes 786464 | tf_op jit(solution)/shard_map/ppermute | solution.py:493
  11.1 1.3 %collective-permute-start.3 = (bf16[2,288,128]{2,1,0:T(8,128)(2,1)S(1)}, bf16[2,288,128]{2,1,0:T(8,128)(2,1)S(1)}, u32[]{:S(2)}, u32[]{:S(2)}) collective-permute-start(bf16[2,288,128]{2,1,0:T(8,128)(2,1)S(1)} %pad_maximum_fusion.1), channel_id=1, source_target_pairs={{1,0},{2,1},{3,2},{4,3},{5,4},{6,5},{7,6},{9,8},{10,9},{11,10},{12... | collective-permute-start | bytes 442376 | tf_op jit(solution)/shard_map/ppermute | solution.py:493
  12.4 4.6 %collective-permute-start.2 = (bf16[2,288,128]{2,1,0:T(8,128)(2,1)S(1)}, bf16[2,288,128]{2,1,0:T(8,128)(2,1)S(1)}, u32[]{:S(2)}, u32[]{:S(2)}) collective-permute-start(bf16[2,288,128]{2,1,0:T(8,128)(2,1)S(1)} %pad_maximum_fusion), channel_id=1, source_target_pairs={{0,1},{1,2},{2,3},{3,4},{4,5},{5,6},{6,7},{8,9},{9,10},{10,11},{11... | collective-permute-start | bytes 442376 | tf_op jit(solution)/shard_map/ppermute | solution.py:493
  17.0 0.0 copy-start.2
  17.0 0.0 copy-start.6
  17.0 7.5 %resample_inner.1 = (f32[192,3072]{1,0:T(8,128)S(1)}, bf16[1024,384]{1,0:T(8,128)(2,1)S(1)}) custom-call(s32[2]{0:T(128)S(1)} %pad_add_fusion.place_ref, bf16[192,3072]{1,0:T(8,128)(2,1)S(1)} %bitcast.13, s32[192,128]{1,0:T(8,128)S(1)} %bitcast.16, bf16[8,24576]{1,0:T(8,128)(2,1)S(1)} %copy-done.4, s32[1,1536]{1,0:T(1,128)S(1)} %reshape.72.src_ref, ...), custom_call_target="tpu_custom_call" | custom-call | flops 2000000000 | bytes 6000000 | tf_op jit(solution)/shard_map/resample_inner/pallas_call | solution.py:171
  24.5 0.0 collective-permute-done.3.right_ref
  24.5 0.0 collective-permute-done.2.left_ref
  24.6 11.4 %estimate.1 = (f32[2,128]{1,0:T(2,128)}, bf16[1024,1536]{1,0:T(8,128)(2,1)S(1)}) custom-call(s32[2]{0:T(128)S(1)} %pad_add_fusion.place_ref, s32[2,96]{1,0:T(2,128)S(1)} %bitcast.15, s32[2,128]{1,0:T(2,128)S(1)} %pad.4.offv_ref, bf16[2,96,3072]{2,1,0:T(8,128)(2,1)S(1)} %copy-done.2, bf16[2,96,3072]{2,1,0:T(8,128)(2,1)S(1)} %copy-done.1, ...), custom_call_target="tpu_custom_call" | custom-call | flops 6000000000 | bytes 20000000 | tf_op jit(solution)/shard_map/estimate/pallas_call | solution.py:410
  36.0 0.0 copy-start
  36.0 1.7 %copy-done = bf16[1024,1536]{1,0:T(8,128)(2,1)} copy-done((bf16[1024,1536]{1,0:T(8,128)(2,1)}, bf16[1024,1536]{1,0:T(8,128)(2,1)S(1)}, u32[]{:S(2)}) %copy-start) | copy-done | bytes 3145752
  37.6 22.6 %all-to-all-start = ((bf16[128,8,1536]{2,1,0:T(8,128)(2,1)}), bf16[128,8,1536]{2,1,0:T(8,128)(2,1)S(1)}, u32[]{:S(2)}, u32[]{:S(2)}) async-start(bf16[128,8,1536]{2,1,0:T(8,128)(2,1)} %bitcast.12), calls=%async_computation | async-start | bytes 6291456 | tf_op jit(solution)/shard_map/all_to_all | solution.py:545
  60.3 4.1 %convert_reduce_fusion.1 = (s32[1536]{0:T(1024)S(1)}, s32[1536]{0:T(1024)S(1)}) fusion(pred[1536]{0:T(1024)(128)(4,1)S(1)} %broadcast_compare_fusion, s32[1536]{0:T(1024)S(1)} %add_select_fusion), kind=kLoop, calls=%fused_computation.1 | loop fusion | flops 18871296 | bytes 19968 | tf_op jit(solution)/shard_map/reduce_sum | solution.py:473
  64.4 0.2 select_reduce_fusion
  64.5 0.1 eq.81
  64.6 0.1 and_convert_fusion.pick_ref
  64.8 36.6 %all-to-all-done = bf16[128,8,1536]{2,1,0:T(8,128)(2,1)S(1)} async-done(((bf16[128,8,1536]{2,1,0:T(8,128)(2,1)}), bf16[128,8,1536]{2,1,0:T(8,128)(2,1)S(1)}, u32[]{:S(2)}, u32[]{:S(2)}) %all-to-all-start) | async-done | bytes 3145760 | tf_op jit(solution)/shard_map/all_to_all | solution.py:545
  101.4 4.4 %place_lines.1 = bf16[2,32,24576]{2,1,0:T(8,128)(2,1)} custom-call(bf16[128,128]{1,0:T(8,128)(2,1)S(1)} %and_convert_fusion.pick_ref, bf16[16,8,8,1536]{3,2,1,0:T(8,128)(2,1)S(1)} %bitcast.11), custom_call_target="tpu_custom_call" | custom-call | flops 1000000000 | bytes 8000000 | tf_op jit(solution)/shard_map/place_lines/pallas_call | solution.py:451
  (22 shorter events, 0.2 us)
Async XLA Ops:
  0.6 6.4 %copy-start.1 = (bf16[2,96,3072]{2,1,0:T(8,128)(2,1)S(1)}, bf16[2,96,3072]{2,1,0:T(8,128)(2,1)}, u32[]{:S(2)}) copy-start(bf16[2,96,3072]{2,1,0:T(8,128)(2,1)} %sec_ref.1) | copy-start | bytes 3538948
  0.6 5.5 %copy-start.7 = (s32[1536]{0:T(1024)S(1)}, s32[1536]{0:T(1024)}, u32[]{:S(2)}) copy-start(s32[1536]{0:T(1024)} %param.11) | copy-start | bytes 18436
  0.7 5.5 %copy-start.8 = (s32[1536]{0:T(1024)S(1)}, s32[1536]{0:T(1024)}, u32[]{:S(2)}) copy-start(s32[1536]{0:T(1024)} %param.12) | copy-start | bytes 18436
  0.7 5.5 %copy-start.3 = (s32[2,1,96]{2,1,0:T(1,128)S(1)}, s32[2,1,96]{2,1,0:T(1,128)}, u32[]{:S(2)}) copy-start(s32[2,1,96]{2,1,0:T(1,128)} %param.10) | copy-start | bytes 2308
  0.7 16.3 %copy-start.5 = (s32[24576]{0:T(1024)S(1)}, s32[24576]{0:T(1024)}, u32[]{:S(2)}) copy-start(s32[24576]{0:T(1024)} %param.13) | copy-start | bytes 294916
  0.7 16.3 %copy-start.4 = (bf16[8,24576]{1,0:T(8,128)(2,1)S(1)}, bf16[8,24576]{1,0:T(8,128)(2,1)}, u32[]{:S(2)}) copy-start(bf16[8,24576]{1,0:T(8,128)(2,1)} %taps_ref.3) | copy-start | bytes 1179652
  3.5 3.6 %collective-permute-start = (bf16[2,64,3072]{2,1,0:T(8,128)(2,1)}, bf16[2,64,3072]{2,1,0:T(8,128)(2,1)S(1)}, u32[]{:S(2)}, u32[]{:S(2)}) collective-permute-start(bf16[2,64,3072]{2,1,0:T(8,128)(2,1)} %get-tuple-element.21), channel_id=1, source_target_pairs={{0,8},{8,16},{16,24},{24,32},{32,40},{40,48},{48,56},{56,64},{64,7... | collective-permute-start | bytes 2359304 | tf_op jit(solution)/shard_map/ppermute | solution.py:493
  4.8 6.2 %collective-permute-start.1 = (bf16[2,64,3072]{2,1,0:T(8,128)(2,1)}, bf16[2,64,3072]{2,1,0:T(8,128)(2,1)S(1)}, u32[]{:S(2)}, u32[]{:S(2)}) collective-permute-start(bf16[2,64,3072]{2,1,0:T(8,128)(2,1)} %get-tuple-element.20), channel_id=1, source_target_pairs={{8,0},{16,8},{24,16},{32,24},{40,32},{48,40},{56,48},{64,56},{72,6... | collective-permute-start | bytes 2359304 | tf_op jit(solution)/shard_map/ppermute | solution.py:493
  11.1 13.4 %collective-permute-start.3 = (bf16[2,288,128]{2,1,0:T(8,128)(2,1)S(1)}, bf16[2,288,128]{2,1,0:T(8,128)(2,1)S(1)}, u32[]{:S(2)}, u32[]{:S(2)}) collective-permute-start(bf16[2,288,128]{2,1,0:T(8,128)(2,1)S(1)} %pad_maximum_fusion.1), channel_id=1, source_target_pairs={{1,0},{2,1},{3,2},{4,3},{5,4},{6,5},{7,6},{9,8},{10,9},{11,10},{12... | collective-permute-start | bytes 442376 | tf_op jit(solution)/shard_map/ppermute | solution.py:493
  12.4 12.1 %collective-permute-start.2 = (bf16[2,288,128]{2,1,0:T(8,128)(2,1)S(1)}, bf16[2,288,128]{2,1,0:T(8,128)(2,1)S(1)}, u32[]{:S(2)}, u32[]{:S(2)}) collective-permute-start(bf16[2,288,128]{2,1,0:T(8,128)(2,1)S(1)} %pad_maximum_fusion), channel_id=1, source_target_pairs={{0,1},{1,2},{2,3},{3,4},{4,5},{5,6},{6,7},{8,9},{9,10},{10,11},{11... | collective-permute-start | bytes 442376 | tf_op jit(solution)/shard_map/ppermute | solution.py:493
  17.0 7.5 %copy-start.2 = (bf16[2,96,3072]{2,1,0:T(8,128)(2,1)S(1)}, bf16[2,96,3072]{2,1,0:T(8,128)(2,1)}, u32[]{:S(2)}) copy-start(bf16[2,96,3072]{2,1,0:T(8,128)(2,1)} %ref_ref.1) | copy-start | bytes 3538948
  17.0 7.5 %copy-start.6 = (bf16[992,256]{1,0:T(8,128)(2,1)S(1)}, bf16[992,256]{1,0:T(8,128)(2,1)}, u32[]{:S(2)}) copy-start(bf16[992,256]{1,0:T(8,128)(2,1)} %constant.39.clone.table_ref) | copy-start | bytes 1523716
  36.0 1.7 %copy-start = (bf16[1024,1536]{1,0:T(8,128)(2,1)}, bf16[1024,1536]{1,0:T(8,128)(2,1)S(1)}, u32[]{:S(2)}) copy-start(bf16[1024,1536]{1,0:T(8,128)(2,1)S(1)} %get-tuple-element.9) | copy-start | bytes 9437188
  37.6 63.8 %all-to-all-start = ((bf16[128,8,1536]{2,1,0:T(8,128)(2,1)}), bf16[128,8,1536]{2,1,0:T(8,128)(2,1)S(1)}, u32[]{:S(2)}, u32[]{:S(2)}) async-start(bf16[128,8,1536]{2,1,0:T(8,128)(2,1)} %bitcast.12), calls=%async_computation | async-start | bytes 6291456 | tf_op jit(solution)/shard_map/all_to_all | solution.py:545

commit v3 on v2

--- a/solution.py
+++ b/solution.py
@@ -185,40 +185,199 @@
     )(place, sec, starts, taps, src, own)
 
 
+def rims_kernel(ref_ref, sec_ref, head_ref, tail_ref, first_ref, last_ref, sems):
+    copies = []
+    for part in range(2):
+        pairs = (
+            (sec_ref.at[part, 0:MARGIN, :], head_ref.at[part]),
+            (sec_ref.at[part, LINES - MARGIN : LINES, :], tail_ref.at[part]),
+        )
+        for to_ref, cols in ((first_ref, slice(0, 128)), (last_ref, slice(COLS - 128, COLS))):
+            pairs += (
+                (
+                    ref_ref.at[part, FIRST_ROW : FIRST_ROW + CHIP_LEN, cols],
+                    to_ref.at[part, 0:CHIP_LEN, :],
+                ),
+                (sec_ref.at[part, :, cols], to_ref.at[part, CHIP_LEN : CHIP_LEN + LINES, :]),
+            )
+        copies += pairs
+    started = [
+        pltpu.make_async_copy(src, dst, sems.at[n]) for n, (src, dst) in enumerate(copies)
+    ]
+    for copy in started:
+        copy.start()
+    for copy in started:
+        copy.wait()
+
+
+def rims(ref, sec):
+    hbm = pl.BlockSpec(memory_space=pltpu.HBM)
+    vmem = pl.BlockSpec(memory_space=pltpu.VMEM)
+    rows = jax.ShapeDtypeStruct((2, MARGIN, COLS), BF)
+    cols = jax.ShapeDtypeStruct((2, CHIP_LEN + LINES, 128), BF)
+    return pl.pallas_call(
+        rims_kernel,
+        out_shape=(rows, rows, cols, cols),
+        in_specs=[hbm] * 2,
+        out_specs=(vmem,) * 4,
+        scratch_shapes=[pltpu.SemaphoreType.DMA((12,))],
+        compiler_params=pltpu.CompilerParams(vmem_limit_bytes=4 * 2**20),
+        cost_estimate=pl.CostEstimate(flops=0, bytes_accessed=4 * 10**6, transcendentals=0),
+        name="rims",
+    )(ref, sec)
+
+
+def side_by_side(half_ref, pairs):
+    rows = []
+    for pair in pairs:
+        at = pl.ds(pl.multiple_of(pair * 128, 128), 128)
+        rows.append(
+            jnp.concatenate(
+                [half_ref[0:CHIP_LEN, at], half_ref[CHIP_LEN : 2 * CHIP_LEN, at]], axis=1
+            )
+        )
+    return jnp.concatenate(rows, axis=0)
+
+
+def first_pass(table_ref, chips_ref, half_ref):
+    fwd = table_ref[864:992, 0:128]
+    for first in range(0, CHIPS * 64, 1024):
+        half_ref[:, first : first + 1024] = jnp.dot(
+            fwd, chips_ref[:, first : first + 1024], preferred_element_type=F32
+        ).astype(BF)
+
+
+def reference_kernel(
+    place_ref,
+    ref_ref,
+    sec_ref,
+    left_ref,
+    right_ref,
+    table_ref,
+    start_ref,
+    taps_ref,
+    spec_ref,
+    edge_ref,
+    rcols_ref,
+    chips_ref,
+    half_ref,
+):
+    for part in range(2):
+        rows = slice(part * CHIP_LEN, (part + 1) * CHIP_LEN)
+        rcols_ref[rows, 0:128] = left_ref[part, 0:CHIP_LEN, :]
+        rcols_ref[rows, 128 : 128 + COLS] = ref_ref[part, FIRST_ROW : FIRST_ROW + CHIP_LEN, :]
+        rcols_ref[rows, 128 + COLS : 256 + COLS] = right_ref[part, 0:CHIP_LEN, :]
+
+    lane = iota((2 * CHIP_LEN, 128), 1)
+
+    def cut(step, carry):
+        near = rcols_ref[:, pl.ds(pl.multiple_of(step * 128, 128), 128)].astype(F32)
+        here = rcols_ref[:, pl.ds(pl.multiple_of(step * 128 + 128, 128), 128)].astype(F32)
+        far = rcols_ref[:, pl.ds(pl.multiple_of(step * 128 + 256, 128), 128)].astype(F32)
+        to = pl.multiple_of(step * 256, 256)
+        even = pltpu.roll(jnp.where(lane >= 112, near, here), 16, 1)
+        odd = pltpu.roll(jnp.where(lane >= 48, here, far), 80, 1)
+        chips_ref[:, pl.ds(to, 128)] = even.astype(BF)
+        chips_ref[:, pl.ds(pl.multiple_of(to + 128, 128), 128)] = odd.astype(BF)
+        return carry
+
+    lax.fori_loop(0, PAIRS // 2, cut, 0)
+    first_pass(table_ref, chips_ref, half_ref)
+
+    def second_pass(step, carry):
+        spec_ref[pl.ds(pl.multiple_of(step * GROUP * CHIP_LEN, 512), GROUP * CHIP_LEN), :] = jnp.dot(
+            side_by_side(half_ref, [step * GROUP + m for m in range(GROUP)]),
+            table_ref[0:256, :],
+            preferred_element_type=F32,
+        )
+        return carry
+
+    lax.fori_loop(0, PAIRS // GROUP, second_pass, 0)
+
+    def joined(ref, rows, cols):
+        return jnp.concatenate([ref[0, rows, cols], ref[1, rows, cols]], axis=0)
+
+    every = slice(0, LINES)
+    rim = slice(CHIP_LEN, CHIP_LEN + LINES)
+    one = slice(0, 128)
+    lefts = (joined(left_ref, rim, one), joined(sec_ref, every, one))
+    rights = (joined(sec_ref, every, slice(COLS - 128, COLS)), joined(right_ref, rim, one))
+    after = joined(sec_ref, every, slice(128, 256))
+    before = joined(sec_ref, every, slice(COLS - 256, COLS - 128))
+    windows = ((0, *lefts, after), (BLOCKS - 1, before, *rights))
+    for place, (block, *cols) in enumerate(windows):
+        near = jnp.concatenate(
+            [half_turned(cols[0], cols[1]), half_turned(cols[1], cols[2])], axis=1
+        )
+        edge_ref[:, place * 128 : (place + 1) * 128] = jnp.dot(
+            near,
+            sinc_band(start_ref, taps_ref, place_ref[1] * BLOCKS + block),
+            preferred_element_type=F32,
+        )
+
+
+def reference_side(*arrays):
+    smem = pl.BlockSpec(memory_space=pltpu.SMEM)
+    vmem = pl.BlockSpec(memory_space=pltpu.VMEM)
+    return pl.pallas_call(
+        reference_kernel,
+        out_shape=(
+            jax.ShapeDtypeStruct((PAIRS * CHIP_LEN, 256), F32),
+            jax.ShapeDtypeStruct((2 * LINES, 256), F32),
+        ),
+        in_specs=[smem] + [vmem] * 7,
+        out_specs=(vmem, vmem),
+        scratch_shapes=[
+            pltpu.VMEM((2 * CHIP_LEN, SCRATCH_BLOCKS * 128), BF),
+            pltpu.VMEM((2 * CHIP_LEN, CHIPS * 64), BF),
+            pltpu.VMEM((2 * CHIP_LEN, CHIPS * 64), BF),
+        ],
+        compiler_params=pltpu.CompilerParams(vmem_limit_bytes=16 * 2**20),
+        cost_estimate=pl.CostEstimate(
+            flops=2 * 10**9, bytes_accessed=6 * 10**6, transcendentals=0
+        ),
+        name="reference_side",
+    )(*arrays)
+
+
 def estimate_kernel(
-    place_ref,
     off_ref,
     offv_ref,
-    ref_ref,
     sec_ref,
     up_ref,
     down_ref,
     left_ref,
     right_ref,
+    above_ref,
+    below_ref,
     table_ref,
-    start_ref,
-    taps_ref,
+    spec_ref,
     sum_ref,
+    edge_ref,
     pick_ref,
     est_ref,
     out_ref,
-    rcols_ref,
     scols_ref,
     chips_ref,
     half_ref,
     tot_ref,
     mom_ref,
     lines_ref,
+    packed_ref,
+    sems,
 ):
     for part in range(2):
-        rows = slice(part * CHIP_LEN, (part + 1) * CHIP_LEN)
-        rcols_ref[rows, 0:128] = left_ref[part, 0:CHIP_LEN, :]
-        rcols_ref[rows, 128 : 128 + COLS] = ref_ref[part, FIRST_ROW : FIRST_ROW + CHIP_LEN, :]
-        rcols_ref[rows, 128 + COLS : 256 + COLS] = right_ref[part, 0:CHIP_LEN, :]
-        rows = slice(part * ROWS, (part + 1) * ROWS)
-        scols_ref[0, rows, :] = left_ref[part, CHIP_LEN:, :].astype(F32)
-        scols_ref[SCRATCH_BLOCKS - 2, rows, :] = right_ref[part, CHIP_LEN:, :].astype(F32)
-        scols_ref[SCRATCH_BLOCKS - 1, rows, :] = jnp.zeros((ROWS, 128), F32)
+        base = part * ROWS
+        own = base + MARGIN
+        low = own + LINES
+        for to, side_ref, cols in (
+            (0, left_ref, slice(0, 128)),
+            (SCRATCH_BLOCKS - 2, right_ref, slice(128, 256)),
+        ):
+            scols_ref[to, base:own, :] = above_ref[part, :, cols].astype(F32)
+            scols_ref[to, own:low, :] = side_ref[part, CHIP_LEN:, :].astype(F32)
+            scols_ref[to, low : base + ROWS, :] = below_ref[part, :, cols].astype(F32)
+        scols_ref[SCRATCH_BLOCKS - 1, base : base + ROWS, :] = jnp.zeros((ROWS, 128), F32)
 
     def widen(step, carry):
         for member in range(2):
@@ -236,67 +395,44 @@
     lax.fori_loop(0, BLOCKS // 2, widen, 0)
 
     lane = iota((CHIP_LEN, 128), 1)
-    lane_all = iota((2 * CHIP_LEN, 128), 1)
-
-    def cut_pair(pair):
-        col = pair * 64 + 112
-        at = pl.multiple_of((col >> 7) * 128, 128)
-        turn = col & 127
-        near = rcols_ref[:, pl.ds(at, 128)].astype(F32)
-        far = rcols_ref[:, pl.ds(pl.multiple_of(at + 128, 128), 128)].astype(F32)
-        both = pltpu.roll(jnp.where(lane_all >= turn, near, far), (128 - turn) & 127, 1)
-        to = pl.multiple_of(pair * 128, 128)
-        chips_ref[:, pl.ds(to, 128)] = both.astype(BF)
-        for part in range(2):
-            found = []
-            for side in range(2):
-                chip = pair * 2 + side
-                row = off_ref[0, chip] + (FIRST_ROW + MARGIN + part * ROWS)
-                col = chip * SPACING + off_ref[1, chip] + 112
-                block = col >> 7
-                turn = col & 127
-                near = scols_ref[block, pl.ds(row, CHIP_LEN), :]
-                far = scols_ref[block + 1, pl.ds(row, CHIP_LEN), :]
-                found.append(
-                    pltpu.roll(
-                        jnp.where(lane >= turn, near, far), (128 + side * 64 - turn) & 127, 1
-                    )
-                )
-            chips_ref[
-                part * CHIP_LEN : (part + 1) * CHIP_LEN,
-                pl.ds(pl.multiple_of(to + CHIPS * 64, 128), 128),
-            ] = jnp.where(lane < 64, found[0], found[1]).astype(BF)
 
     def cut(step, carry):
         for member in range(2):
-            cut_pair(step * 2 + member)
+            pair = step * 2 + member
+            to = pl.multiple_of(pair * 128, 128)
+            for part in range(2):
+                found = []
+                for side in range(2):
+                    chip = pair * 2 + side
+                    row = off_ref[0, chip] + (FIRST_ROW + MARGIN + part * ROWS)
+                    col = chip * SPACING + off_ref[1, chip] + 112
+                    block = col >> 7
+                    turn = col & 127
+                    near = scols_ref[block, pl.ds(row, CHIP_LEN), :]
+                    far = scols_ref[block + 1, pl.ds(row, CHIP_LEN), :]
+                    found.append(
+                        pltpu.roll(
+                            jnp.where(lane >= turn, near, far), (128 + side * 64 - turn) & 127, 1
+                        )
+                    )
+                chips_ref[part * CHIP_LEN : (part + 1) * CHIP_LEN, pl.ds(to, 128)] = jnp.where(
+                    lane < 64, found[0], found[1]
+                ).astype(BF)
         return carry
 
     lax.fori_loop(0, PAIRS // 2, cut, 0)
-
-    fwd = table_ref[864:992, 0:128]
-    for first in range(0, CHIPS * 128, 1024):
-        half_ref[:, first : first + 1024] = jnp.dot(
-            fwd, chips_ref[:, first : first + 1024], preferred_element_type=F32
-        ).astype(BF)
+    first_pass(table_ref, chips_ref, half_ref)
 
     lag_row = (iota((LAG_COUNT, 128), 0) - LAG_COUNT // 2).astype(F32) / OVERSAMPLE
 
     def correlate(step, carry):
-        def gathered(base):
-            rows = []
-            for member in range(GROUP):
-                at = pl.ds(pl.multiple_of(base + (step * GROUP + member) * 128, 128), 128)
-                rows.append(
-                    jnp.concatenate(
-                        [half_ref[0:CHIP_LEN, at], half_ref[CHIP_LEN : 2 * CHIP_LEN, at]], axis=1
-                    )
-                )
-            return jnp.concatenate(rows, axis=0)
-
-        spec_ref = jnp.dot(gathered(0), table_ref[0:256, :], preferred_element_type=F32)
-        spec_sec = jnp.dot(gathered(CHIPS * 64), table_ref[256:512, :], preferred_element_type=F32)
-        rr, ri = spec_ref[:, :128], spec_ref[:, 128:]
+        rows = pl.ds(pl.multiple_of(step * GROUP * CHIP_LEN, 512), GROUP * CHIP_LEN)
+        spec_sec = jnp.dot(
+            side_by_side(half_ref, [step * GROUP + m for m in range(GROUP)]),
+            table_ref[256:512, :],
+            preferred_element_type=F32,
+        )
+        rr, ri = spec_ref[rows, :128], spec_ref[rows, 128:]
         sr, si = spec_sec[:, :128], spec_sec[:, 128:]
         cross = jnp.concatenate([rr * sr + ri * si, ri * sr - rr * si], axis=1).astype(BF)
         middle = jnp.dot(cross, table_ref[512:768, :], preferred_element_type=F32).astype(BF)
@@ -341,12 +477,12 @@
 
         whole = over(total) + EPS
         sides.append((over(moment) / whole, over(total * lag_lane) / whole))
-    own = (lanes >> 1) == iota(wide, 0)
+    own_chip = (lanes >> 1) == iota(wide, 0)
     even = (lanes & 1) == 0
 
     def spread(which):
         values = jnp.where(even, sides[0][which], sides[1][which])
-        return jnp.sum(jnp.where(own, values, 0.0), axis=0, keepdims=True)
+        return jnp.sum(jnp.where(own_chip, values, 0.0), axis=0, keepdims=True)
 
     offsets = offv_ref[...].astype(F32)
     est_az = offsets[0:1, :] + spread(0)
@@ -357,7 +493,11 @@
     cos_all = jnp.broadcast_to(jnp.cos(angle), (8, 128))
     sin_all = jnp.broadcast_to(jnp.sin(angle), (8, 128))
 
-    def turned(block, summed):
+    def turned(block):
+        if block in (0, BLOCKS - 1):
+            summed = edge_ref[:, 0:128] if block == 0 else edge_ref[:, 128:256]
+        else:
+            summed = sum_ref[:, block * 128 : (block + 1) * 128]
         chip = block * 4 + (iota((8, 128), 1) >> 5)
         cosine = jnp.take_along_axis(cos_all, chip, axis=1)[0:1, :]
         sine = jnp.take_along_axis(sin_all, chip, axis=1)[0:1, :]
@@ -368,68 +508,52 @@
         lines_ref[base : base + LINES, at] = (re * cosine + im * sine).astype(BF)
         lines_ref[base + LINES : base + 2 * LINES, at] = (im * cosine - re * sine).astype(BF)
 
-    first_own = CHIP_LEN + MARGIN
-    rg = place_ref[1]
-
-    def joined(ref, rows, cols):
-        return jnp.concatenate([ref[0, rows, cols], ref[1, rows, cols]], axis=0)
-
-    every = slice(0, LINES)
-    rim = slice(first_own, first_own + LINES)
-    for block in (0, BLOCKS - 1):
-        cols = []
-        for at in range(block - 1, block + 2):
-            if at < 0:
-                cols.append(joined(left_ref, rim, slice(0, 128)))
-            elif at >= BLOCKS:
-                cols.append(joined(right_ref, rim, slice(0, 128)))
-            else:
-                cols.append(joined(sec_ref, every, slice(at * 128, (at + 1) * 128)))
-        near = jnp.concatenate(
-            [half_turned(cols[0], cols[1]), half_turned(cols[1], cols[2])], axis=1
-        )
-        turned(
-            block,
-            jnp.dot(
-                near,
-                sinc_band(start_ref, taps_ref, rg * BLOCKS + block),
-                preferred_element_type=F32,
-            ),
-        )
-    for block in range(1, BLOCKS - 1):
-        turned(block, sum_ref[:, block * 128 : (block + 1) * 128])
+    copies = []
     for first in range(0, WIDTH, 256):
-        out_ref[:, first : first + 256] = jnp.dot(
-            pick_ref[...], lines_ref[:, first : first + 256], preferred_element_type=F32
+        at = slice(first, first + 256)
+        for block in (first // 128, first // 128 + 1):
+            turned(block)
+            turned(block + HALF)
+        packed_ref[:, at] = jnp.dot(
+            pick_ref[...], lines_ref[:, at], preferred_element_type=F32
         ).astype(BF)
-
-
-def estimate(place, off, offv, *arrays):
+        copy = pltpu.make_async_copy(
+            packed_ref.at[:, at], out_ref.at[:, at], sems.at[first // 256]
+        )
+        copy.start()
+        copies.append(copy)
+    for copy in copies:
+        copy.wait()
+
+
+def estimate(off, offv, *arrays):
     smem = pl.BlockSpec(memory_space=pltpu.SMEM)
     vmem = pl.BlockSpec(memory_space=pltpu.VMEM)
+    hbm = pl.BlockSpec(memory_space=pltpu.HBM)
     return pl.pallas_call(
         estimate_kernel,
         out_shape=(
             jax.ShapeDtypeStruct((2, 128), F32),
             jax.ShapeDtypeStruct((OWNERS * 8, WIDTH), BF),
         ),
-        in_specs=[smem] * 2 + [vmem] * 12,
-        out_specs=(vmem, vmem),
+        in_specs=[smem] + [vmem] * 13,
+        out_specs=(vmem, hbm),
         scratch_shapes=[
-            pltpu.VMEM((2 * CHIP_LEN, SCRATCH_BLOCKS * 128), BF),
             pltpu.VMEM((SCRATCH_BLOCKS, 2 * ROWS, 128), F32),
-            pltpu.VMEM((2 * CHIP_LEN, CHIPS * 128), BF),
-            pltpu.VMEM((2 * CHIP_LEN, CHIPS * 128), BF),
+            pltpu.VMEM((2 * CHIP_LEN, CHIPS * 64), BF),
+            pltpu.VMEM((2 * CHIP_LEN, CHIPS * 64), BF),
             pltpu.VMEM((PAIRS, 128), F32),
             pltpu.VMEM((PAIRS, 128), F32),
             pltpu.VMEM((4 * LINES, WIDTH), BF),
+            pltpu.VMEM((OWNERS * 8, WIDTH), BF),
+            pltpu.SemaphoreType.DMA((WIDTH // 256,)),
         ],
         compiler_params=pltpu.CompilerParams(vmem_limit_bytes=36 * 2**20),
         cost_estimate=pl.CostEstimate(
             flops=6 * 10**9, bytes_accessed=20 * 10**6, transcendentals=0
         ),
         name="estimate",
-    )(place, off, offv, *arrays)
+    )(off, offv, *arrays)
 
 
 def place_kernel(pick_ref, arr_ref, out_ref):
@@ -500,22 +624,19 @@
     rg = lax.axis_index("rg")
     place = jnp.stack([az, rg]).astype(jnp.int32)
     starts = band_start.reshape(PIECES * BLOCKS, 128)
-    up, down = neighbours(
-        "az", secondary_slc[:, :MARGIN, :], secondary_slc[:, LINES - MARGIN :, :]
+    table = kernel_table()
+    head, tail, first, last = rims(reference_slc, secondary_slc)
+    left, right = neighbours("rg", first, last)
+    up, down = neighbours("az", head, tail)
+
+    def corner(rows):
+        return jnp.concatenate([left[:, rows, :], right[:, rows, :]], axis=2)
+
+    above, below = neighbours(
+        "az",
+        corner(slice(CHIP_LEN, CHIP_LEN + MARGIN)),
+        corner(slice(CHIP_LEN + LINES - MARGIN, CHIP_LEN + LINES)),
     )
-
-    def edge(cols):
-        return jnp.concatenate(
-            [
-                reference_slc[:, FIRST_ROW : FIRST_ROW + CHIP_LEN, cols],
-                up[:, :, cols],
-                secondary_slc[:, :, cols],
-                down[:, :, cols],
-            ],
-            axis=1,
-        )
-
-    left, right = neighbours("rg", edge(slice(0, 128)), edge(slice(COLS - 128, COLS)))
     summed, pick_sent = resample_inner(
         place,
         secondary_slc.reshape(2 * LINES, COLS),
@@ -524,22 +645,25 @@
         src_row.reshape(1, ALL_LINES),
         line_owner.reshape(1, ALL_LINES),
     )
+    spectra, edges = reference_side(
+        place, reference_slc, secondary_slc, left, right, table, starts, band_taps
+    )
     off = chip_offsets[:, 0, :]
     offv = jnp.pad(off, ((0, 0), (0, 128 - CHIPS)))
     est, packed = estimate(
-        place,
         off,
         offv,
-        reference_slc,
         secondary_slc,
         up,
         down,
         left,
         right,
-        kernel_table(),
-        starts,
-        band_taps,
+        above,
+        below,
+        table,
+        spectra,
         summed,
+        edges,
         pick_sent,
     )
     arrived = lax.all_to_all(packed, BOTH, 0, 0, tiled=True)

time: 106 us -> 114 us (1.075)
  Pallas kernels: 23.3 us -> 31.7 us
  waiting for transfers between devices: 40.6 us -> 36.6 us
  local copies, waits for them, and re-layouts: 5.44 us -> 8.9 us
    pallas_call x0 -> x2, Pallas kernels: none -> 6.08 us  [the longest x1 5.17 us: reference_side(): pl.pallas_call(reference_kernel, out_shape=(jax.ShapeDtypeStruct((PAIRS *...]
    all_to_all x1, starting transfers between devices: 22.6 us -> 16.5 us  [per_device(): arrived = lax.all_to_all(packed, BOTH, 0, 0, tiled=True)]
    unnamed x18 -> x28, local copies, waits for them, and re-layouts: 1.7 us -> 7.39 us
    ppermute x4 -> x6, starting transfers between devices: 8.47 us -> 14.1 us  [neighbours(): return (lax.ppermute(last, axis, up), lax.ppermute(first, axis, down))]
    ppermute x4 -> x6, waiting for transfers between devices: 3.95 us -> 0.02 us  [neighbours(): return (lax.ppermute(last, axis, up), lax.ppermute(first, axis, down))]
    slice x5 -> x2, local copies, waits for them, and re-layouts: 3.63 us -> 0.02 us  [corner(): return jnp.concatenate([left[:, rows, :], right[:, rows, :]], axis=2)]
    pallas_call x1, Pallas kernels: 11.4 us -> 13.8 us  [estimate(): pl.pallas_call(estimate_kernel, out_shape=(jax.ShapeDtypeStruct((2, 128),...]
  transfers between devices with their start and end apart: 5 -> 7, of which waited for: 2 -> 1; matrix products, arithmetic and copies ran while one was open for 5% -> 5% of each run, Pallas kernels for 7% -> 11%
where the time goes in v3:
time: 114 us; the launch traced here: 113 us
  waiting for transfers between devices  36.6 us (32%)
  Pallas kernels  31.7 us (28%)
  starting transfers between devices  30.7 us (27%)
  local copies, waits for them, and re-layouts  8.9 us (8%)
  other arithmetic  4.51 us (4%)
    all_to_all x1, waiting for transfers between devices, per_device(): arrived = lax.all_to_all(packed, BOTH, 0, 0, tiled=True)  36.6 us
    all_to_all x1, starting transfers between devices, per_device(): arrived = lax.all_to_all(packed, BOTH, 0, 0, tiled=True)  16.5 us
    ppermute x6, starting transfers between devices, neighbours(): return (lax.ppermute(last, axis, up), lax.ppermute(first, axis, down))  14.1 us
    pallas_call x1, Pallas kernels, estimate(): pl.pallas_call(estimate_kernel, out_shape=(jax.ShapeDtypeStruct((2, 128),...  13.8 us
    pallas_call x1, Pallas kernels, resample_inner(): pl.pallas_call(resample_kernel, out_shape=(jax.ShapeDtypeStruct((2 * LINE...  7.47 us
    unnamed x28, local copies, waits for them, and re-layouts  7.39 us
    pallas_call x1, Pallas kernels, reference_side(): pl.pallas_call(reference_kernel, out_shape=(jax.ShapeDtypeStruct((PAIRS *...  5.17 us
    pallas_call x1, Pallas kernels, place_lines(): pl.pallas_call(place_kernel, grid=(PIECES,), out_shape=jax.ShapeDtypeStru...  4.39 us
  transfers between devices with their start and end apart: 7, of which 1 were waited for; matrix products, arithmetic and copies ran while one was open for 5% of the time, Pallas kernels for 11%

profile of v3, /device:TPU:0, one launch (start us, length us, event | category | flops | bytes accessed | tf_op | source)
XLA Modules:
  0.0 113.3 jit_solution(6079318682904264361)
XLA Ops:
  0.6 0.0 copy-start.1
  0.6 1.3 %copy-done.1 = bf16[2,96,3072]{2,1,0:T(8,128)(2,1)S(1)} copy-done((bf16[2,96,3072]{2,1,0:T(8,128)(2,1)S(1)}, bf16[2,96,3072]{2,1,0:T(8,128)(2,1)}, u32[]{:S(2)}) %copy-start.1) | copy-done | bytes 1179672
  1.9 1.3 %copy-done.3 = bf16[2,96,3072]{2,1,0:T(8,128)(2,1)S(1)} copy-done((bf16[2,96,3072]{2,1,0:T(8,128)(2,1)S(1)}, bf16[2,96,3072]{2,1,0:T(8,128)(2,1)}, u32[]{:S(2)}) %copy-start.3) | copy-done | bytes 1179672
  3.2 0.9 rims.1
  4.1 3.5 %collective-permute-start.2 = (bf16[2,160,128]{2,1,0:T(8,128)(2,1)S(1)}, bf16[2,160,128]{2,1,0:T(8,128)(2,1)S(1)}, u32[]{:S(2)}, u32[]{:S(2)}) collective-permute-start(bf16[2,160,128]{2,1,0:T(8,128)(2,1)S(1)} %get-tuple-element.14), channel_id=1, source_target_pairs={{0,1},{1,2},{2,3},{3,4},{4,5},{5,6},{6,7},{8,9},{9,10},{10,11},{11... | collective-permute-start | bytes 245768 | tf_op jit(solution)/shard_map/ppermute | solution.py:617
  7.6 1.3 %collective-permute-start.3 = (bf16[2,160,128]{2,1,0:T(8,128)(2,1)S(1)}, bf16[2,160,128]{2,1,0:T(8,128)(2,1)S(1)}, u32[]{:S(2)}, u32[]{:S(2)}) collective-permute-start(bf16[2,160,128]{2,1,0:T(8,128)(2,1)S(1)} %get-tuple-element.15), channel_id=1, source_target_pairs={{1,0},{2,1},{3,2},{4,3},{5,4},{6,5},{7,6},{9,8},{10,9},{11,10},{12... | collective-permute-start | bytes 245768 | tf_op jit(solution)/shard_map/ppermute | solution.py:617
  8.9 1.5 %collective-permute-start = (bf16[2,64,3072]{2,1,0:T(8,128)(2,1)S(1)}, bf16[2,64,3072]{2,1,0:T(8,128)(2,1)S(1)}, u32[]{:S(2)}, u32[]{:S(2)}) collective-permute-start(bf16[2,64,3072]{2,1,0:T(8,128)(2,1)S(1)} %get-tuple-element.12), channel_id=1, source_target_pairs={{0,8},{8,16},{16,24},{24,32},{32,40},{40,48},{48,56},{56,64},{64,7... | collective-permute-start | bytes 2359304 | tf_op jit(solution)/shard_map/ppermute | solution.py:617
  10.4 1.3 %collective-permute-start.1 = (bf16[2,64,3072]{2,1,0:T(8,128)(2,1)S(1)}, bf16[2,64,3072]{2,1,0:T(8,128)(2,1)S(1)}, u32[]{:S(2)}, u32[]{:S(2)}) collective-permute-start(bf16[2,64,3072]{2,1,0:T(8,128)(2,1)S(1)} %get-tuple-element.13), channel_id=1, source_target_pairs={{8,0},{16,8},{24,16},{32,24},{40,32},{48,40},{56,48},{64,56},{72,6... | collective-permute-start | bytes 2359304 | tf_op jit(solution)/shard_map/ppermute | solution.py:617
  11.7 0.7 reshape.72.src_ref
  12.4 0.7 reshape.73.own_ref
  13.1 0.1 pad_add_fusion.place_ref
  13.2 1.3 %copy-done.4 = bf16[2,96,3072]{2,1,0:T(8,128)(2,1)S(1)} copy-done((bf16[2,96,3072]{2,1,0:T(8,128)(2,1)S(1)}, bf16[2,96,3072]{2,1,0:T(8,128)(2,1)}, u32[]{:S(2)}) %copy-start.4) | copy-done | bytes 1179672
  14.5 1.0 copy-done.7
  15.5 0.9 copy-done.9
  16.4 0.0 copy-start.11
  16.4 7.5 %resample_inner.1 = (f32[192,3072]{1,0:T(8,128)S(1)}, bf16[1024,384]{1,0:T(8,128)(2,1)S(1)}) custom-call(s32[2]{0:T(128)S(1)} %pad_add_fusion.place_ref, bf16[192,3072]{1,0:T(8,128)(2,1)S(1)} %bitcast.13, s32[192,128]{1,0:T(8,128)S(1)} %bitcast.16, bf16[8,24576]{1,0:T(8,128)(2,1)S(1)} %copy-done.7, s32[1,1536]{1,0:T(1,128)S(1)} %reshape.72.src_ref, ...), custom_call_target="tpu_custom_call" | custom-call | flops 2000000000 | bytes 6000000 | tf_op jit(solution)/shard_map/resample_inner/pallas_call | solution.py:171
  23.9 0.0 collective-permute-done.3.right_ref
  24.0 1.3 %collective-permute-start.5 = (bf16[2,64,256]{2,1,0:T(8,128)(2,1)S(1)}, bf16[2,64,256]{2,1,0:T(8,128)(2,1)S(1)}, u32[]{:S(2)}, u32[]{:S(2)}) collective-permute-start(bf16[2,64,256]{2,1,0:T(8,128)(2,1)S(1)} %pad_maximum_fusion.1), channel_id=1, source_target_pairs={{8,0},{16,8},{24,16},{32,24},{40,32},{48,40},{56,48},{64,56},{72,6... | collective-permute-start | bytes 196616 | tf_op jit(solution)/shard_map/ppermute | solution.py:617
  25.3 5.3 %collective-permute-start.4 = (bf16[2,64,256]{2,1,0:T(8,128)(2,1)S(1)}, bf16[2,64,256]{2,1,0:T(8,128)(2,1)S(1)}, u32[]{:S(2)}, u32[]{:S(2)}) collective-permute-start(bf16[2,64,256]{2,1,0:T(8,128)(2,1)S(1)} %pad_maximum_fusion), channel_id=1, source_target_pairs={{0,8},{8,16},{16,24},{24,32},{32,40},{40,48},{48,56},{56,64},{64,7... | collective-permute-start | bytes 196616 | tf_op jit(solution)/shard_map/ppermute | solution.py:617
  30.6 5.2 %reference_side.1 = (f32[3072,256]{1,0:T(8,128)S(1)}, f32[192,256]{1,0:T(8,128)S(1)}) custom-call(s32[2]{0:T(128)S(1)} %pad_add_fusion.place_ref, bf16[2,96,3072]{2,1,0:T(8,128)(2,1)S(1)} %copy-done.2, bf16[2,96,3072]{2,1,0:T(8,128)(2,1)S(1)} %copy-done.5, bf16[2,160,128]{2,1,0:T(8,128)(2,1)S(1)} %collective-permute-done.2.left_ref, ...), custom_call_target="tpu_custom_call" | custom-call | flops 2000000000 | bytes 6000000 | tf_op jit(solution)/shard_map/reference_side/pallas_call | solution.py:322
  35.8 0.0 collective-permute-done.5.below_ref
  35.8 0.0 collective-permute-done.up_ref
  35.8 13.8 %estimate.1 = (f32[2,128]{1,0:T(2,128)}, bf16[1024,1536]{1,0:T(8,128)(2,1)S(1)}) custom-call(s32[2,96]{1,0:T(2,128)S(1)} %bitcast.15, s32[2,128]{1,0:T(2,128)S(1)} %pad.4.offv_ref, bf16[2,96,3072]{2,1,0:T(8,128)(2,1)S(1)} %copy-done.5, bf16[2,64,3072]{2,1,0:T(8,128)(2,1)S(1)} %collective-permute-done.up_ref, ...), custom_call_target="tpu_custom_call" | custom-call | flops 6000000000 | bytes 20000000 | tf_op jit(solution)/shard_map/estimate/pallas_call | solution.py:533
  49.6 0.0 copy-start
  49.6 1.7 %copy-done = bf16[1024,1536]{1,0:T(8,128)(2,1)} copy-done((bf16[1024,1536]{1,0:T(8,128)(2,1)}, bf16[1024,1536]{1,0:T(8,128)(2,1)S(1)}, u32[]{:S(2)}) %copy-start) | copy-done | bytes 3145752
  51.2 16.5 %all-to-all-start = ((bf16[128,8,1536]{2,1,0:T(8,128)(2,1)}), bf16[128,8,1536]{2,1,0:T(8,128)(2,1)S(1)}, u32[]{:S(2)}, u32[]{:S(2)}) async-start(bf16[128,8,1536]{2,1,0:T(8,128)(2,1)} %bitcast.12), calls=%async_computation | async-start | bytes 6291456 | tf_op jit(solution)/shard_map/all_to_all | solution.py:669
  67.8 4.1 %convert_reduce_fusion.1 = (s32[1536]{0:T(1024)S(1)}, s32[1536]{0:T(1024)S(1)}) fusion(pred[1536]{0:T(1024)(128)(4,1)S(1)} %broadcast_compare_fusion, s32[1536]{0:T(1024)S(1)} %add_select_fusion), kind=kLoop, calls=%fused_computation.1 | loop fusion | flops 18871296 | bytes 19968 | tf_op jit(solution)/shard_map/reduce_sum | solution.py:597
  72.0 0.2 select_reduce_fusion
  72.1 0.1 eq.81
  72.2 0.1 and_convert_fusion.pick_ref
  72.3 36.6 %all-to-all-done = bf16[128,8,1536]{2,1,0:T(8,128)(2,1)S(1)} async-done(((bf16[128,8,1536]{2,1,0:T(8,128)(2,1)}), bf16[128,8,1536]{2,1,0:T(8,128)(2,1)S(1)}, u32[]{:S(2)}, u32[]{:S(2)}) %all-to-all-start) | async-done | bytes 3145760 | tf_op jit(solution)/shard_map/all_to_all | solution.py:669
  108.9 4.4 %place_lines.1 = bf16[2,32,24576]{2,1,0:T(8,128)(2,1)} custom-call(bf16[128,128]{1,0:T(8,128)(2,1)S(1)} %and_convert_fusion.pick_ref, bf16[16,8,8,1536]{3,2,1,0:T(8,128)(2,1)S(1)} %bitcast.11), custom_call_target="tpu_custom_call" | custom-call | flops 1000000000 | bytes 8000000 | tf_op jit(solution)/shard_map/place_lines/pallas_call | solution.py:575
  (35 shorter events, 0.1 us)
Async XLA Ops:
  0.6 1.3 %copy-start.1 = (bf16[2,96,3072]{2,1,0:T(8,128)(2,1)S(1)}, bf16[2,96,3072]{2,1,0:T(8,128)(2,1)}, u32[]{:S(2)}) copy-start(bf16[2,96,3072]{2,1,0:T(8,128)(2,1)} %ref_ref.3) | copy-start | bytes 3538948
  1.9 1.3 %copy-start.3 = (bf16[2,96,3072]{2,1,0:T(8,128)(2,1)S(1)}, bf16[2,96,3072]{2,1,0:T(8,128)(2,1)}, u32[]{:S(2)}) copy-start(bf16[2,96,3072]{2,1,0:T(8,128)(2,1)} %sec_ref.5) | copy-start | bytes 3538948
  4.1 19.8 %collective-permute-start.2 = (bf16[2,160,128]{2,1,0:T(8,128)(2,1)S(1)}, bf16[2,160,128]{2,1,0:T(8,128)(2,1)S(1)}, u32[]{:S(2)}, u32[]{:S(2)}) collective-permute-start(bf16[2,160,128]{2,1,0:T(8,128)(2,1)S(1)} %get-tuple-element.14), channel_id=1, source_target_pairs={{0,1},{1,2},{2,3},{3,4},{4,5},{5,6},{6,7},{8,9},{9,10},{10,11},{11... | collective-permute-start | bytes 245768 | tf_op jit(solution)/shard_map/ppermute | solution.py:617
  7.6 16.3 %collective-permute-start.3 = (bf16[2,160,128]{2,1,0:T(8,128)(2,1)S(1)}, bf16[2,160,128]{2,1,0:T(8,128)(2,1)S(1)}, u32[]{:S(2)}, u32[]{:S(2)}) collective-permute-start(bf16[2,160,128]{2,1,0:T(8,128)(2,1)S(1)} %get-tuple-element.15), channel_id=1, source_target_pairs={{1,0},{2,1},{3,2},{4,3},{5,4},{6,5},{7,6},{9,8},{10,9},{11,10},{12... | collective-permute-start | bytes 245768 | tf_op jit(solution)/shard_map/ppermute | solution.py:617
  8.9 26.9 %collective-permute-start = (bf16[2,64,3072]{2,1,0:T(8,128)(2,1)S(1)}, bf16[2,64,3072]{2,1,0:T(8,128)(2,1)S(1)}, u32[]{:S(2)}, u32[]{:S(2)}) collective-permute-start(bf16[2,64,3072]{2,1,0:T(8,128)(2,1)S(1)} %get-tuple-element.12), channel_id=1, source_target_pairs={{0,8},{8,16},{16,24},{24,32},{32,40},{40,48},{48,56},{56,64},{64,7... | collective-permute-start | bytes 2359304 | tf_op jit(solution)/shard_map/ppermute | solution.py:617
  10.4 25.4 %collective-permute-start.1 = (bf16[2,64,3072]{2,1,0:T(8,128)(2,1)S(1)}, bf16[2,64,3072]{2,1,0:T(8,128)(2,1)S(1)}, u32[]{:S(2)}, u32[]{:S(2)}) collective-permute-start(bf16[2,64,3072]{2,1,0:T(8,128)(2,1)S(1)} %get-tuple-element.13), channel_id=1, source_target_pairs={{8,0},{16,8},{24,16},{32,24},{40,32},{48,40},{56,48},{64,56},{72,6... | collective-permute-start | bytes 2359304 | tf_op jit(solution)/shard_map/ppermute | solution.py:617
  13.2 1.3 %copy-start.4 = (bf16[2,96,3072]{2,1,0:T(8,128)(2,1)S(1)}, bf16[2,96,3072]{2,1,0:T(8,128)(2,1)}, u32[]{:S(2)}) copy-start(bf16[2,96,3072]{2,1,0:T(8,128)(2,1)} %sec_ref.5) | copy-start | bytes 3538948
  14.5 1.0 copy-start.7
  15.5 0.9 copy-start.9
  16.3 7.5 %copy-start.6 = (s32[2,1,96]{2,1,0:T(1,128)S(1)}, s32[2,1,96]{2,1,0:T(1,128)}, u32[]{:S(2)}) copy-start(s32[2,1,96]{2,1,0:T(1,128)} %param.10) | copy-start | bytes 2308
  16.4 14.2 %copy-start.2 = (bf16[2,96,3072]{2,1,0:T(8,128)(2,1)S(1)}, bf16[2,96,3072]{2,1,0:T(8,128)(2,1)}, u32[]{:S(2)}) copy-start(bf16[2,96,3072]{2,1,0:T(8,128)(2,1)} %ref_ref.3) | copy-start | bytes 3538948
  16.4 14.2 %copy-start.5 = (bf16[2,96,3072]{2,1,0:T(8,128)(2,1)S(1)}, bf16[2,96,3072]{2,1,0:T(8,128)(2,1)}, u32[]{:S(2)}) copy-start(bf16[2,96,3072]{2,1,0:T(8,128)(2,1)} %sec_ref.5) | copy-start | bytes 3538948
  16.4 14.2 %copy-start.8 = (bf16[8,24576]{1,0:T(8,128)(2,1)S(1)}, bf16[8,24576]{1,0:T(8,128)(2,1)}, u32[]{:S(2)}) copy-start(bf16[8,24576]{1,0:T(8,128)(2,1)} %taps_ref.3) | copy-start | bytes 1179652
  16.4 14.2 %copy-start.10 = (s32[24576]{0:T(1024)S(1)}, s32[24576]{0:T(1024)}, u32[]{:S(2)}) copy-start(s32[24576]{0:T(1024)} %param.13) | copy-start | bytes 294916
  16.4 14.2 %copy-start.11 = (bf16[992,256]{1,0:T(8,128)(2,1)S(1)}, bf16[992,256]{1,0:T(8,128)(2,1)}, u32[]{:S(2)}) copy-start(bf16[992,256]{1,0:T(8,128)(2,1)} %constant.39.clone.table_ref) | copy-start | bytes 1523716
  24.0 11.8 %collective-permute-start.5 = (bf16[2,64,256]{2,1,0:T(8,128)(2,1)S(1)}, bf16[2,64,256]{2,1,0:T(8,128)(2,1)S(1)}, u32[]{:S(2)}, u32[]{:S(2)}) collective-permute-start(bf16[2,64,256]{2,1,0:T(8,128)(2,1)S(1)} %pad_maximum_fusion.1), channel_id=1, source_target_pairs={{8,0},{16,8},{24,16},{32,24},{40,32},{48,40},{56,48},{64,56},{72,6... | collective-permute-start | bytes 196616 | tf_op jit(solution)/shard_map/ppermute | solution.py:617
  25.3 10.5 %collective-permute-start.4 = (bf16[2,64,256]{2,1,0:T(8,128)(2,1)S(1)}, bf16[2,64,256]{2,1,0:T(8,128)(2,1)S(1)}, u32[]{:S(2)}, u32[]{:S(2)}) collective-permute-start(bf16[2,64,256]{2,1,0:T(8,128)(2,1)S(1)} %pad_maximum_fusion), channel_id=1, source_target_pairs={{0,8},{8,16},{16,24},{24,32},{32,40},{40,48},{48,56},{56,64},{64,7... | collective-permute-start | bytes 196616 | tf_op jit(solution)/shard_map/ppermute | solution.py:617
  49.6 1.7 %copy-start = (bf16[1024,1536]{1,0:T(8,128)(2,1)}, bf16[1024,1536]{1,0:T(8,128)(2,1)S(1)}, u32[]{:S(2)}) copy-start(bf16[1024,1536]{1,0:T(8,128)(2,1)S(1)} %get-tuple-element.21) | copy-start | bytes 9437188
  51.2 16.5 %copy-start.13 = (s32[1536]{0:T(1024)S(1)}, s32[1536]{0:T(1024)}, u32[]{:S(2)}) copy-start(s32[1536]{0:T(1024)} %param.12) | copy-start | bytes 18436
  51.2 16.6 %copy-start.12 = (s32[1536]{0:T(1024)S(1)}, s32[1536]{0:T(1024)}, u32[]{:S(2)}) copy-start(s32[1536]{0:T(1024)} %param.11) | copy-start | bytes 18436
  51.2 57.7 %all-to-all-start = ((bf16[128,8,1536]{2,1,0:T(8,128)(2,1)}), bf16[128,8,1536]{2,1,0:T(8,128)(2,1)S(1)}, u32[]{:S(2)}, u32[]{:S(2)}) async-start(bf16[128,8,1536]{2,1,0:T(8,128)(2,1)} %bitcast.12), calls=%async_computation | async-start | bytes 6291456 | tf_op jit(solution)/shard_map/all_to_all | solution.py:669

commit v4 on v3

v4 whole, which is shorter than its diff:
```python
import math

import jax
import jax.numpy as jnp
import ml_dtypes
import numpy as np
from jax import lax
from jax.experimental import pallas as pl
from jax.experimental.pallas import tpu as pltpu
from jax.sharding import PartitionSpec as P

CHIP_LEN = 64
OVERSAMPLE = 16
LAG_COUNT = 48
TAP_COUNT = 8
SPACING = 32
MARGIN = 64
PHASE_RATE = 2.0
EPS = 1e-06

TILES = 16
PIECES = 8
OWNERS = 128
LINES = 96
COLS = 3072
BLOCKS = COLS // 128
ALL_LINES = 1536
CHIPS = 96
PAIRS = CHIPS // 2
OWNER_CAP = 32
FIRST_ROW = 16
ROWS = LINES + 2 * MARGIN
HALF = BLOCKS // 2
WIDTH = HALF * 128
LINE_SPAN = 256
SCRATCH_BLOCKS = BLOCKS + 3
GROUP = 8
RIM_VMEM = 61 * 2**20
BOTH = ("az", "rg")
BF = jnp.bfloat16
F32 = jnp.float32


def numpy_tables():
    ids = np.arange(CHIP_LEN)
    angles = -2.0 * math.pi / CHIP_LEN * (ids[:, None] * ids[None, :] % CHIP_LEN)
    scale = 1.0 / math.sqrt(CHIP_LEN)

    def low(values):
        return values.astype(np.float32).astype(ml_dtypes.bfloat16).astype(np.float32)

    four = (low(np.cos(angles) * scale), low(np.sin(angles) * scale))
    steps = np.arange(LAG_COUNT) - LAG_COUNT // 2
    freq = np.where(ids < CHIP_LEN // 2, ids, ids - CHIP_LEN)
    turns = steps[:, None] * freq[None, :] % (OVERSAMPLE * CHIP_LEN)
    lifted = 2.0 * math.pi / (OVERSAMPLE * CHIP_LEN) * turns
    lift = (low(np.cos(lifted) * scale), low(np.sin(lifted) * scale))
    return four, lift


def kernel_table():
    four, lift = numpy_tables()

    def stacked(re, im):
        out = np.zeros((2 * re.shape[0], 256), np.float32)
        out[:, :128] = np.block([[re, -im], [im, re]])
        return out

    def paired(re, im, starts):
        out = np.zeros((2, 128, 2, 2, 64), np.float32)
        count = re.shape[0]
        for chip, first in enumerate(starts):
            rows = slice(first, first + CHIP_LEN)
            out[0, rows, 0, chip, :count] = re.T
            out[0, rows, 1, chip, :count] = im.T
            out[1, rows, 0, chip, :count] = -im.T
            out[1, rows, 1, chip, :count] = re.T
        return out.reshape(256, 256)

    whole = np.concatenate(
        [
            paired(*four, (0, 32)),
            paired(*four, (0, 64)),
            paired(*lift, (0, 64)),
            stacked(*lift),
            stacked(*four),
        ]
    )
    return jnp.asarray(whole.astype(ml_dtypes.bfloat16))


smem = pl.BlockSpec(memory_space=pltpu.SMEM)
vmem = pl.BlockSpec(memory_space=pltpu.VMEM)
hbm = pl.BlockSpec(memory_space=pltpu.HBM)


def iota(shape, dim):
    return lax.broadcasted_iota(jnp.int32, shape, dim)


def half_turned(left, right):
    lane = iota(left.shape, 1)
    return pltpu.roll(jnp.where(lane >= 64, left.astype(F32), right.astype(F32)), 64, 1).astype(BF)


def begin(sems, *pairs):
    started = [pltpu.make_async_copy(src, dst, sems.at[n]) for n, (src, dst) in enumerate(pairs)]
    for copy in started:
        copy.start()
    return started


def band_copies(rg, start_hbm, taps_hbm, start_ref, taps_ref):
    return (
        (start_hbm.at[pl.ds(pl.multiple_of(rg * BLOCKS, 8), BLOCKS), :], start_ref),
        (taps_hbm.at[:, pl.ds(pl.multiple_of(rg * COLS, 128), COLS)], taps_ref),
    )


def sinc_band(start_ref, taps_ref, block):
    start = start_ref[pl.ds(block, 1), :] - block * 128 + MARGIN
    taps = taps_ref[:, pl.ds(pl.multiple_of(block * 128, 128), 128)].astype(F32)
    offset = iota((256, 128), 0) - start
    band = jnp.zeros((256, 128), F32)
    for tap in range(TAP_COUNT):
        band = jnp.where(offset == tap, taps[tap : tap + 1, :], band)
    return band.astype(BF)


def resample_kernel(
    place_ref,
    sec_hbm,
    start_hbm,
    taps_hbm,
    src_ref,
    own_ref,
    sum_ref,
    pick_ref,
    sec_ref,
    start_ref,
    taps_ref,
    shift_ref,
    sems,
):
    az = place_ref[0]
    rg = place_ref[1]
    fetch = begin(
        sems, (sec_hbm, sec_ref), *band_copies(rg, start_hbm, taps_hbm, start_ref, taps_ref)
    )

    line_block = jnp.minimum(jnp.maximum(az * LINES - 8, 0) // 128, ALL_LINES // 128 - 2)

    def spanned(ref):
        return jnp.concatenate(
            [ref[pl.ds(line_block, 1), :], ref[pl.ds(line_block + 1, 1), :]], axis=1
        )

    local = spanned(src_ref) - az * LINES
    owner = spanned(own_ref)
    here = (local >= 0) & (local < LINES)
    tagged = jnp.where(here, owner, -1).astype(F32)
    tagged_col = jnp.transpose(jnp.broadcast_to(tagged, (128, LINE_SPAN)))
    tagged_col = jnp.concatenate([tagged_col, tagged_col], axis=1)
    square = (LINE_SPAN, LINE_SPAN)
    earlier = iota(square, 0) < iota(square, 1)
    same = (tagged_col == tagged) & earlier
    rank = jnp.sum(jnp.where(same, 1.0, 0.0), axis=0, keepdims=True)
    slot = jnp.where(here, tagged * 2.0 + rank, -1.0)
    marked = jnp.where(here, local + 1, 0).astype(F32)
    marked_col = jnp.transpose(jnp.broadcast_to(marked, (128, LINE_SPAN))).astype(BF)
    for first in range(0, 1024, 256):
        ids = iota((256, LINE_SPAN), 0) + first
        wanted = ((ids >> 3) * 2 + ((ids >> 1) & 1)).astype(F32)
        hot = jnp.where(slot == wanted, 1.0, 0.0).astype(BF)
        found = jnp.dot(hot, marked_col, preferred_element_type=F32).astype(jnp.int32)
        ids = iota((256, 128), 0) + first
        base = ((ids >> 2) & 1) * (2 * LINES) + (ids & 1) * LINES - 1
        target = jnp.where(found > 0, found + base, -1)
        for block in range(3):
            lanes = iota((256, 128), 1) + block * 128
            pick_ref[first : first + 256, block * 128 : (block + 1) * 128] = jnp.where(
                lanes == target, 1.0, 0.0
            ).astype(BF)

    for copy in fetch:
        copy.wait()

    def move(step, carry):
        at = pl.multiple_of(step * 128, 128)
        shift_ref[:, pl.ds(at, 128)] = half_turned(
            sec_ref[:, pl.ds(pl.multiple_of(at - 128, 128), 128)], sec_ref[:, pl.ds(at, 128)]
        )
        return carry

    lax.fori_loop(1, BLOCKS, move, 0)
    start_ref[...] = start_ref[...] - rg * COLS

    def window(step, carry):
        for member in range(2):
            block = step * 2 + member + 1
            at = pl.multiple_of(block * 128, 128)
            sum_ref[:, pl.ds(at, 128)] = jnp.dot(
                shift_ref[:, pl.ds(at, 256)],
                sinc_band(start_ref, taps_ref, block),
                preferred_element_type=F32,
            )
        return carry

    lax.fori_loop(0, (BLOCKS - 2) // 2, window, 0)


def resample_inner(place, sec, starts, taps, src, own):
    return pl.pallas_call(
        resample_kernel,
        out_shape=(
            jax.ShapeDtypeStruct((2 * LINES, COLS), F32),
            jax.ShapeDtypeStruct((OWNERS * 8, 4 * LINES), BF),
        ),
        in_specs=[smem] + [hbm] * 3 + [vmem] * 2,
        out_specs=(vmem, vmem),
        scratch_shapes=[
            pltpu.VMEM((2 * LINES, COLS), BF),
            pltpu.VMEM((BLOCKS, 128), jnp.int32),
            pltpu.VMEM((TAP_COUNT, COLS), BF),
            pltpu.VMEM((2 * LINES, COLS), BF),
            pltpu.SemaphoreType.DMA((3,)),
        ],
        compiler_params=pltpu.CompilerParams(vmem_limit_bytes=16 * 2**20),
        cost_estimate=pl.CostEstimate(
            flops=2 * 10**9, bytes_accessed=6 * 10**6, transcendentals=0
        ),
        name="resample_inner",
    )(place, sec, starts, taps, src, own)


def rims_kernel(sec_hbm, head_ref, tail_ref, sems):
    for copy in begin(
        sems,
        (sec_hbm.at[:, 0:MARGIN, :], head_ref),
        (sec_hbm.at[:, LINES - MARGIN : LINES, :], tail_ref),
    ):
        copy.wait()


def rims(sec):
    rows = jax.ShapeDtypeStruct((2, MARGIN, COLS), BF)
    return pl.pallas_call(
        rims_kernel,
        out_shape=(rows, rows),
        in_specs=[hbm],
        out_specs=(vmem, vmem),
        scratch_shapes=[pltpu.SemaphoreType.DMA((2,))],
        compiler_params=pltpu.CompilerParams(vmem_limit_bytes=RIM_VMEM),
        name="rims",
    )(sec)


def edges_kernel(ref_hbm, sec_hbm, up_ref, down_ref, first_ref, last_ref, sems):
    own = CHIP_LEN + MARGIN
    pairs = []
    for to_ref, cols in ((first_ref, slice(0, 128)), (last_ref, slice(COLS - 128, COLS))):
        pairs += [
            (
                ref_hbm.at[:, FIRST_ROW : FIRST_ROW + CHIP_LEN, cols],
                to_ref.at[:, 0:CHIP_LEN, :],
            ),
            (sec_hbm.at[:, :, cols], to_ref.at[:, own : own + LINES, :]),
        ]
    fetch = begin(sems, *pairs)
    for to_ref, cols in ((first_ref, slice(0, 128)), (last_ref, slice(COLS - 128, COLS))):
        for part in range(2):
            to_ref[part, CHIP_LEN:own, :] = up_ref[part, :, cols]
            to_ref[part, own + LINES :, :] = down_ref[part, :, cols]
    for copy in fetch:
        copy.wait()


def rg_edges(ref, sec, up, down):
    cols = jax.ShapeDtypeStruct((2, CHIP_LEN + ROWS, 128), BF)
    return pl.pallas_call(
        edges_kernel,
        out_shape=(cols, cols),
        in_specs=[hbm, hbm, vmem, vmem],
        out_specs=(vmem, vmem),
        scratch_shapes=[pltpu.SemaphoreType.DMA((4,))],
        compiler_params=pltpu.CompilerParams(vmem_limit_bytes=8 * 2**20),
        name="rg_edges",
    )(ref, sec, up, down)


def side_by_side(half, pairs):
    rows = []
    for pair in pairs:
        if isinstance(pair, int):
            at = slice(pair * 128, (pair + 1) * 128)
        else:
            at = pl.ds(pl.multiple_of(pair * 128, 128), 128)
        rows.append(
            jnp.concatenate([half[0:CHIP_LEN, at], half[CHIP_LEN : 2 * CHIP_LEN, at]], axis=1)
        )
    return jnp.concatenate(rows, axis=0)


def first_pass(table_ref, chips_ref, half_ref):
    fwd = table_ref[864:992, 0:128]
    for first in range(0, CHIPS * 64, 1024):
        half_ref[:, first : first + 1024] = jnp.dot(
            fwd, chips_ref[:, first : first + 1024], preferred_element_type=F32
        ).astype(BF)


def even_pair(near, here):
    lane = iota(near.shape, 1)
    return pltpu.roll(jnp.where(lane >= 112, near, here), 16, 1).astype(BF)


def odd_pair(here, far):
    lane = iota(far.shape, 1)
    return pltpu.roll(jnp.where(lane >= 48, here, far), 80, 1).astype(BF)


def reference_kernel(ref_hbm, table_ref, spec_ref, rcols_ref, chips_ref, half_ref, sems):
    rows = slice(FIRST_ROW, FIRST_ROW + CHIP_LEN)
    fetch = begin(
        sems,
        *(
            (
                ref_hbm.at[part, rows, :],
                rcols_ref.at[part * CHIP_LEN : (part + 1) * CHIP_LEN, 128 : 128 + COLS],
            )
            for part in range(2)
        ),
    )
    none = jnp.zeros((2 * CHIP_LEN, 128), BF)
    rcols_ref[:, 0:128] = none
    rcols_ref[:, 128 + COLS : 256 + COLS] = none
    for copy in fetch:
        copy.wait()

    def cut(step, carry):
        def block(at):
            return rcols_ref[:, pl.ds(pl.multiple_of(at * 128, 128), 128)].astype(F32)

        near, here, far = block(step), block(step + 1), block(step + 2)
        to = pl.multiple_of(step * 256, 256)
        chips_ref[:, pl.ds(to, 128)] = even_pair(near, here)
        chips_ref[:, pl.ds(pl.multiple_of(to + 128, 128), 128)] = odd_pair(here, far)
        return carry

    lax.fori_loop(0, PAIRS // 2, cut, 0)
    first_pass(table_ref, chips_ref, half_ref)

    for step in range(PAIRS // GROUP):
        at = step * GROUP * CHIP_LEN
        spec_ref[at : at + GROUP * CHIP_LEN, :] = jnp.dot(
            side_by_side(half_ref, range(step * GROUP, (step + 1) * GROUP)),
            table_ref[0:256, :],
            preferred_element_type=F32,
        )


def reference_side(ref, table):
    return pl.pallas_call(
        reference_kernel,
        out_shape=jax.ShapeDtypeStruct((PAIRS * CHIP_LEN, 256), F32),
        in_specs=[hbm, vmem],
        out_specs=vmem,
        scratch_shapes=[
            pltpu.VMEM((2 * CHIP_LEN, SCRATCH_BLOCKS * 128), BF),
            pltpu.VMEM((2 * CHIP_LEN, CHIPS * 64), BF),
            pltpu.VMEM((2 * CHIP_LEN, CHIPS * 64), BF),
            pltpu.SemaphoreType.DMA((2,)),
        ],
        compiler_params=pltpu.CompilerParams(vmem_limit_bytes=12 * 2**20),
        cost_estimate=pl.CostEstimate(
            flops=2 * 10**9, bytes_accessed=6 * 10**6, transcendentals=0
        ),
        name="reference_side",
    )(ref, table)


def cut_pair(off_ref, scols_ref, pair, first_block):
    lane = iota((CHIP_LEN, 128), 1)
    parts = []
    for part in range(2):
        found = []
        for side in range(2):
            chip = pair * 2 + side
            row = off_ref[0, chip] + (FIRST_ROW + MARGIN + part * ROWS)
            col = chip * SPACING + off_ref[1, chip] + 112
            block = (col >> 7) - first_block
            turn = col & 127
            near = scols_ref[block, pl.ds(row, CHIP_LEN), :]
            far = scols_ref[block + 1, pl.ds(row, CHIP_LEN), :]
            found.append(
                pltpu.roll(jnp.where(lane >= turn, near, far), (128 + side * 64 - turn) & 127, 1)
            )
        parts.append(jnp.where(lane < 64, found[0], found[1]).astype(BF))
    return parts


def correlated(spec_ref, spec_sec, table_ref, count):
    rr, ri = spec_ref[:, :128], spec_ref[:, 128:]
    sr, si = spec_sec[:, :128], spec_sec[:, 128:]
    cross = jnp.concatenate([rr * sr + ri * si, ri * sr - rr * si], axis=1).astype(BF)
    middle = jnp.dot(cross, table_ref[512:768, :], preferred_element_type=F32).astype(BF)
    columns = []
    for m in range(count):
        rows = middle[m * CHIP_LEN : (m + 1) * CHIP_LEN]
        columns.append(jnp.concatenate([rows[:, :128], rows[:, 128:]], axis=0))
    corr = jnp.dot(
        table_ref[768:864, 0:128], jnp.concatenate(columns, axis=1), preferred_element_type=F32
    )
    lag_row = (iota((LAG_COUNT, 128), 0) - LAG_COUNT // 2).astype(F32) / OVERSAMPLE
    sums = []
    for m in range(count):
        re = corr[:LAG_COUNT, m * 128 : (m + 1) * 128]
        im = corr[LAG_COUNT:, m * 128 : (m + 1) * 128]
        energy = re * re + im * im
        weight = energy * energy
        sums.append(
            (
                jnp.sum(weight, axis=0, keepdims=True),
                jnp.sum(weight * lag_row, axis=0, keepdims=True),
            )
        )
    return sums


def inner_kernel(
    off_ref,
    sec_hbm,
    up_ref,
    down_ref,
    table_ref,
    spec_ref,
    tot_ref,
    mom_ref,
    sec_ref,
    scols_ref,
    chips_ref,
    half_ref,
    sems,
):
    fetch = begin(sems, (sec_hbm, sec_ref))
    none = jnp.zeros((2 * ROWS, 128), F32)
    for block in (0, SCRATCH_BLOCKS - 2, SCRATCH_BLOCKS - 1):
        scols_ref[block] = none

    def widen_rims(step, carry):
        for member in range(2):
            block = step * 2 + member
            at = pl.ds(pl.multiple_of(block * 128, 128), 128)
            for part in range(2):
                base = part * ROWS
                low = base + MARGIN + LINES
                scols_ref[block + 1, base : base + MARGIN, :] = up_ref[part, :, at].astype(F32)
                scols_ref[block + 1, low : base + ROWS, :] = down_ref[part, :, at].astype(F32)
        return carry

    lax.fori_loop(0, BLOCKS // 2, widen_rims, 0)
    for copy in fetch:
        copy.wait()

    def widen(step, carry):
        for member in range(2):
            block = step * 2 + member
            at = pl.ds(pl.multiple_of(block * 128, 128), 128)
            for part in range(2):
                own = part * ROWS + MARGIN
                scols_ref[block + 1, own : own + LINES, :] = sec_ref[part, :, at].astype(F32)
        return carry

    lax.fori_loop(0, BLOCKS // 2, widen, 0)

    def cut(step, carry):
        for member in range(2):
            pair = step * 2 + member
            to = pl.ds(pl.multiple_of(pair * 128, 128), 128)
            re, im = cut_pair(off_ref, scols_ref, pair, 0)
            chips_ref[0:CHIP_LEN, to] = re
            chips_ref[CHIP_LEN : 2 * CHIP_LEN, to] = im
        return carry

    lax.fori_loop(0, PAIRS // 2, cut, 0)
    first_pass(table_ref, chips_ref, half_ref)

    def correlate(step, carry):
        size = GROUP * CHIP_LEN
        spec_sec = jnp.dot(
            side_by_side(half_ref, [step * GROUP + m for m in range(GROUP)]),
            table_ref[256:512, :],
            preferred_element_type=F32,
        )
        spec = spec_ref[pl.ds(pl.multiple_of(step * size, size), size), :]
        for m, (total, moment) in enumerate(correlated(spec, spec_sec, table_ref, GROUP)):
            row = pl.ds(step * GROUP + m, 1)
            tot_ref[row, :] = total
            mom_ref[row, :] = moment
        return carry

    lax.fori_loop(0, PAIRS // GROUP, correlate, 0)


def inner_pairs(off, sec, up, down, table, spectra):
    sums = jax.ShapeDtypeStruct((PAIRS, 128), F32)
    return pl.pallas_call(
        inner_kernel,
        out_shape=(sums, sums),
        in_specs=[smem, hbm] + [vmem] * 4,
        out_specs=(vmem, vmem),
        scratch_shapes=[
            pltpu.VMEM((2, LINES, COLS), BF),
            pltpu.VMEM((SCRATCH_BLOCKS, 2 * ROWS, 128), F32),
            pltpu.VMEM((2 * CHIP_LEN, CHIPS * 64), BF),
            pltpu.VMEM((2 * CHIP_LEN, CHIPS * 64), BF),
            pltpu.SemaphoreType.DMA((1,)),
        ],
        compiler_params=pltpu.CompilerParams(vmem_limit_bytes=24 * 2**20),
        cost_estimate=pl.CostEstimate(
            flops=6 * 10**9, bytes_accessed=20 * 10**6, transcendentals=0
        ),
        name="inner_pairs",
    )(off, sec, up, down, table, spectra)


def finish_kernel(
    place_ref,
    off_ref,
    offv_ref,
    first_ref,
    last_ref,
    sec_hbm,
    start_hbm,
    taps_hbm,
    left_ref,
    right_ref,
    table_ref,
    tot_ref,
    mom_ref,
    sum_hbm,
    pick_hbm,
    est_ref,
    out_ref,
    sum_ref,
    pick_ref,
    near_ref,
    start_ref,
    taps_ref,
    scols_ref,
    lines_ref,
    packed_ref,
    sems,
    out_sems,
):
    rg = place_ref[1]
    fetch = begin(
        sems,
        *band_copies(rg, start_hbm, taps_hbm, start_ref, taps_ref),
        (sec_hbm.at[:, :, 128:256], near_ref.at[0]),
        (sec_hbm.at[:, :, COLS - 256 : COLS - 128], near_ref.at[1]),
        (sum_hbm, sum_ref),
        (pick_hbm, pick_ref),
    )
    own_rows = slice(CHIP_LEN + MARGIN, CHIP_LEN + MARGIN + LINES)
    sides = (
        (left_ref, first_ref, 0),
        (last_ref, right_ref, 3),
    )
    for near_side, far_side, at in sides:
        for part in range(2):
            base = part * ROWS
            scols_ref[at, base : base + ROWS, :] = near_side[part, CHIP_LEN:, :].astype(F32)
            scols_ref[at + 1, base : base + ROWS, :] = far_side[part, CHIP_LEN:, :].astype(F32)
        scols_ref[at + 2] = jnp.zeros((2 * ROWS, 128), F32)

    def both_parts(ref, rows):
        return jnp.concatenate([ref[0, rows, :], ref[1, rows, :]], axis=0)

    chip_rows = slice(0, CHIP_LEN)
    columns = [
        even_pair(
            both_parts(left_ref, chip_rows).astype(F32),
            both_parts(first_ref, chip_rows).astype(F32),
        ),
        odd_pair(
            both_parts(last_ref, chip_rows).astype(F32),
            both_parts(right_ref, chip_rows).astype(F32),
        ),
        jnp.concatenate(cut_pair(off_ref, scols_ref, 0, 0), axis=0),
        jnp.concatenate(cut_pair(off_ref, scols_ref, PAIRS - 1, BLOCKS - 3), axis=0),
    ]
    half = jnp.dot(
        table_ref[864:992, 0:128],
        jnp.concatenate(columns, axis=1),
        preferred_element_type=F32,
    ).astype(BF)
    spec = jnp.dot(
        side_by_side(half, (0, 1)), table_ref[0:256, :], preferred_element_type=F32
    )
    spec_sec = jnp.dot(
        side_by_side(half, (2, 3)), table_ref[256:512, :], preferred_element_type=F32
    )
    outer = correlated(spec, spec_sec, table_ref, 2)

    wide = (PAIRS, 128)
    lanes = iota(wide, 1)
    pairs = iota(wide, 0)

    def completed(ref, which):
        return jnp.where(
            pairs == 0,
            outer[0][which],
            jnp.where(pairs == PAIRS - 1, outer[1][which], ref[...]),
        )

    total = completed(tot_ref, 0)
    moment = completed(mom_ref, 1)
    lag_lane = ((lanes & 63) - LAG_COUNT // 2).astype(F32) / OVERSAMPLE
    found = []
    for side in range(2):
        mask = (lanes < 64) if side == 0 else (lanes >= 64)

        def over(values):
            return jnp.sum(jnp.where(mask, values, 0.0), axis=1, keepdims=True)

        whole = over(total) + EPS
        found.append((over(moment) / whole, over(total * lag_lane) / whole))
    own_chip = (lanes >> 1) == pairs
    even = (lanes & 1) == 0

    def spread(which):
        values = jnp.where(even, found[0][which], found[1][which])
        return jnp.sum(jnp.where(own_chip, values, 0.0), axis=0, keepdims=True)

    offsets = offv_ref[...].astype(F32)
    est_az = offsets[0:1, :] + spread(0)
    est_rg = offsets[1:2, :] + spread(1)
    est_ref[0:1, :] = est_az
    est_ref[1:2, :] = est_rg
    angle = PHASE_RATE * est_az
    cos_all = jnp.broadcast_to(jnp.cos(angle), (8, 128))
    sin_all = jnp.broadcast_to(jnp.sin(angle), (8, 128))

    for copy in fetch:
        copy.wait()
    start_ref[...] = start_ref[...] - rg * COLS
    every = slice(0, LINES)
    edge_columns = {
        0: (
            both_parts(left_ref, own_rows),
            both_parts(first_ref, own_rows),
            both_parts(near_ref.at[0], every),
        ),
        BLOCKS - 1: (
            both_parts(near_ref.at[1], every),
            both_parts(last_ref, own_rows),
            both_parts(right_ref, own_rows),
        ),
    }

    def turned(block):
        if block in edge_columns:
            cols = edge_columns[block]
            near = jnp.concatenate(
                [half_turned(cols[0], cols[1]), half_turned(cols[1], cols[2])], axis=1
            )
            summed = jnp.dot(
                near, sinc_band(start_ref, taps_ref, block), preferred_element_type=F32
            )
        else:
            summed = sum_ref[:, block * 128 : (block + 1) * 128]
        chip = block * 4 + (iota((8, 128), 1) >> 5)
        cosine = jnp.take_along_axis(cos_all, chip, axis=1)[0:1, :]
        sine = jnp.take_along_axis(sin_all, chip, axis=1)[0:1, :]
        re, im = summed[:LINES], summed[LINES:]
        half = block // HALF
        at = slice((block - half * HALF) * 128, (block - half * HALF + 1) * 128)
        base = half * 2 * LINES
        lines_ref[base : base + LINES, at] = (re * cosine + im * sine).astype(BF)
        lines_ref[base + LINES : base + 2 * LINES, at] = (im * cosine - re * sine).astype(BF)

    copies = []
    for first in range(0, WIDTH, 256):
        at = slice(first, first + 256)
        for block in (first // 128, first // 128 + 1):
            turned(block)
            turned(block + HALF)
        packed_ref[:, at] = jnp.dot(
            pick_ref[...], lines_ref[:, at], preferred_element_type=F32
        ).astype(BF)
        copy = pltpu.make_async_copy(
            packed_ref.at[:, at], out_ref.at[:, at], out_sems.at[first // 256]
        )
        copy.start()
        copies.append(copy)
    for copy in copies:
        copy.wait()


def finish(place, off, offv, first, last, *arrays):
    return pl.pallas_call(
        finish_kernel,
        out_shape=(
            jax.ShapeDtypeStruct((2, 128), F32),
            jax.ShapeDtypeStruct((OWNERS * 8, WIDTH), BF),
        ),
        in_specs=[smem] * 2 + [vmem] * 3 + [hbm] * 3 + [vmem] * 5 + [hbm] * 2,
        out_specs=(vmem, hbm),
        scratch_shapes=[
            pltpu.VMEM((2 * LINES, COLS), F32),
            pltpu.VMEM((OWNERS * 8, 4 * LINES), BF),
            pltpu.VMEM((2, 2, LINES, 128), BF),
            pltpu.VMEM((BLOCKS, 128), jnp.int32),
            pltpu.VMEM((TAP_COUNT, COLS), BF),
            pltpu.VMEM((6, 2 * ROWS, 128), F32),
            pltpu.VMEM((4 * LINES, WIDTH), BF),
            pltpu.VMEM((OWNERS * 8, WIDTH), BF),
            pltpu.SemaphoreType.DMA((6,)),
            pltpu.SemaphoreType.DMA((WIDTH // 256,)),
        ],
        compiler_params=pltpu.CompilerParams(vmem_limit_bytes=52 * 2**20),
        cost_estimate=pl.CostEstimate(
            flops=2 * 10**9, bytes_accessed=10 * 10**6, transcendentals=0
        ),
        name="finish",
    )(place, off, offv, first, last, *arrays)


def place_kernel(pick_ref, arr_ref, out_ref):
    pick = pick_ref[...]
    for first in range(0, WIDTH, 256):
        lines = jnp.dot(
            pick,
            arr_ref[:, 0, :, first : first + 256].reshape(128, 256),
            preferred_element_type=F32,
        ).astype(BF)
        for half in range(2):
            at = slice(half * WIDTH + first, half * WIDTH + first + 256)
            for part in range(2):
                base = half * 64 + part * OWNER_CAP
                out_ref[part, :, at] = lines[base : base + OWNER_CAP, :]


def place_lines(pick, arrived):
    return pl.pallas_call(
        place_kernel,
        grid=(PIECES,),
        out_shape=jax.ShapeDtypeStruct((2, OWNER_CAP, COLS * PIECES), BF),
        in_specs=[
            pl.BlockSpec((128, 128), lambda r: (0, 0)),
            pl.BlockSpec((TILES, 1, 8, WIDTH), lambda r: (0, r, 0, 0)),
        ],
        out_specs=pl.BlockSpec((2, OWNER_CAP, COLS), lambda r: (0, 0, r)),
        compiler_params=pltpu.CompilerParams(vmem_limit_bytes=20 * 2**20),
        cost_estimate=pl.CostEstimate(
            flops=10**9, bytes_accessed=8 * 10**6, transcendentals=0
        ),
        name="place_lines",
    )(pick, arrived)


def owner_table(src_row, line_owner, me):
    tile = src_row // LINES
    owned = line_owner == me
    ids = jnp.arange(ALL_LINES, dtype=jnp.int32)
    before = owned[None, :] & (ids[None, :] < ids[:, None])
    rank = jnp.sum(before.astype(jnp.int32), axis=1)
    rank_tile = jnp.sum((before & (tile[None, :] == tile[:, None])).astype(jnp.int32), axis=1)
    outs = jnp.arange(OWNER_CAP, dtype=jnp.int32)
    hit = owned[None, :] & (rank[None, :] == outs[:, None])
    code = jnp.sum(jnp.where(hit, (tile * 2 + rank_tile + 1)[None, :], 0), axis=1) - 1
    rows = jnp.arange(128, dtype=jnp.int32)[:, None]
    cols = jnp.arange(128, dtype=jnp.int32)[None, :]
    slot = jnp.tile(code, 4)[:, None]
    pick = (
        (slot == (cols >> 3) * 2 + ((cols >> 1) & 1))
        & ((rows >> 6) == ((cols >> 2) & 1))
        & (((rows >> 5) & 1) == (cols & 1))
    )
    return pick.astype(BF)


def neighbours(axis, first, last):
    count = lax.axis_size(axis)
    up = [(i, i + 1) for i in range(count - 1)]
    down = [(i + 1, i) for i in range(count - 1)]
    return lax.ppermute(last, axis, up), lax.ppermute(first, axis, down)


def per_device(
    reference_slc, secondary_slc, chip_offsets, src_row, line_owner, band_start, band_taps
):
    az = lax.axis_index("az")
    rg = lax.axis_index("rg")
    place = jnp.stack([az, rg]).astype(jnp.int32)
    starts = band_start.reshape(PIECES * BLOCKS, 128)
    table = kernel_table()
    up, down = neighbours("az", *rims(secondary_slc))
    summed, pick_sent = resample_inner(
        place,
        secondary_slc.reshape(2 * LINES, COLS),
        starts,
        band_taps,
        src_row.reshape(ALL_LINES // 128, 128),
        line_owner.reshape(ALL_LINES // 128, 128),
    )
    spectra = reference_side(reference_slc, table)
    first, last = rg_edges(reference_slc, secondary_slc, up, down)
    left, right = neighbours("rg", first, last)
    off = chip_offsets[:, 0, :]
    offv = jnp.pad(off, ((0, 0), (0, 128 - CHIPS)))
    total, moment = inner_pairs(off, secondary_slc, up, down, table, spectra)
    est, packed = finish(
        place,
        off,
        offv,
        first,
        last,
        secondary_slc,
        starts,
        band_taps,
        left,
        right,
        table,
        total,
        moment,
        summed,
        pick_sent,
    )
    arrived = lax.all_to_all(packed, BOTH, 0, 0, tiled=True)
    pick = owner_table(src_row, line_owner, az * PIECES + rg)
    resampled = place_lines(pick, arrived.reshape(TILES, PIECES, 8, WIDTH))
    return est[:, None, :CHIPS], resampled


def solution(mesh):
    return jax.shard_map(
        per_device,
        mesh=mesh,
        in_specs=(
            P(None, "az", "rg"),
            P(None, "az", "rg"),
            P(None, "az", "rg"),
            P(),
            P(),
            P(),
            P(),
        ),
        out_specs=(P(None, "az", "rg"), P(None, BOTH, None)),
        check_vma=False,
    )
```

time: 114 us -> 105 us (0.921)
  starting transfers between devices: 30.7 us -> 24.6 us
  local copies, waits for them, and re-layouts: 8.9 us -> 4.01 us
  Pallas kernels: 31.7 us -> 33.9 us
    ppermute x6 -> x4, starting transfers between devices: 14.1 us -> 7.99 us  [neighbours(): return (lax.ppermute(last, axis, up), lax.ppermute(first, axis, down))]
    unnamed x28 -> x24, local copies, waits for them, and re-layouts: 7.39 us -> 3.24 us
    pallas_call x3 -> x5, Pallas kernels: 19.8 us -> 21.7 us  [the longest x1 8.37 us: inner_pairs(): pl.pallas_call(inner_kernel, out_shape=(sums, sums), in_specs=[smem, hbm]...]
    reshape x2 -> x0, local copies, waits for them, and re-layouts: 1.41 us -> none  [the longest x1 0.7 us: per_device(): src_row.reshape(1, ALL_LINES)]
  transfers between devices with their start and end apart: 7 -> 5, of which waited for: 1 -> 1; matrix products, arithmetic and copies ran while one was open for 5% -> 5% of each run, Pallas kernels for 11% -> 19%
where the time goes in v4:
time: 105 us; the launch traced here: 104 us
  waiting for transfers between devices  36.6 us (35%)
  Pallas kernels  33.9 us (32%)
  starting transfers between devices  24.6 us (23%)
  other arithmetic  4.5 us (4%)
  local copies, waits for them, and re-layouts  4.01 us (4%)
    all_to_all x1, waiting for transfers between devices, per_device(): arrived = lax.all_to_all(packed, BOTH, 0, 0, tiled=True)  36.6 us
    all_to_all x1, starting transfers between devices, per_device(): arrived = lax.all_to_all(packed, BOTH, 0, 0, tiled=True)  16.6 us
    pallas_call x1, Pallas kernels, inner_pairs(): pl.pallas_call(inner_kernel, out_shape=(sums, sums), in_specs=[smem, hbm]...  8.37 us
    ppermute x4, starting transfers between devices, neighbours(): return (lax.ppermute(last, axis, up), lax.ppermute(first, axis, down))  7.99 us
    pallas_call x1, Pallas kernels, resample_inner(): pl.pallas_call(resample_kernel, out_shape=(jax.ShapeDtypeStruct((2 * LINE...  7.81 us
    pallas_call x1, Pallas kernels, finish(): pl.pallas_call(finish_kernel, out_shape=(jax.ShapeDtypeStruct((2, 128), F...  7.28 us
    pallas_call x1, Pallas kernels, place_lines(): pl.pallas_call(place_kernel, grid=(PIECES,), out_shape=jax.ShapeDtypeStru...  4.39 us
    reduce_sum x1, other arithmetic, owner_table(): rank = jnp.sum(before.astype(jnp.int32), axis=1)  4.11 us
  transfers between devices with their start and end apart: 5, of which 1 were waited for; matrix products, arithmetic and copies ran while one was open for 5% of the time, Pallas kernels for 19%

profile of v4, /device:TPU:0, one launch (start us, length us, event | category | flops | bytes accessed | tf_op | source)
XLA Modules:
  0.0 104.5 jit_solution(940141251335757790)
XLA Ops:
  0.6 2.5 %rims.1 = (bf16[2,64,3072]{2,1,0:T(8,128)(2,1)}, bf16[2,64,3072]{2,1,0:T(8,128)(2,1)}) custom-call(bf16[2,96,3072]{2,1,0:T(8,128)(2,1)} %sec_hbm.7), custom_call_target="tpu_custom_call" | custom-call | tf_op jit(solution)/shard_map/rims/pallas_call | solution.py:247
  3.2 1.3 %collective-permute-start = (bf16[2,64,3072]{2,1,0:T(8,128)(2,1)}, bf16[2,64,3072]{2,1,0:T(8,128)(2,1)S(1)}, u32[]{:S(2)}, u32[]{:S(2)}) collective-permute-start(bf16[2,64,3072]{2,1,0:T(8,128)(2,1)} %get-tuple-element.12), channel_id=1, source_target_pairs={{0,8},{8,16},{16,24},{24,32},{32,40},{40,48},{48,56},{56,64},{64,7... | collective-permute-start | bytes 2359304 | tf_op jit(solution)/shard_map/ppermute | solution.py:788
  4.5 1.3 %collective-permute-start.1 = (bf16[2,64,3072]{2,1,0:T(8,128)(2,1)}, bf16[2,64,3072]{2,1,0:T(8,128)(2,1)S(1)}, u32[]{:S(2)}, u32[]{:S(2)}) collective-permute-start(bf16[2,64,3072]{2,1,0:T(8,128)(2,1)} %get-tuple-element.13), channel_id=1, source_target_pairs={{8,0},{16,8},{24,16},{32,24},{40,32},{48,40},{56,48},{64,56},{72,6... | collective-permute-start | bytes 2359304 | tf_op jit(solution)/shard_map/ppermute | solution.py:788
  5.8 0.7 pad.4.offv_ref
  6.5 0.1 pad_add_fusion.place_ref
  6.6 1.3 %copy-done.1 = bf16[2,96,3072]{2,1,0:T(8,128)(2,1)S(1)} copy-done((bf16[2,96,3072]{2,1,0:T(8,128)(2,1)S(1)}, bf16[2,96,3072]{2,1,0:T(8,128)(2,1)}, u32[]{:S(2)}) %copy-start.1) | copy-done | bytes 1179672
  7.9 1.0 copy-done.8
  8.9 0.0 copy-start.7
  8.9 3.4 %reference_side.1.spec_ref = f32[3072,256]{1,0:T(8,128)S(1)} custom-call(bf16[2,96,3072]{2,1,0:T(8,128)(2,1)S(1)} %copy-done.1, bf16[992,256]{1,0:T(8,128)(2,1)S(1)} %copy-done.8), custom_call_target="tpu_custom_call" | custom-call | flops 2000000000 | bytes 6000000 | tf_op jit(solution)/shard_map/reference_side/pallas_call | solution.py:363
  12.3 0.0 copy-done
  12.3 0.0 copy-done.3
  12.3 0.0 copy-done.4
  12.3 0.0 copy-done.6
  12.3 0.0 copy-start.2
  12.4 7.8 %resample_inner.1 = (f32[192,3072]{1,0:T(8,128)S(1)}, bf16[1024,384]{1,0:T(8,128)(2,1)S(1)}) custom-call(s32[2]{0:T(128)S(1)} %pad_add_fusion.place_ref, bf16[192,3072]{1,0:T(8,128)(2,1)S(1)} %bitcast.14, s32[192,128]{1,0:T(8,128)S(1)} %bitcast.20, bf16[8,24576]{1,0:T(8,128)(2,1)S(1)} %copy-done.6, s32[12,128]{1,0:T(8,128)S(1)} %bitcast.15, ...), custom_call_target="tpu_custom_call" | custom-call | flops 2000000000 | bytes 6000000 | tf_op jit(solution)/shard_map/resample_inner/pallas_call | solution.py:213
  20.2 0.9 copy-done.11
  21.1 0.0 collective-permute-done.up_ref
  21.1 0.0 collective-permute-done.1.down_ref
  21.1 0.1 rg_edges.1
  21.2 4.1 %collective-permute-start.2 = (bf16[2,288,128]{2,1,0:T(8,128)(2,1)S(1)}, bf16[2,288,128]{2,1,0:T(8,128)(2,1)S(1)}, u32[]{:S(2)}, u32[]{:S(2)}) collective-permute-start(bf16[2,288,128]{2,1,0:T(8,128)(2,1)S(1)} %get-tuple-element.15.last_ref), channel_id=1, source_target_pairs={{0,1},{1,2},{2,3},{3,4},{4,5},{5,6},{6,7},{8,9},{9,10},{10,11},{11... | collective-permute-start | bytes 442376 | tf_op jit(solution)/shard_map/ppermute | solution.py:788
  25.3 1.3 %collective-permute-start.3 = (bf16[2,288,128]{2,1,0:T(8,128)(2,1)S(1)}, bf16[2,288,128]{2,1,0:T(8,128)(2,1)S(1)}, u32[]{:S(2)}, u32[]{:S(2)}) collective-permute-start(bf16[2,288,128]{2,1,0:T(8,128)(2,1)S(1)} %get-tuple-element.14.first_ref), channel_id=1, source_target_pairs={{1,0},{2,1},{3,2},{4,3},{5,4},{6,5},{7,6},{9,8},{10,9},{11,10},{12... | collective-permute-start | bytes 442376 | tf_op jit(solution)/shard_map/ppermute | solution.py:788
  26.6 8.4 %inner_pairs.1 = (f32[48,128]{1,0:T(8,128)S(1)}, f32[48,128]{1,0:T(8,128)S(1)}) custom-call(s32[2,96]{1,0:T(2,128)S(1)} %bitcast.18, bf16[2,96,3072]{2,1,0:T(8,128)(2,1)S(1)} %copy-done, bf16[2,64,3072]{2,1,0:T(8,128)(2,1)S(1)} %collective-permute-done.up_ref, bf16[2,64,3072]{2,1,0:T(8,128)(2,1)S(1)} %collective-permute-done.1.down_ref, ...), custom_call_target="tpu_custom_call" | custom-call | flops 6000000000 | bytes 20000000 | tf_op jit(solution)/shard_map/inner_pairs/pallas_call | solution.py:507
  35.0 0.0 collective-permute-done.2.left_ref
  35.0 0.0 collective-permute-done.3.right_ref
  35.0 7.3 %finish.1 = (f32[2,128]{1,0:T(2,128)}, bf16[1024,1536]{1,0:T(8,128)(2,1)}) custom-call(s32[2]{0:T(128)S(1)} %pad_add_fusion.place_ref, s32[2,96]{1,0:T(2,128)S(1)} %bitcast.19, s32[2,128]{1,0:T(2,128)S(1)} %pad.4.offv_ref, bf16[2,288,128]{2,1,0:T(8,128)(2,1)S(1)} %get-tuple-element.14.first_ref, bf16[2,288,128]{2,1,0:T(8,128)(2,1)S(1)} %get-tuple-element.15.last_ref, ...), custom_call_target="tpu_custom_call" | custom-call | flops 2000000000 | bytes 10000000 | tf_op jit(solution)/shard_map/finish/pallas_call | solution.py:702
  42.3 16.6 %all-to-all-start = ((bf16[128,8,1536]{2,1,0:T(8,128)(2,1)}), bf16[128,8,1536]{2,1,0:T(8,128)(2,1)S(1)}, u32[]{:S(2)}, u32[]{:S(2)}) async-start(bf16[128,8,1536]{2,1,0:T(8,128)(2,1)} %bitcast.22), calls=%async_computation | async-start | bytes 6291456 | tf_op jit(solution)/shard_map/all_to_all | solution.py:831
  58.9 4.1 %convert_reduce_fusion.1 = (s32[1536]{0:T(1024)S(1)}, s32[1536]{0:T(1024)S(1)}) fusion(pred[1536]{0:T(1024)(128)(4,1)S(1)} %broadcast_compare_fusion, s32[1536]{0:T(1024)S(1)} %add_select_fusion), kind=kLoop, calls=%fused_computation.1 | loop fusion | flops 18871296 | bytes 19968 | tf_op jit(solution)/shard_map/reduce_sum | solution.py:768
  63.1 0.2 select_reduce_fusion
  63.2 0.1 eq.81
  63.3 0.1 and_convert_fusion.pick_ref
  63.5 36.6 %all-to-all-done = bf16[128,8,1536]{2,1,0:T(8,128)(2,1)S(1)} async-done(((bf16[128,8,1536]{2,1,0:T(8,128)(2,1)}), bf16[128,8,1536]{2,1,0:T(8,128)(2,1)S(1)}, u32[]{:S(2)}, u32[]{:S(2)}) %all-to-all-start) | async-done | bytes 3145760 | tf_op jit(solution)/shard_map/all_to_all | solution.py:831
  100.1 4.4 %place_lines.1 = bf16[2,32,24576]{2,1,0:T(8,128)(2,1)} custom-call(bf16[128,128]{1,0:T(8,128)(2,1)S(1)} %and_convert_fusion.pick_ref, bf16[16,8,8,1536]{3,2,1,0:T(8,128)(2,1)S(1)} %bitcast.13), custom_call_target="tpu_custom_call" | custom-call | flops 1000000000 | bytes 8000000 | tf_op jit(solution)/shard_map/place_lines/pallas_call | solution.py:746
  (23 shorter events, 0.1 us)
Async XLA Ops:
  3.2 17.9 %collective-permute-start = (bf16[2,64,3072]{2,1,0:T(8,128)(2,1)}, bf16[2,64,3072]{2,1,0:T(8,128)(2,1)S(1)}, u32[]{:S(2)}, u32[]{:S(2)}) collective-permute-start(bf16[2,64,3072]{2,1,0:T(8,128)(2,1)} %get-tuple-element.12), channel_id=1, source_target_pairs={{0,8},{8,16},{16,24},{24,32},{32,40},{40,48},{48,56},{56,64},{64,7... | collective-permute-start | bytes 2359304 | tf_op jit(solution)/shard_map/ppermute | solution.py:788
  4.5 16.6 %collective-permute-start.1 = (bf16[2,64,3072]{2,1,0:T(8,128)(2,1)}, bf16[2,64,3072]{2,1,0:T(8,128)(2,1)S(1)}, u32[]{:S(2)}, u32[]{:S(2)}) collective-permute-start(bf16[2,64,3072]{2,1,0:T(8,128)(2,1)} %get-tuple-element.13), channel_id=1, source_target_pairs={{8,0},{16,8},{24,16},{32,24},{40,32},{48,40},{56,48},{64,56},{72,6... | collective-permute-start | bytes 2359304 | tf_op jit(solution)/shard_map/ppermute | solution.py:788
  6.6 1.3 %copy-start.1 = (bf16[2,96,3072]{2,1,0:T(8,128)(2,1)S(1)}, bf16[2,96,3072]{2,1,0:T(8,128)(2,1)}, u32[]{:S(2)}) copy-start(bf16[2,96,3072]{2,1,0:T(8,128)(2,1)} %ref_hbm.3) | copy-start | bytes 3538948
  7.9 1.0 copy-start.8
  8.9 3.4 %copy-start = (bf16[2,96,3072]{2,1,0:T(8,128)(2,1)S(1)}, bf16[2,96,3072]{2,1,0:T(8,128)(2,1)}, u32[]{:S(2)}) copy-start(bf16[2,96,3072]{2,1,0:T(8,128)(2,1)} %sec_hbm.7) | copy-start | bytes 3538948
  8.9 3.4 %copy-start.3 = (s32[1536]{0:T(1024)S(1)}, s32[1536]{0:T(1024)}, u32[]{:S(2)}) copy-start(s32[1536]{0:T(1024)} %param.11) | copy-start | bytes 18436
  8.9 3.4 %copy-start.4 = (s32[1536]{0:T(1024)S(1)}, s32[1536]{0:T(1024)}, u32[]{:S(2)}) copy-start(s32[1536]{0:T(1024)} %param.12) | copy-start | bytes 18436
  8.9 3.4 %copy-start.6 = (bf16[8,24576]{1,0:T(8,128)(2,1)S(1)}, bf16[8,24576]{1,0:T(8,128)(2,1)}, u32[]{:S(2)}) copy-start(bf16[8,24576]{1,0:T(8,128)(2,1)} %taps_hbm.3) | copy-start | bytes 1179652
  8.9 3.4 %copy-start.7 = (s32[24576]{0:T(1024)S(1)}, s32[24576]{0:T(1024)}, u32[]{:S(2)}) copy-start(s32[24576]{0:T(1024)} %param.13) | copy-start | bytes 294916
  12.3 8.8 %copy-start.2 = (bf16[2,96,3072]{2,1,0:T(8,128)(2,1)S(1)}, bf16[2,96,3072]{2,1,0:T(8,128)(2,1)}, u32[]{:S(2)}) copy-start(bf16[2,96,3072]{2,1,0:T(8,128)(2,1)} %ref_hbm.3) | copy-start | bytes 3538948
  20.2 0.9 copy-start.11
  21.1 4.2 %copy-start.10 = (f32[192,3072]{1,0:T(8,128)}, f32[192,3072]{1,0:T(8,128)S(1)}, u32[]{:S(2)}) copy-start(f32[192,3072]{1,0:T(8,128)S(1)} %get-tuple-element.18.sum_hbm) | copy-start | bytes 7077892
  21.1 5.5 %copy-start.5 = (s32[2,1,96]{2,1,0:T(1,128)S(1)}, s32[2,1,96]{2,1,0:T(1,128)}, u32[]{:S(2)}) copy-start(s32[2,1,96]{2,1,0:T(1,128)} %param.10) | copy-start | bytes 2308
  21.1 5.5 %copy-start.9 = (bf16[992,256]{1,0:T(8,128)(2,1)S(1)}, bf16[992,256]{1,0:T(8,128)(2,1)}, u32[]{:S(2)}) copy-start(bf16[992,256]{1,0:T(8,128)(2,1)} %constant.39.clone.table_ref) | copy-start | bytes 1523716
  21.2 13.8 %collective-permute-start.2 = (bf16[2,288,128]{2,1,0:T(8,128)(2,1)S(1)}, bf16[2,288,128]{2,1,0:T(8,128)(2,1)S(1)}, u32[]{:S(2)}, u32[]{:S(2)}) collective-permute-start(bf16[2,288,128]{2,1,0:T(8,128)(2,1)S(1)} %get-tuple-element.15.last_ref), channel_id=1, source_target_pairs={{0,1},{1,2},{2,3},{3,4},{4,5},{5,6},{6,7},{8,9},{9,10},{10,11},{11... | collective-permute-start | bytes 442376 | tf_op jit(solution)/shard_map/ppermute | solution.py:788
  25.3 9.7 %collective-permute-start.3 = (bf16[2,288,128]{2,1,0:T(8,128)(2,1)S(1)}, bf16[2,288,128]{2,1,0:T(8,128)(2,1)S(1)}, u32[]{:S(2)}, u32[]{:S(2)}) collective-permute-start(bf16[2,288,128]{2,1,0:T(8,128)(2,1)S(1)} %get-tuple-element.14.first_ref), channel_id=1, source_target_pairs={{1,0},{2,1},{3,2},{4,3},{5,4},{6,5},{7,6},{9,8},{10,9},{11,10},{12... | collective-permute-start | bytes 442376 | tf_op jit(solution)/shard_map/ppermute | solution.py:788
  42.3 57.7 %all-to-all-start = ((bf16[128,8,1536]{2,1,0:T(8,128)(2,1)}), bf16[128,8,1536]{2,1,0:T(8,128)(2,1)S(1)}, u32[]{:S(2)}, u32[]{:S(2)}) async-start(bf16[128,8,1536]{2,1,0:T(8,128)(2,1)} %bitcast.22), calls=%async_computation | async-start | bytes 6291456 | tf_op jit(solution)/shard_map/all_to_all | solution.py:831

commit v5 on v4

--- a/solution.py
+++ b/solution.py
@@ -35,7 +35,10 @@
 LINE_SPAN = 256
 SCRATCH_BLOCKS = BLOCKS + 3
 GROUP = 8
-RIM_VMEM = 61 * 2**20
+BAND_ROWS = 32
+TABLE = (992, 256)
+RIM_VMEM = 16 * 2**20
+OWN_VMEM = 44 * 2**20
 BOTH = ("az", "rg")
 BF = jnp.bfloat16
 F32 = jnp.float32
@@ -120,32 +123,53 @@
 def sinc_band(start_ref, taps_ref, block):
     start = start_ref[pl.ds(block, 1), :] - block * 128 + MARGIN
     taps = taps_ref[:, pl.ds(pl.multiple_of(block * 128, 128), 128)].astype(F32)
-    offset = iota((256, 128), 0) - start
-    band = jnp.zeros((256, 128), F32)
-    for tap in range(TAP_COUNT):
-        band = jnp.where(offset == tap, taps[tap : tap + 1, :], band)
-    return band.astype(BF)
-
-
-def resample_kernel(
+    chunks = []
+    for first in range(0, 256, BAND_ROWS):
+        offset = iota((BAND_ROWS, 128), 0) - (start - first)
+        band = jnp.zeros((BAND_ROWS, 128), F32)
+        for tap in range(TAP_COUNT):
+            band = jnp.where(offset == tap, taps[tap : tap + 1, :], band)
+        chunks.append(band.astype(BF))
+    return jnp.concatenate(chunks, axis=0)
+
+
+def own_kernel(
     place_ref,
     sec_hbm,
     start_hbm,
     taps_hbm,
     src_ref,
     own_ref,
+    ref_hbm,
+    table_hbm,
     sum_ref,
     pick_ref,
+    spec_ref,
     sec_ref,
     start_ref,
     taps_ref,
     shift_ref,
+    table_ref,
+    rcols_ref,
+    chips_ref,
+    half_ref,
     sems,
 ):
     az = place_ref[0]
     rg = place_ref[1]
+    rows = slice(FIRST_ROW, FIRST_ROW + CHIP_LEN)
     fetch = begin(
-        sems, (sec_hbm, sec_ref), *band_copies(rg, start_hbm, taps_hbm, start_ref, taps_ref)
+        sems,
+        (sec_hbm, sec_ref),
+        *band_copies(rg, start_hbm, taps_hbm, start_ref, taps_ref),
+        (table_hbm, table_ref),
+        *(
+            (
+                ref_hbm.at[part, rows, :],
+                rcols_ref.at[part * CHIP_LEN : (part + 1) * CHIP_LEN, 128 : 128 + COLS],
+            )
+            for part in range(2)
+        ),
     )
 
     line_block = jnp.minimum(jnp.maximum(az * LINES - 8, 0) // 128, ALL_LINES // 128 - 2)
@@ -207,58 +231,77 @@
         return carry
 
     lax.fori_loop(0, (BLOCKS - 2) // 2, window, 0)
-
-
-def resample_inner(place, sec, starts, taps, src, own):
+    reference_spectra(table_ref, spec_ref, rcols_ref, chips_ref, half_ref)
+
+
+def own_side(place, sec, starts, taps, src, own, ref, table):
     return pl.pallas_call(
-        resample_kernel,
+        own_kernel,
         out_shape=(
             jax.ShapeDtypeStruct((2 * LINES, COLS), F32),
             jax.ShapeDtypeStruct((OWNERS * 8, 4 * LINES), BF),
-        ),
-        in_specs=[smem] + [hbm] * 3 + [vmem] * 2,
-        out_specs=(vmem, vmem),
+            jax.ShapeDtypeStruct((PAIRS * CHIP_LEN, 256), F32),
+        ),
+        in_specs=[smem] + [hbm] * 3 + [vmem] * 2 + [hbm] * 2,
+        out_specs=(vmem,) * 3,
         scratch_shapes=[
             pltpu.VMEM((2 * LINES, COLS), BF),
             pltpu.VMEM((BLOCKS, 128), jnp.int32),
             pltpu.VMEM((TAP_COUNT, COLS), BF),
             pltpu.VMEM((2 * LINES, COLS), BF),
-            pltpu.SemaphoreType.DMA((3,)),
+            pltpu.VMEM(TABLE, BF),
+            pltpu.VMEM((2 * CHIP_LEN, SCRATCH_BLOCKS * 128), BF),
+            pltpu.VMEM((2 * CHIP_LEN, CHIPS * 64), BF),
+            pltpu.VMEM((2 * CHIP_LEN, CHIPS * 64), BF),
+            pltpu.SemaphoreType.DMA((6,)),
         ],
-        compiler_params=pltpu.CompilerParams(vmem_limit_bytes=16 * 2**20),
+        compiler_params=pltpu.CompilerParams(vmem_limit_bytes=OWN_VMEM),
         cost_estimate=pl.CostEstimate(
             flops=2 * 10**9, bytes_accessed=6 * 10**6, transcendentals=0
         ),
-        name="resample_inner",
-    )(place, sec, starts, taps, src, own)
-
-
-def rims_kernel(sec_hbm, head_ref, tail_ref, sems):
-    for copy in begin(
-        sems,
-        (sec_hbm.at[:, 0:MARGIN, :], head_ref),
-        (sec_hbm.at[:, LINES - MARGIN : LINES, :], tail_ref),
-    ):
+        name="own_side",
+    )(place, sec, starts, taps, src, own, ref, table)
+
+
+def rims_kernel(place_ref, sec_hbm, mate_ref, other_ref, sems):
+    odd = place_ref[0] & 1
+    pairs = []
+    for to_ref, at in ((other_ref, odd), (mate_ref, 1 - odd)):
+        first = at * (LINES - MARGIN)
+        for part in range(2):
+            for row in range(0, MARGIN, 32):
+                pairs.append(
+                    (
+                        sec_hbm.at[part, pl.ds(pl.multiple_of(first + row, 16), 32), :],
+                        to_ref.at[part, row : row + 32, :],
+                    )
+                )
+    for copy in begin(sems, *pairs):
         copy.wait()
 
 
-def rims(sec):
+def rims(place, sec):
     rows = jax.ShapeDtypeStruct((2, MARGIN, COLS), BF)
     return pl.pallas_call(
         rims_kernel,
         out_shape=(rows, rows),
-        in_specs=[hbm],
-        out_specs=(vmem, vmem),
-        scratch_shapes=[pltpu.SemaphoreType.DMA((2,))],
+        in_specs=[smem, hbm],
+        out_specs=(hbm, hbm),
+        scratch_shapes=[pltpu.SemaphoreType.DMA((8,))],
         compiler_params=pltpu.CompilerParams(vmem_limit_bytes=RIM_VMEM),
         name="rims",
-    )(sec)
-
-
-def edges_kernel(ref_hbm, sec_hbm, up_ref, down_ref, first_ref, last_ref, sems):
+    )(place, sec)
+
+
+def edges_kernel(place_ref, ref_hbm, sec_hbm, near_ref, far_ref, mate_ref, other_ref, sems):
+    odd_rows = place_ref[0] & 1
+    odd = place_ref[1] & 1
     own = CHIP_LEN + MARGIN
     pairs = []
-    for to_ref, cols in ((first_ref, slice(0, 128)), (last_ref, slice(COLS - 128, COLS))):
+    sides = []
+    for to_ref, at in ((mate_ref, 1 - odd), (other_ref, odd)):
+        cols = pl.ds(pl.multiple_of(at * (COLS - 128), 128), 128)
+        sides.append((to_ref, cols))
         pairs += [
             (
                 ref_hbm.at[:, FIRST_ROW : FIRST_ROW + CHIP_LEN, cols],
@@ -267,25 +310,26 @@
             (sec_hbm.at[:, :, cols], to_ref.at[:, own : own + LINES, :]),
         ]
     fetch = begin(sems, *pairs)
-    for to_ref, cols in ((first_ref, slice(0, 128)), (last_ref, slice(COLS - 128, COLS))):
-        for part in range(2):
-            to_ref[part, CHIP_LEN:own, :] = up_ref[part, :, cols]
-            to_ref[part, own + LINES :, :] = down_ref[part, :, cols]
+    for to_ref, cols in sides:
+        for rows_ref, low in ((near_ref, 1 - odd_rows), (far_ref, odd_rows)):
+            at = pl.ds(pl.multiple_of(CHIP_LEN + low * (MARGIN + LINES), 16), MARGIN)
+            for part in range(2):
+                to_ref[part, at, :] = rows_ref[part, :, cols]
     for copy in fetch:
         copy.wait()
 
 
-def rg_edges(ref, sec, up, down):
+def rg_edges(place, ref, sec, near, far):
     cols = jax.ShapeDtypeStruct((2, CHIP_LEN + ROWS, 128), BF)
     return pl.pallas_call(
         edges_kernel,
         out_shape=(cols, cols),
-        in_specs=[hbm, hbm, vmem, vmem],
+        in_specs=[smem, hbm, hbm, vmem, vmem],
         out_specs=(vmem, vmem),
         scratch_shapes=[pltpu.SemaphoreType.DMA((4,))],
         compiler_params=pltpu.CompilerParams(vmem_limit_bytes=8 * 2**20),
         name="rg_edges",
-    )(ref, sec, up, down)
+    )(place, ref, sec, near, far)
 
 
 def side_by_side(half, pairs):
@@ -319,23 +363,10 @@
     return pltpu.roll(jnp.where(lane >= 48, here, far), 80, 1).astype(BF)
 
 
-def reference_kernel(ref_hbm, table_ref, spec_ref, rcols_ref, chips_ref, half_ref, sems):
-    rows = slice(FIRST_ROW, FIRST_ROW + CHIP_LEN)
-    fetch = begin(
-        sems,
-        *(
-            (
-                ref_hbm.at[part, rows, :],
-                rcols_ref.at[part * CHIP_LEN : (part + 1) * CHIP_LEN, 128 : 128 + COLS],
-            )
-            for part in range(2)
-        ),
-    )
+def reference_spectra(table_ref, spec_ref, rcols_ref, chips_ref, half_ref):
     none = jnp.zeros((2 * CHIP_LEN, 128), BF)
     rcols_ref[:, 0:128] = none
     rcols_ref[:, 128 + COLS : 256 + COLS] = none
-    for copy in fetch:
-        copy.wait()
 
     def cut(step, carry):
         def block(at):
@@ -357,26 +388,6 @@
             table_ref[0:256, :],
             preferred_element_type=F32,
         )
-
-
-def reference_side(ref, table):
-    return pl.pallas_call(
-        reference_kernel,
-        out_shape=jax.ShapeDtypeStruct((PAIRS * CHIP_LEN, 256), F32),
-        in_specs=[hbm, vmem],
-        out_specs=vmem,
-        scratch_shapes=[
-            pltpu.VMEM((2 * CHIP_LEN, SCRATCH_BLOCKS * 128), BF),
-            pltpu.VMEM((2 * CHIP_LEN, CHIPS * 64), BF),
-            pltpu.VMEM((2 * CHIP_LEN, CHIPS * 64), BF),
-            pltpu.SemaphoreType.DMA((2,)),
-        ],
-        compiler_params=pltpu.CompilerParams(vmem_limit_bytes=12 * 2**20),
-        cost_estimate=pl.CostEstimate(
-            flops=2 * 10**9, bytes_accessed=6 * 10**6, transcendentals=0
-        ),
-        name="reference_side",
-    )(ref, table)
 
 
 def cut_pair(off_ref, scols_ref, pair, first_block):
@@ -428,21 +439,24 @@
 
 
 def inner_kernel(
+    place_ref,
     off_ref,
     sec_hbm,
-    up_ref,
-    down_ref,
-    table_ref,
+    near_ref,
+    far_ref,
+    table_hbm,
     spec_ref,
     tot_ref,
     mom_ref,
     sec_ref,
+    table_ref,
     scols_ref,
     chips_ref,
     half_ref,
     sems,
 ):
-    fetch = begin(sems, (sec_hbm, sec_ref))
+    fetch = begin(sems, (sec_hbm, sec_ref), (table_hbm, table_ref))
+    odd = place_ref[0] & 1
     none = jnp.zeros((2 * ROWS, 128), F32)
     for block in (0, SCRATCH_BLOCKS - 2, SCRATCH_BLOCKS - 1):
         scols_ref[block] = none
@@ -452,10 +466,11 @@
             block = step * 2 + member
             at = pl.ds(pl.multiple_of(block * 128, 128), 128)
             for part in range(2):
-                base = part * ROWS
-                low = base + MARGIN + LINES
-                scols_ref[block + 1, base : base + MARGIN, :] = up_ref[part, :, at].astype(F32)
-                scols_ref[block + 1, low : base + ROWS, :] = down_ref[part, :, at].astype(F32)
+                for rows_ref, low in ((near_ref, 1 - odd), (far_ref, odd)):
+                    first = pl.multiple_of(part * ROWS + low * (MARGIN + LINES), 8)
+                    scols_ref[block + 1, pl.ds(first, MARGIN), :] = rows_ref[part, :, at].astype(
+                        F32
+                    )
         return carry
 
     lax.fori_loop(0, BLOCKS // 2, widen_rims, 0)
@@ -502,40 +517,41 @@
     lax.fori_loop(0, PAIRS // GROUP, correlate, 0)
 
 
-def inner_pairs(off, sec, up, down, table, spectra):
+def inner_pairs(place, off, sec, near, far, table, spectra):
     sums = jax.ShapeDtypeStruct((PAIRS, 128), F32)
     return pl.pallas_call(
         inner_kernel,
         out_shape=(sums, sums),
-        in_specs=[smem, hbm] + [vmem] * 4,
+        in_specs=[smem, smem, hbm, vmem, vmem, hbm, vmem],
         out_specs=(vmem, vmem),
         scratch_shapes=[
             pltpu.VMEM((2, LINES, COLS), BF),
+            pltpu.VMEM(TABLE, BF),
             pltpu.VMEM((SCRATCH_BLOCKS, 2 * ROWS, 128), F32),
             pltpu.VMEM((2 * CHIP_LEN, CHIPS * 64), BF),
             pltpu.VMEM((2 * CHIP_LEN, CHIPS * 64), BF),
-            pltpu.SemaphoreType.DMA((1,)),
+            pltpu.SemaphoreType.DMA((2,)),
         ],
         compiler_params=pltpu.CompilerParams(vmem_limit_bytes=24 * 2**20),
         cost_estimate=pl.CostEstimate(
             flops=6 * 10**9, bytes_accessed=20 * 10**6, transcendentals=0
         ),
         name="inner_pairs",
-    )(off, sec, up, down, table, spectra)
+    )(place, off, sec, near, far, table, spectra)
 
 
 def finish_kernel(
     place_ref,
     off_ref,
     offv_ref,
-    first_ref,
-    last_ref,
+    sent_mate_ref,
+    sent_other_ref,
+    got_mate_ref,
+    got_other_ref,
     sec_hbm,
     start_hbm,
     taps_hbm,
-    left_ref,
-    right_ref,
-    table_ref,
+    table_hbm,
     tot_ref,
     mom_ref,
     sum_hbm,
@@ -547,13 +563,18 @@
     near_ref,
     start_ref,
     taps_ref,
+    table_ref,
+    edge_ref,
+    padded_ref,
     scols_ref,
     lines_ref,
     packed_ref,
+    table_sem,
     sems,
     out_sems,
 ):
     rg = place_ref[1]
+    fetch_table = begin(table_sem, (table_hbm, table_ref))
     fetch = begin(
         sems,
         *band_copies(rg, start_hbm, taps_hbm, start_ref, taps_ref),
@@ -562,6 +583,20 @@
         (sum_hbm, sum_ref),
         (pick_hbm, pick_ref),
     )
+    left_ref, first_ref, last_ref, right_ref = (edge_ref.at[n] for n in range(4))
+
+    def ordered(refs):
+        for to_ref, from_ref in zip((left_ref, first_ref, last_ref, right_ref), refs):
+            to_ref[...] = from_ref[...]
+
+    @pl.when((rg & 1) == 0)
+    def _():
+        ordered((got_other_ref, sent_other_ref, sent_mate_ref, got_mate_ref))
+
+    @pl.when((rg & 1) == 1)
+    def _():
+        ordered((got_mate_ref, sent_mate_ref, sent_other_ref, got_other_ref))
+
     own_rows = slice(CHIP_LEN + MARGIN, CHIP_LEN + MARGIN + LINES)
     sides = (
         (left_ref, first_ref, 0),
@@ -590,6 +625,8 @@
         jnp.concatenate(cut_pair(off_ref, scols_ref, 0, 0), axis=0),
         jnp.concatenate(cut_pair(off_ref, scols_ref, PAIRS - 1, BLOCKS - 3), axis=0),
     ]
+    for copy in fetch_table:
+        copy.wait()
     half = jnp.dot(
         table_ref[864:992, 0:128],
         jnp.concatenate(columns, axis=1),
@@ -633,7 +670,9 @@
         values = jnp.where(even, found[0][which], found[1][which])
         return jnp.sum(jnp.where(own_chip, values, 0.0), axis=0, keepdims=True)
 
-    offsets = offv_ref[...].astype(F32)
+    padded_ref[...] = jnp.zeros((8, 128), jnp.int32)
+    padded_ref[0:2, 0:CHIPS] = offv_ref[...]
+    offsets = padded_ref[...].astype(F32)
     est_az = offsets[0:1, :] + spread(0)
     est_rg = offsets[1:2, :] + spread(1)
     est_ref[0:1, :] = est_az
@@ -698,14 +737,14 @@
         copy.wait()
 
 
-def finish(place, off, offv, first, last, *arrays):
+def finish(place, off, *arrays):
     return pl.pallas_call(
         finish_kernel,
         out_shape=(
             jax.ShapeDtypeStruct((2, 128), F32),
             jax.ShapeDtypeStruct((OWNERS * 8, WIDTH), BF),
         ),
-        in_specs=[smem] * 2 + [vmem] * 3 + [hbm] * 3 + [vmem] * 5 + [hbm] * 2,
+        in_specs=[smem] * 2 + [vmem] * 5 + [hbm] * 4 + [vmem] * 2 + [hbm] * 2,
         out_specs=(vmem, hbm),
         scratch_shapes=[
             pltpu.VMEM((2 * LINES, COLS), F32),
@@ -713,9 +752,13 @@
             pltpu.VMEM((2, 2, LINES, 128), BF),
             pltpu.VMEM((BLOCKS, 128), jnp.int32),
             pltpu.VMEM((TAP_COUNT, COLS), BF),
+            pltpu.VMEM(TABLE, BF),
+            pltpu.VMEM((4, 2, CHIP_LEN + ROWS, 128), BF),
+            pltpu.VMEM((8, 128), jnp.int32),
             pltpu.VMEM((6, 2 * ROWS, 128), F32),
             pltpu.VMEM((4 * LINES, WIDTH), BF),
             pltpu.VMEM((OWNERS * 8, WIDTH), BF),
+            pltpu.SemaphoreType.DMA((1,)),
             pltpu.SemaphoreType.DMA((6,)),
             pltpu.SemaphoreType.DMA((WIDTH // 256,)),
         ],
@@ -724,7 +767,7 @@
             flops=2 * 10**9, bytes_accessed=10 * 10**6, transcendentals=0
         ),
         name="finish",
-    )(place, off, offv, first, last, *arrays)
+    )(place, off, off, *arrays)
 
 
 def place_kernel(pick_ref, arr_ref, out_ref):
@@ -781,11 +824,14 @@
     return pick.astype(BF)
 
 
-def neighbours(axis, first, last):
+def exchanged(axis, mate, other):
     count = lax.axis_size(axis)
-    up = [(i, i + 1) for i in range(count - 1)]
-    down = [(i + 1, i) for i in range(count - 1)]
-    return lax.ppermute(last, axis, up), lax.ppermute(first, axis, down)
+
+    def swap(block, first):
+        pairs = [(i, i + 1) for i in range(first, count - 1, 2)]
+        return lax.ppermute(block, axis, pairs + [(j, i) for i, j in pairs])
+
+    return swap(mate, 0), swap(other, 1)
 
 
 def per_device(
@@ -796,32 +842,29 @@
     place = jnp.stack([az, rg]).astype(jnp.int32)
     starts = band_start.reshape(PIECES * BLOCKS, 128)
     table = kernel_table()
-    up, down = neighbours("az", *rims(secondary_slc))
-    summed, pick_sent = resample_inner(
+    near, far = exchanged("az", *rims(place, secondary_slc))
+    summed, pick_sent, spectra = own_side(
         place,
         secondary_slc.reshape(2 * LINES, COLS),
         starts,
         band_taps,
         src_row.reshape(ALL_LINES // 128, 128),
         line_owner.reshape(ALL_LINES // 128, 128),
-    )
-    spectra = reference_side(reference_slc, table)
-    first, last = rg_edges(reference_slc, secondary_slc, up, down)
-    left, right = neighbours("rg", first, last)
+        reference_slc,
+        table,
+    )
+    sent = rg_edges(place, reference_slc, secondary_slc, near, far)
+    got = exchanged("rg", *sent)
     off = chip_offsets[:, 0, :]
-    offv = jnp.pad(off, ((0, 0), (0, 128 - CHIPS)))
-    total, moment = inner_pairs(off, secondary_slc, up, down, table, spectra)
+    total, moment = inner_pairs(place, off, secondary_slc, near, far, table, spectra)
     est, packed = finish(
         place,
         off,
-        offv,
-        first,
-        last,
+        *sent,
+        *got,
         secondary_slc,
         starts,
         band_taps,
-        left,
-        right,
         table,
         total,
         moment,

time: 105 us -> 105 us (level)
  starting transfers between devices: 24.6 us -> 19.1 us
  local copies, waits for them, and re-layouts: 4.01 us -> 8.26 us
    unnamed x24 -> x32, local copies, waits for them, and re-layouts: 3.24 us -> 8.17 us
    ppermute x4, starting transfers between devices: 7.99 us -> 3.11 us  [swap(): return lax.ppermute(block, axis, pairs + [(j, i) for i, j in pairs])]
    pallas_call x5 -> x4, Pallas kernels: 22.2 us -> 23.6 us  [the longest x1 11.5 us: own_side(): pl.pallas_call(own_kernel, out_shape=(jax.ShapeDtypeStruct((2 * LINES, CO...]
  transfers between devices with their start and end apart: 5 -> 5, of which waited for: 1 -> 1; matrix products, arithmetic and copies ran while one was open for 5% -> 4% of each run, Pallas kernels for 19% -> 19%
where the time goes in v5:
time: 105 us; the launch traced here: 104 us
  waiting for transfers between devices  36.6 us (35%)
  Pallas kernels  34.8 us (33%)
  starting transfers between devices  19.1 us (18%)
  local copies, waits for them, and re-layouts  8.26 us (8%)
  other arithmetic  4.49 us (4%)
    all_to_all x1, waiting for transfers between devices, per_device(): arrived = lax.all_to_all(packed, BOTH, 0, 0, tiled=True)  36.6 us
    all_to_all x1, starting transfers between devices, per_device(): arrived = lax.all_to_all(packed, BOTH, 0, 0, tiled=True)  16 us
    pallas_call x1, Pallas kernels, own_side(): pl.pallas_call(own_kernel, out_shape=(jax.ShapeDtypeStruct((2 * LINES, CO...  11.5 us
    pallas_call x1, Pallas kernels, inner_pairs(): pl.pallas_call(inner_kernel, out_shape=(sums, sums), in_specs=[smem, smem...  8.78 us
    unnamed x32, local copies, waits for them, and re-layouts  8.17 us
    pallas_call x1, Pallas kernels, finish(): pl.pallas_call(finish_kernel, out_shape=(jax.ShapeDtypeStruct((2, 128), F...  6.8 us
    pallas_call x1, Pallas kernels, place_lines(): pl.pallas_call(place_kernel, grid=(PIECES,), out_shape=jax.ShapeDtypeStru...  4.38 us
    reduce_sum x1, other arithmetic, owner_table(): rank = jnp.sum(before.astype(jnp.int32), axis=1)  4.09 us
  transfers between devices with their start and end apart: 5, of which 1 were waited for; matrix products, arithmetic and copies ran while one was open for 4% of the time, Pallas kernels for 19%

profile of v5, /device:TPU:0, one launch (start us, length us, event | category | flops | bytes accessed | tf_op | source)
XLA Modules:
  0.0 104.1 jit_solution(3006196301630710382)
XLA Ops:
  0.6 0.1 pad_add_fusion.place_ref
  0.7 1.3 %copy-done = bf16[2,96,3072]{2,1,0:T(8,128)(2,1)S(1)} copy-done((bf16[2,96,3072]{2,1,0:T(8,128)(2,1)S(1)}, bf16[2,96,3072]{2,1,0:T(8,128)(2,1)}, u32[]{:S(2)}) %copy-start) | copy-done | bytes 1179672
  2.0 2.7 %rims.1 = (bf16[2,64,3072]{2,1,0:T(8,128)(2,1)S(1)}, bf16[2,64,3072]{2,1,0:T(8,128)(2,1)S(1)}) custom-call(s32[2]{0:T(128)S(1)} %pad_add_fusion.place_ref, bf16[2,96,3072]{2,1,0:T(8,128)(2,1)S(1)} %copy-done), custom_call_target="tpu_custom_call" | custom-call | tf_op jit(solution)/shard_map/rims/pallas_call | solution.py:285
  4.6 0.1 collective-permute-start
  4.7 0.7 collective-permute-start.1
  5.5 0.0 copy-start.1
  5.5 1.3 %copy-done.1 = bf16[2,96,3072]{2,1,0:T(8,128)(2,1)S(1)} copy-done((bf16[2,96,3072]{2,1,0:T(8,128)(2,1)S(1)}, bf16[2,96,3072]{2,1,0:T(8,128)(2,1)}, u32[]{:S(2)}) %copy-start.1) | copy-done | bytes 1179672
  6.7 1.3 %copy-done.2 = bf16[2,96,3072]{2,1,0:T(8,128)(2,1)S(1)} copy-done((bf16[2,96,3072]{2,1,0:T(8,128)(2,1)S(1)}, bf16[2,96,3072]{2,1,0:T(8,128)(2,1)}, u32[]{:S(2)}) %copy-start.2) | copy-done | bytes 1179672
  8.0 0.7 copy-done.3
  8.7 0.7 copy-done.5
  9.4 1.0 copy-done.7
  10.4 0.9 copy-done.9
  11.3 1.0 copy-done.12
  12.3 11.5 %own_side.1 = (f32[192,3072]{1,0:T(8,128)S(1)}, bf16[1024,384]{1,0:T(8,128)(2,1)S(1)}, f32[3072,256]{1,0:T(8,128)S(1)}) custom-call(s32[2]{0:T(128)S(1)} %pad_add_fusion.place_ref, bf16[192,3072]{1,0:T(8,128)(2,1)S(1)} %bitcast.14, s32[192,128]{1,0:T(8,128)S(1)} %bitcast.17, bf16[8,24576]{1,0:T(8,128)(2,1)S(1)} %copy-done.7, s32[12,128]{1,0:T(8,128)S(1)} %bitcast.15, ...), custom_call_target="tpu_custom_call" | custom-call | flops 2000000000 | bytes 6000000 | tf_op jit(solution)/shard_map/own_side/pallas_call | solution.py:238
  23.8 0.0 copy-start.11
  23.9 0.7 rg_edges.1
  24.5 1.7 %collective-permute-start.2 = (bf16[2,288,128]{2,1,0:T(8,128)(2,1)S(1)}, bf16[2,288,128]{2,1,0:T(8,128)(2,1)S(1)}, u32[]{:S(2)}, u32[]{:S(2)}) collective-permute-start(bf16[2,288,128]{2,1,0:T(8,128)(2,1)S(1)} %get-tuple-element.15.sent_mate_ref), channel_id=1, source_target_pairs={{0,1},{2,3},{4,5},{6,7},{1,0},{3,2},{5,4},{7,6},{8,9},{10,11},{12,... | collective-permute-start | bytes 442376 | tf_op jit(solution)/shard_map/ppermute | solution.py:832
  26.2 0.7 collective-permute-start.3
  26.9 0.0 copy-start.8
  26.9 0.0 copy-start.10
  26.9 0.0 copy-start.13
  26.9 8.8 %inner_pairs.1 = (f32[48,128]{1,0:T(8,128)S(1)}, f32[48,128]{1,0:T(8,128)S(1)}) custom-call(s32[2]{0:T(128)S(1)} %pad_add_fusion.place_ref, s32[2,96]{1,0:T(2,128)S(1)} %bitcast.19, bf16[2,96,3072]{2,1,0:T(8,128)(2,1)S(1)} %copy-done.1, bf16[2,64,3072]{2,1,0:T(8,128)(2,1)S(1)} %collective-permute-done.near_ref, ...), custom_call_target="tpu_custom_call" | custom-call | flops 6000000000 | bytes 20000000 | tf_op jit(solution)/shard_map/inner_pairs/pallas_call | solution.py:522
  35.8 6.8 %finish.1 = (f32[2,128]{1,0:T(2,128)}, bf16[1024,1536]{1,0:T(8,128)(2,1)}) custom-call(s32[2]{0:T(128)S(1)} %pad_add_fusion.place_ref, s32[2,96]{1,0:T(2,128)S(1)} %bitcast.20, s32[2,96]{1,0:T(2,128)S(1)} %bitcast.21, bf16[2,288,128]{2,1,0:T(8,128)(2,1)S(1)} %get-tuple-element.15.sent_mate_ref, bf16[2,288,128]{2,1,0:T(8,128)(2,1)S(1)} %get-tuple-element.16.sent_other_ref, ...), custom_call_target="tpu_custom_call" | custom-call | flops 2000000000 | bytes 10000000 | tf_op jit(solution)/shard_map/finish/pallas_call | solution.py:741
  42.6 0.0 copy-start.6
  42.6 0.0 copy-start.4
  42.6 16.0 %all-to-all-start = ((bf16[128,8,1536]{2,1,0:T(8,128)(2,1)}), bf16[128,8,1536]{2,1,0:T(8,128)(2,1)S(1)}, u32[]{:S(2)}, u32[]{:S(2)}) async-start(bf16[128,8,1536]{2,1,0:T(8,128)(2,1)} %bitcast.22), calls=%async_computation | async-start | bytes 6291456 | tf_op jit(solution)/shard_map/all_to_all | solution.py:874
  58.6 4.1 %convert_reduce_fusion.1 = (s32[1536]{0:T(1024)S(1)}, s32[1536]{0:T(1024)S(1)}) fusion(pred[1536]{0:T(1024)(128)(4,1)S(1)} %broadcast_compare_fusion, s32[1536]{0:T(1024)S(1)} %add_select_fusion), kind=kLoop, calls=%fused_computation.1 | loop fusion | flops 18871296 | bytes 19968 | tf_op jit(solution)/shard_map/reduce_sum | solution.py:811
  62.8 0.2 select_reduce_fusion
  62.9 0.1 eq.81
  63.0 0.1 and_convert_fusion.pick_ref
  63.2 36.6 %all-to-all-done = bf16[128,8,1536]{2,1,0:T(8,128)(2,1)S(1)} async-done(((bf16[128,8,1536]{2,1,0:T(8,128)(2,1)}), bf16[128,8,1536]{2,1,0:T(8,128)(2,1)S(1)}, u32[]{:S(2)}, u32[]{:S(2)}) %all-to-all-start) | async-done | bytes 3145760 | tf_op jit(solution)/shard_map/all_to_all | solution.py:874
  99.8 4.4 %place_lines.1 = bf16[2,32,24576]{2,1,0:T(8,128)(2,1)} custom-call(bf16[128,128]{1,0:T(8,128)(2,1)S(1)} %and_convert_fusion.pick_ref, bf16[16,8,8,1536]{3,2,1,0:T(8,128)(2,1)S(1)} %bitcast.13), custom_call_target="tpu_custom_call" | custom-call | flops 1000000000 | bytes 8000000 | tf_op jit(solution)/shard_map/place_lines/pallas_call | solution.py:789
  (29 shorter events, 0.1 us)
Async XLA Ops:
  0.7 1.3 %copy-start = (bf16[2,96,3072]{2,1,0:T(8,128)(2,1)S(1)}, bf16[2,96,3072]{2,1,0:T(8,128)(2,1)}, u32[]{:S(2)}) copy-start(bf16[2,96,3072]{2,1,0:T(8,128)(2,1)} %sec_hbm.7) | copy-start | bytes 3538948
  4.6 19.2 %collective-permute-start = (bf16[2,64,3072]{2,1,0:T(8,128)(2,1)S(1)}, bf16[2,64,3072]{2,1,0:T(8,128)(2,1)S(1)}, u32[]{:S(2)}, u32[]{:S(2)}) collective-permute-start(bf16[2,64,3072]{2,1,0:T(8,128)(2,1)S(1)} %get-tuple-element.13), channel_id=1, source_target_pairs={{0,8},{16,24},{32,40},{48,56},{64,72},{80,88},{96,104},{112,120},{... | collective-permute-start | bytes 2359304 | tf_op jit(solution)/shard_map/ppermute | solution.py:832
  4.7 19.1 %collective-permute-start.1 = (bf16[2,64,3072]{2,1,0:T(8,128)(2,1)S(1)}, bf16[2,64,3072]{2,1,0:T(8,128)(2,1)S(1)}, u32[]{:S(2)}, u32[]{:S(2)}) collective-permute-start(bf16[2,64,3072]{2,1,0:T(8,128)(2,1)S(1)} %get-tuple-element.14), channel_id=1, source_target_pairs={{8,16},{24,32},{40,48},{56,64},{72,80},{88,96},{104,112},{16,8},{3... | collective-permute-start | bytes 2359304 | tf_op jit(solution)/shard_map/ppermute | solution.py:832
  5.5 1.3 %copy-start.1 = (bf16[2,96,3072]{2,1,0:T(8,128)(2,1)S(1)}, bf16[2,96,3072]{2,1,0:T(8,128)(2,1)}, u32[]{:S(2)}) copy-start(bf16[2,96,3072]{2,1,0:T(8,128)(2,1)} %sec_hbm.7) | copy-start | bytes 3538948
  6.7 1.3 %copy-start.2 = (bf16[2,96,3072]{2,1,0:T(8,128)(2,1)S(1)}, bf16[2,96,3072]{2,1,0:T(8,128)(2,1)}, u32[]{:S(2)}) copy-start(bf16[2,96,3072]{2,1,0:T(8,128)(2,1)} %ref_hbm.3) | copy-start | bytes 3538948
  8.0 0.7 copy-start.3
  8.7 0.7 copy-start.5
  9.4 1.0 copy-start.7
  10.4 0.9 copy-start.9
  11.3 1.0 copy-start.12
  23.8 11.9 %copy-start.14 = (f32[192,3072]{1,0:T(8,128)}, f32[192,3072]{1,0:T(8,128)S(1)}, u32[]{:S(2)}) copy-start(f32[192,3072]{1,0:T(8,128)S(1)} %get-tuple-element.20.sum_hbm) | copy-start | bytes 7077892
  23.8 11.9 %copy-start.15 = (bf16[1024,384]{1,0:T(8,128)(2,1)}, bf16[1024,384]{1,0:T(8,128)(2,1)S(1)}, u32[]{:S(2)}) copy-start(bf16[1024,384]{1,0:T(8,128)(2,1)S(1)} %get-tuple-element.21.pick_hbm) | copy-start | bytes 2359300
  23.8 3.0 %copy-start.11 = (s32[2,1,96]{2,1,0:T(1,128)S(1)}, s32[2,1,96]{2,1,0:T(1,128)}, u32[]{:S(2)}) copy-start(s32[2,1,96]{2,1,0:T(1,128)} %param.10) | copy-start | bytes 2308
  24.5 11.2 %collective-permute-start.2 = (bf16[2,288,128]{2,1,0:T(8,128)(2,1)S(1)}, bf16[2,288,128]{2,1,0:T(8,128)(2,1)S(1)}, u32[]{:S(2)}, u32[]{:S(2)}) collective-permute-start(bf16[2,288,128]{2,1,0:T(8,128)(2,1)S(1)} %get-tuple-element.15.sent_mate_ref), channel_id=1, source_target_pairs={{0,1},{2,3},{4,5},{6,7},{1,0},{3,2},{5,4},{7,6},{8,9},{10,11},{12,... | collective-permute-start | bytes 442376 | tf_op jit(solution)/shard_map/ppermute | solution.py:832
  26.2 9.5 %collective-permute-start.3 = (bf16[2,288,128]{2,1,0:T(8,128)(2,1)S(1)}, bf16[2,288,128]{2,1,0:T(8,128)(2,1)S(1)}, u32[]{:S(2)}, u32[]{:S(2)}) collective-permute-start(bf16[2,288,128]{2,1,0:T(8,128)(2,1)S(1)} %get-tuple-element.16.sent_other_ref), channel_id=1, source_target_pairs={{1,2},{3,4},{5,6},{2,1},{4,3},{6,5},{9,10},{11,12},{13,14},{10,9},... | collective-permute-start | bytes 442376 | tf_op jit(solution)/shard_map/ppermute | solution.py:832
  26.9 8.9 %copy-start.8 = (bf16[8,24576]{1,0:T(8,128)(2,1)S(1)}, bf16[8,24576]{1,0:T(8,128)(2,1)}, u32[]{:S(2)}) copy-start(bf16[8,24576]{1,0:T(8,128)(2,1)} %taps_hbm.3) | copy-start | bytes 1179652
  26.9 8.9 %copy-start.10 = (s32[24576]{0:T(1024)S(1)}, s32[24576]{0:T(1024)}, u32[]{:S(2)}) copy-start(s32[24576]{0:T(1024)} %param.13) | copy-start | bytes 294916
  26.9 8.9 %copy-start.13 = (bf16[992,256]{1,0:T(8,128)(2,1)S(1)}, bf16[992,256]{1,0:T(8,128)(2,1)}, u32[]{:S(2)}) copy-start(bf16[992,256]{1,0:T(8,128)(2,1)} %constant.39.clone.table_hbm) | copy-start | bytes 1523716
  42.6 16.0 %copy-start.6 = (s32[1536]{0:T(1024)S(1)}, s32[1536]{0:T(1024)}, u32[]{:S(2)}) copy-start(s32[1536]{0:T(1024)} %param.12) | copy-start | bytes 18436
  42.6 16.0 %copy-start.4 = (s32[1536]{0:T(1024)S(1)}, s32[1536]{0:T(1024)}, u32[]{:S(2)}) copy-start(s32[1536]{0:T(1024)} %param.11) | copy-start | bytes 18436
  42.6 57.2 %all-to-all-start = ((bf16[128,8,1536]{2,1,0:T(8,128)(2,1)}), bf16[128,8,1536]{2,1,0:T(8,128)(2,1)S(1)}, u32[]{:S(2)}, u32[]{:S(2)}) async-start(bf16[128,8,1536]{2,1,0:T(8,128)(2,1)} %bitcast.22), calls=%async_computation | async-start | bytes 6291456 | tf_op jit(solution)/shard_map/all_to_all | solution.py:874

commit v6 on v5

--- a/solution.py
+++ b/solution.py
@@ -34,8 +34,9 @@
 WIDTH = HALF * 128
 LINE_SPAN = 256
 SCRATCH_BLOCKS = BLOCKS + 3
-GROUP = 8
-BAND_ROWS = 32
+GROUP = 24
+BAND_ROWS = 64
+PLACED = 4
 TABLE = (992, 256)
 RIM_VMEM = 16 * 2**20
 OWN_VMEM = 44 * 2**20
@@ -134,7 +135,6 @@
 
 
 def own_kernel(
-    place_ref,
     sec_hbm,
     start_hbm,
     taps_hbm,
@@ -155,8 +155,8 @@
     half_ref,
     sems,
 ):
-    az = place_ref[0]
-    rg = place_ref[1]
+    az = lax.axis_index("az")
+    rg = lax.axis_index("rg")
     rows = slice(FIRST_ROW, FIRST_ROW + CHIP_LEN)
     fetch = begin(
         sems,
@@ -209,19 +209,15 @@
     for copy in fetch:
         copy.wait()
 
-    def move(step, carry):
-        at = pl.multiple_of(step * 128, 128)
-        shift_ref[:, pl.ds(at, 128)] = half_turned(
-            sec_ref[:, pl.ds(pl.multiple_of(at - 128, 128), 128)], sec_ref[:, pl.ds(at, 128)]
+    for at in range(128, COLS, 128):
+        shift_ref[:, at : at + 128] = half_turned(
+            sec_ref[:, at - 128 : at], sec_ref[:, at : at + 128]
         )
-        return carry
-
-    lax.fori_loop(1, BLOCKS, move, 0)
     start_ref[...] = start_ref[...] - rg * COLS
 
     def window(step, carry):
-        for member in range(2):
-            block = step * 2 + member + 1
+        for member in range(22):
+            block = step * 22 + member + 1
             at = pl.multiple_of(block * 128, 128)
             sum_ref[:, pl.ds(at, 128)] = jnp.dot(
                 shift_ref[:, pl.ds(at, 256)],
@@ -230,11 +226,11 @@
             )
         return carry
 
-    lax.fori_loop(0, (BLOCKS - 2) // 2, window, 0)
+    lax.fori_loop(0, (BLOCKS - 2) // 22, window, 0)
     reference_spectra(table_ref, spec_ref, rcols_ref, chips_ref, half_ref)
 
 
-def own_side(place, sec, starts, taps, src, own, ref, table):
+def own_side(sec, starts, taps, src, own, ref, table):
     return pl.pallas_call(
         own_kernel,
         out_shape=(
@@ -242,7 +238,7 @@
             jax.ShapeDtypeStruct((OWNERS * 8, 4 * LINES), BF),
             jax.ShapeDtypeStruct((PAIRS * CHIP_LEN, 256), F32),
         ),
-        in_specs=[smem] + [hbm] * 3 + [vmem] * 2 + [hbm] * 2,
+        in_specs=[hbm] * 3 + [vmem] * 2 + [hbm] * 2,
         out_specs=(vmem,) * 3,
         scratch_shapes=[
             pltpu.VMEM((2 * LINES, COLS), BF),
@@ -260,11 +256,11 @@
             flops=2 * 10**9, bytes_accessed=6 * 10**6, transcendentals=0
         ),
         name="own_side",
-    )(place, sec, starts, taps, src, own, ref, table)
-
-
-def rims_kernel(place_ref, sec_hbm, mate_ref, other_ref, sems):
-    odd = place_ref[0] & 1
+    )(sec, starts, taps, src, own, ref, table)
+
+
+def rims_kernel(sec_hbm, mate_ref, other_ref, sems):
+    odd = lax.axis_index("az") & 1
     pairs = []
     for to_ref, at in ((other_ref, odd), (mate_ref, 1 - odd)):
         first = at * (LINES - MARGIN)
@@ -280,22 +276,25 @@
         copy.wait()
 
 
-def rims(place, sec):
+def rims(sec):
     rows = jax.ShapeDtypeStruct((2, MARGIN, COLS), BF)
     return pl.pallas_call(
         rims_kernel,
         out_shape=(rows, rows),
-        in_specs=[smem, hbm],
+        in_specs=[hbm],
         out_specs=(hbm, hbm),
         scratch_shapes=[pltpu.SemaphoreType.DMA((8,))],
         compiler_params=pltpu.CompilerParams(vmem_limit_bytes=RIM_VMEM),
+        cost_estimate=pl.CostEstimate(
+            flops=4 * 10**9, bytes_accessed=4 * 10**6, transcendentals=0
+        ),
         name="rims",
-    )(place, sec)
-
-
-def edges_kernel(place_ref, ref_hbm, sec_hbm, near_ref, far_ref, mate_ref, other_ref, sems):
-    odd_rows = place_ref[0] & 1
-    odd = place_ref[1] & 1
+    )(sec)
+
+
+def edges_kernel(ref_hbm, sec_hbm, near_ref, far_ref, mate_ref, other_ref, sems):
+    odd_rows = lax.axis_index("az") & 1
+    odd = lax.axis_index("rg") & 1
     own = CHIP_LEN + MARGIN
     pairs = []
     sides = []
@@ -319,17 +318,20 @@
         copy.wait()
 
 
-def rg_edges(place, ref, sec, near, far):
+def rg_edges(ref, sec, near, far):
     cols = jax.ShapeDtypeStruct((2, CHIP_LEN + ROWS, 128), BF)
     return pl.pallas_call(
         edges_kernel,
         out_shape=(cols, cols),
-        in_specs=[smem, hbm, hbm, vmem, vmem],
+        in_specs=[hbm, hbm, vmem, vmem],
         out_specs=(vmem, vmem),
         scratch_shapes=[pltpu.SemaphoreType.DMA((4,))],
         compiler_params=pltpu.CompilerParams(vmem_limit_bytes=8 * 2**20),
+        cost_estimate=pl.CostEstimate(
+            flops=4 * 10**9, bytes_accessed=4 * 10**6, transcendentals=0
+        ),
         name="rg_edges",
-    )(place, ref, sec, near, far)
+    )(ref, sec, near, far)
 
 
 def side_by_side(half, pairs):
@@ -372,13 +374,15 @@
         def block(at):
             return rcols_ref[:, pl.ds(pl.multiple_of(at * 128, 128), 128)].astype(F32)
 
-        near, here, far = block(step), block(step + 1), block(step + 2)
-        to = pl.multiple_of(step * 256, 256)
-        chips_ref[:, pl.ds(to, 128)] = even_pair(near, here)
-        chips_ref[:, pl.ds(pl.multiple_of(to + 128, 128), 128)] = odd_pair(here, far)
+        for member in range(4):
+            first = step * 4 + member
+            near, here, far = block(first), block(first + 1), block(first + 2)
+            to = pl.multiple_of(first * 256, 256)
+            chips_ref[:, pl.ds(to, 128)] = even_pair(near, here)
+            chips_ref[:, pl.ds(pl.multiple_of(to + 128, 128), 128)] = odd_pair(here, far)
         return carry
 
-    lax.fori_loop(0, PAIRS // 2, cut, 0)
+    lax.fori_loop(0, PAIRS // 8, cut, 0)
     first_pass(table_ref, chips_ref, half_ref)
 
     for step in range(PAIRS // GROUP):
@@ -439,7 +443,6 @@
 
 
 def inner_kernel(
-    place_ref,
     off_ref,
     sec_hbm,
     near_ref,
@@ -456,14 +459,14 @@
     sems,
 ):
     fetch = begin(sems, (sec_hbm, sec_ref), (table_hbm, table_ref))
-    odd = place_ref[0] & 1
+    odd = lax.axis_index("az") & 1
     none = jnp.zeros((2 * ROWS, 128), F32)
     for block in (0, SCRATCH_BLOCKS - 2, SCRATCH_BLOCKS - 1):
         scols_ref[block] = none
 
     def widen_rims(step, carry):
-        for member in range(2):
-            block = step * 2 + member
+        for member in range(4):
+            block = step * 4 + member
             at = pl.ds(pl.multiple_of(block * 128, 128), 128)
             for part in range(2):
                 for rows_ref, low in ((near_ref, 1 - odd), (far_ref, odd)):
@@ -473,31 +476,31 @@
                     )
         return carry
 
-    lax.fori_loop(0, BLOCKS // 2, widen_rims, 0)
+    lax.fori_loop(0, BLOCKS // 4, widen_rims, 0)
     for copy in fetch:
         copy.wait()
 
     def widen(step, carry):
-        for member in range(2):
-            block = step * 2 + member
+        for member in range(4):
+            block = step * 4 + member
             at = pl.ds(pl.multiple_of(block * 128, 128), 128)
             for part in range(2):
                 own = part * ROWS + MARGIN
                 scols_ref[block + 1, own : own + LINES, :] = sec_ref[part, :, at].astype(F32)
         return carry
 
-    lax.fori_loop(0, BLOCKS // 2, widen, 0)
+    lax.fori_loop(0, BLOCKS // 4, widen, 0)
 
     def cut(step, carry):
-        for member in range(2):
-            pair = step * 2 + member
+        for member in range(8):
+            pair = step * 8 + member
             to = pl.ds(pl.multiple_of(pair * 128, 128), 128)
             re, im = cut_pair(off_ref, scols_ref, pair, 0)
             chips_ref[0:CHIP_LEN, to] = re
             chips_ref[CHIP_LEN : 2 * CHIP_LEN, to] = im
         return carry
 
-    lax.fori_loop(0, PAIRS // 2, cut, 0)
+    lax.fori_loop(0, PAIRS // 8, cut, 0)
     first_pass(table_ref, chips_ref, half_ref)
 
     def correlate(step, carry):
@@ -517,12 +520,12 @@
     lax.fori_loop(0, PAIRS // GROUP, correlate, 0)
 
 
-def inner_pairs(place, off, sec, near, far, table, spectra):
+def inner_pairs(off, sec, near, far, table, spectra):
     sums = jax.ShapeDtypeStruct((PAIRS, 128), F32)
     return pl.pallas_call(
         inner_kernel,
         out_shape=(sums, sums),
-        in_specs=[smem, smem, hbm, vmem, vmem, hbm, vmem],
+        in_specs=[smem, hbm, vmem, vmem, hbm, vmem],
         out_specs=(vmem, vmem),
         scratch_shapes=[
             pltpu.VMEM((2, LINES, COLS), BF),
@@ -537,11 +540,10 @@
             flops=6 * 10**9, bytes_accessed=20 * 10**6, transcendentals=0
         ),
         name="inner_pairs",
-    )(place, off, sec, near, far, table, spectra)
+    )(off, sec, near, far, table, spectra)
 
 
 def finish_kernel(
-    place_ref,
     off_ref,
     offv_ref,
     sent_mate_ref,
@@ -573,7 +575,7 @@
     sems,
     out_sems,
 ):
-    rg = place_ref[1]
+    rg = lax.axis_index("rg")
     fetch_table = begin(table_sem, (table_hbm, table_ref))
     fetch = begin(
         sems,
@@ -737,14 +739,14 @@
         copy.wait()
 
 
-def finish(place, off, *arrays):
+def finish(off, *arrays):
     return pl.pallas_call(
         finish_kernel,
         out_shape=(
             jax.ShapeDtypeStruct((2, 128), F32),
             jax.ShapeDtypeStruct((OWNERS * 8, WIDTH), BF),
         ),
-        in_specs=[smem] * 2 + [vmem] * 5 + [hbm] * 4 + [vmem] * 2 + [hbm] * 2,
+        in_specs=[smem] + [vmem] * 5 + [hbm] * 4 + [vmem] * 2 + [hbm] * 2,
         out_specs=(vmem, hbm),
         scratch_shapes=[
             pltpu.VMEM((2 * LINES, COLS), F32),
@@ -767,34 +769,36 @@
             flops=2 * 10**9, bytes_accessed=10 * 10**6, transcendentals=0
         ),
         name="finish",
-    )(place, off, off, *arrays)
+    )(off, off, *arrays)
 
 
 def place_kernel(pick_ref, arr_ref, out_ref):
     pick = pick_ref[...]
     for first in range(0, WIDTH, 256):
-        lines = jnp.dot(
-            pick,
-            arr_ref[:, 0, :, first : first + 256].reshape(128, 256),
-            preferred_element_type=F32,
-        ).astype(BF)
-        for half in range(2):
-            at = slice(half * WIDTH + first, half * WIDTH + first + 256)
-            for part in range(2):
-                base = half * 64 + part * OWNER_CAP
-                out_ref[part, :, at] = lines[base : base + OWNER_CAP, :]
+        for piece in range(PLACED):
+            lines = jnp.dot(
+                pick,
+                arr_ref[:, piece, :, first : first + 256].reshape(128, 256),
+                preferred_element_type=F32,
+            ).astype(BF)
+            for half in range(2):
+                begin_at = piece * COLS + half * WIDTH + first
+                at = slice(begin_at, begin_at + 256)
+                for part in range(2):
+                    base = half * 64 + part * OWNER_CAP
+                    out_ref[part, :, at] = lines[base : base + OWNER_CAP, :]
 
 
 def place_lines(pick, arrived):
     return pl.pallas_call(
         place_kernel,
-        grid=(PIECES,),
+        grid=(PIECES // PLACED,),
         out_shape=jax.ShapeDtypeStruct((2, OWNER_CAP, COLS * PIECES), BF),
         in_specs=[
             pl.BlockSpec((128, 128), lambda r: (0, 0)),
-            pl.BlockSpec((TILES, 1, 8, WIDTH), lambda r: (0, r, 0, 0)),
+            pl.BlockSpec((TILES, PLACED, 8, WIDTH), lambda r: (0, r, 0, 0)),
         ],
-        out_specs=pl.BlockSpec((2, OWNER_CAP, COLS), lambda r: (0, 0, r)),
+        out_specs=pl.BlockSpec((2, OWNER_CAP, PLACED * COLS), lambda r: (0, 0, r)),
         compiler_params=pltpu.CompilerParams(vmem_limit_bytes=20 * 2**20),
         cost_estimate=pl.CostEstimate(
             flops=10**9, bytes_accessed=8 * 10**6, transcendentals=0
@@ -839,12 +843,10 @@
 ):
     az = lax.axis_index("az")
     rg = lax.axis_index("rg")
-    place = jnp.stack([az, rg]).astype(jnp.int32)
     starts = band_start.reshape(PIECES * BLOCKS, 128)
     table = kernel_table()
-    near, far = exchanged("az", *rims(place, secondary_slc))
+    near, far = exchanged("az", *rims(secondary_slc))
     summed, pick_sent, spectra = own_side(
-        place,
         secondary_slc.reshape(2 * LINES, COLS),
         starts,
         band_taps,
@@ -853,12 +855,11 @@
         reference_slc,
         table,
     )
-    sent = rg_edges(place, reference_slc, secondary_slc, near, far)
+    sent = rg_edges(reference_slc, secondary_slc, near, far)
     got = exchanged("rg", *sent)
     off = chip_offsets[:, 0, :]
-    total, moment = inner_pairs(place, off, secondary_slc, near, far, table, spectra)
+    total, moment = inner_pairs(off, secondary_slc, near, far, table, spectra)
     est, packed = finish(
-        place,
         off,
         *sent,
         *got,

time: 105 us -> 91.7 us (0.87)
  Pallas kernels: 34.8 us -> 23.2 us
  local copies, waits for them, and re-layouts: 8.26 us -> 2.94 us
  starting transfers between devices: 19.1 us -> 23.5 us
    pallas_call x4, Pallas kernels: 16.5 us -> 10.5 us  [the longest x1 5.71 us: inner_pairs(): pl.pallas_call(inner_kernel, out_shape=(sums, sums), in_specs=[smem, hbm,...]
    pallas_call x1, Pallas kernels: 11.5 us -> 5.98 us  [own_side(): pl.pallas_call(own_kernel, out_shape=(jax.ShapeDtypeStruct((2 * LINES, CO...]
    unnamed x32 -> x22, local copies, waits for them, and re-layouts: 8.17 us -> 2.85 us
    all_to_all x1, starting transfers between devices: 16 us -> 20.5 us  [per_device(): arrived = lax.all_to_all(packed, BOTH, 0, 0, tiled=True)]
  transfers between devices with their start and end apart: 5 -> 5, of which waited for: 1 -> 1; matrix products, arithmetic and copies ran while one was open for 4% -> 5% of each run, Pallas kernels for 19% -> 13%
where the time goes in v6:
time: 91.7 us; the launch traced here: 91.5 us
  waiting for transfers between devices  36.4 us (40%)
  starting transfers between devices  23.5 us (26%)
  Pallas kernels  23.2 us (25%)
  other arithmetic  4.43 us (5%)
  local copies, waits for them, and re-layouts  2.94 us (3%)
    all_to_all x1, waiting for transfers between devices, per_device(): arrived = lax.all_to_all(packed, BOTH, 0, 0, tiled=True)  36.4 us
    all_to_all x1, starting transfers between devices, per_device(): arrived = lax.all_to_all(packed, BOTH, 0, 0, tiled=True)  20.5 us
    pallas_call x1, Pallas kernels, finish(): pl.pallas_call(finish_kernel, out_shape=(jax.ShapeDtypeStruct((2, 128), F...  6.8 us
    pallas_call x1, Pallas kernels, own_side(): pl.pallas_call(own_kernel, out_shape=(jax.ShapeDtypeStruct((2 * LINES, CO...  5.98 us
    pallas_call x1, Pallas kernels, inner_pairs(): pl.pallas_call(inner_kernel, out_shape=(sums, sums), in_specs=[smem, hbm,...  5.71 us
    reduce_sum x1, other arithmetic, owner_table(): rank = jnp.sum(before.astype(jnp.int32), axis=1)  4.11 us
    ppermute x4, starting transfers between devices, swap(): return lax.ppermute(block, axis, pairs + [(j, i) for i, j in pairs])  3.03 us
    unnamed x22, local copies, waits for them, and re-layouts  2.85 us
  transfers between devices with their start and end apart: 5, of which 1 were waited for; matrix products, arithmetic and copies ran while one was open for 5% of the time, Pallas kernels for 13%

profile of v6, /device:TPU:0, one launch (start us, length us, event | category | flops | bytes accessed | tf_op | source)
XLA Modules:
  0.0 91.5 jit_solution(8340571583034936452)
XLA Ops:
  0.6 0.0 copy-start.2
  0.6 0.0 copy-start
  0.7 0.0 copy-start.1
  0.7 0.0 copy-start.3
  0.7 1.4 %copy-done.3 = bf16[2,96,3072]{2,1,0:T(8,128)(2,1)S(1)} copy-done((bf16[2,96,3072]{2,1,0:T(8,128)(2,1)S(1)}, bf16[2,96,3072]{2,1,0:T(8,128)(2,1)}, u32[]{:S(2)}) %copy-start.3) | copy-done | bytes 1179672
  2.0 2.1 %rims.1 = (bf16[2,64,3072]{2,1,0:T(8,128)(2,1)S(1)}, bf16[2,64,3072]{2,1,0:T(8,128)(2,1)S(1)}) custom-call(bf16[2,96,3072]{2,1,0:T(8,128)(2,1)S(1)} %copy-done.3), custom_call_target="tpu_custom_call" | custom-call | flops 4000000000 | bytes 4000000 | tf_op jit(solution)/shard_map/rims/pallas_call | solution.py:281
  4.2 0.1 collective-permute-start
  4.3 0.7 collective-permute-start.1
  5.0 0.0 copy-done.2
  5.0 0.0 copy-done
  5.0 0.0 copy-done.1
  5.0 0.0 copy-done.4
  5.1 6.0 %own_side.1 = (f32[192,3072]{1,0:T(8,128)S(1)}, bf16[1024,384]{1,0:T(8,128)(2,1)S(1)}, f32[3072,256]{1,0:T(8,128)S(1)}) custom-call(bf16[192,3072]{1,0:T(8,128)(2,1)S(1)} %bitcast.14, s32[192,128]{1,0:T(8,128)S(1)} %bitcast.15, bf16[8,24576]{1,0:T(8,128)(2,1)S(1)} %copy-done.5, s32[12,128]{1,0:T(8,128)S(1)} %bitcast.12, s32[12,128]{1,0:T(8,128)S(1)} %bitcast.13, ...), custom_call_target="tpu_custom_call" | custom-call | flops 2000000000 | bytes 6000000 | tf_op jit(solution)/shard_map/own_side/pallas_call | solution.py:234
  11.1 0.0 copy-start.7
  11.1 0.0 collective-permute-done.near_ref
  11.1 0.0 collective-permute-done.1.far_ref
  11.1 0.1 rg_edges.1
  11.2 1.2 %copy-done.9 = f32[192,3072]{1,0:T(8,128)} copy-done((f32[192,3072]{1,0:T(8,128)}, f32[192,3072]{1,0:T(8,128)S(1)}, u32[]{:S(2)}) %copy-start.9) | copy-done | bytes 2359320
  12.5 0.2 copy-done.10
  12.7 1.6 %collective-permute-start.2 = (bf16[2,288,128]{2,1,0:T(8,128)(2,1)S(1)}, bf16[2,288,128]{2,1,0:T(8,128)(2,1)S(1)}, u32[]{:S(2)}, u32[]{:S(2)}) collective-permute-start(bf16[2,288,128]{2,1,0:T(8,128)(2,1)S(1)} %get-tuple-element.15.sent_mate_ref), channel_id=1, source_target_pairs={{0,1},{2,3},{4,5},{6,7},{1,0},{3,2},{5,4},{7,6},{8,9},{10,11},{12,... | collective-permute-start | bytes 442376 | tf_op jit(solution)/shard_map/ppermute | solution.py:836
  14.3 0.7 collective-permute-start.3
  15.0 5.7 %inner_pairs.1 = (f32[48,128]{1,0:T(8,128)S(1)}, f32[48,128]{1,0:T(8,128)S(1)}) custom-call(s32[2,96]{1,0:T(2,128)S(1)} %bitcast.17, bf16[2,96,3072]{2,1,0:T(8,128)(2,1)S(1)} %copy-done.4, bf16[2,64,3072]{2,1,0:T(8,128)(2,1)S(1)} %collective-permute-done.near_ref, bf16[2,64,3072]{2,1,0:T(8,128)(2,1)S(1)} %collective-permute-done.1.far_ref, ...), custom_call_target="tpu_custom_call" | custom-call | flops 6000000000 | bytes 20000000 | tf_op jit(solution)/shard_map/inner_pairs/pallas_call | solution.py:525
  20.7 0.0 collective-permute-done.2.got_mate_ref
  20.7 0.0 collective-permute-done.3.got_other_ref
  20.7 6.8 %finish.1 = (f32[2,128]{1,0:T(2,128)}, bf16[1024,1536]{1,0:T(8,128)(2,1)}) custom-call(s32[2,96]{1,0:T(2,128)S(1)} %bitcast.18, s32[2,96]{1,0:T(2,128)S(1)} %bitcast.19, bf16[2,288,128]{2,1,0:T(8,128)(2,1)S(1)} %get-tuple-element.15.sent_mate_ref, bf16[2,288,128]{2,1,0:T(8,128)(2,1)S(1)} %get-tuple-element.16.sent_other_ref, ...), custom_call_target="tpu_custom_call" | custom-call | flops 2000000000 | bytes 10000000 | tf_op jit(solution)/shard_map/finish/pallas_call | solution.py:743
  27.5 20.5 %all-to-all-start = ((bf16[128,8,1536]{2,1,0:T(8,128)(2,1)}), bf16[128,8,1536]{2,1,0:T(8,128)(2,1)S(1)}, u32[]{:S(2)}, u32[]{:S(2)}) async-start(bf16[128,8,1536]{2,1,0:T(8,128)(2,1)} %bitcast.20), calls=%async_computation | async-start | bytes 6291456 | tf_op jit(solution)/shard_map/all_to_all | solution.py:875
  48.0 4.1 %convert_reduce_fusion.1 = (s32[1536]{0:T(1024)S(1)}, s32[1536]{0:T(1024)S(1)}) fusion(pred[1536]{0:T(1024)(128)(4,1)S(1)} %broadcast_compare_fusion, s32[1536]{0:T(1024)S(1)} %add_select_fusion), kind=kLoop, calls=%fused_computation.1 | loop fusion | flops 18871296 | bytes 19968 | tf_op jit(solution)/shard_map/reduce_sum | solution.py:815
  52.1 0.2 select_reduce_fusion
  52.3 0.1 eq.81
  52.4 0.1 and_convert_fusion.pick_ref
  52.5 36.4 %all-to-all-done = bf16[128,8,1536]{2,1,0:T(8,128)(2,1)S(1)} async-done(((bf16[128,8,1536]{2,1,0:T(8,128)(2,1)}), bf16[128,8,1536]{2,1,0:T(8,128)(2,1)S(1)}, u32[]{:S(2)}, u32[]{:S(2)}) %all-to-all-start) | async-done | bytes 3145760 | tf_op jit(solution)/shard_map/all_to_all | solution.py:875
  89.0 2.5 %place_lines.1 = bf16[2,32,24576]{2,1,0:T(8,128)(2,1)} custom-call(bf16[128,128]{1,0:T(8,128)(2,1)S(1)} %and_convert_fusion.pick_ref, bf16[16,8,8,1536]{3,2,1,0:T(8,128)(2,1)S(1)} %bitcast.11), custom_call_target="tpu_custom_call" | custom-call | flops 1000000000 | bytes 8000000 | tf_op jit(solution)/shard_map/place_lines/pallas_call | solution.py:793
  (18 shorter events, 0.1 us)
Async XLA Ops:
  0.6 4.4 %copy-start.2 = (bf16[2,96,3072]{2,1,0:T(8,128)(2,1)S(1)}, bf16[2,96,3072]{2,1,0:T(8,128)(2,1)}, u32[]{:S(2)}) copy-start(bf16[2,96,3072]{2,1,0:T(8,128)(2,1)} %ref_hbm.3) | copy-start | bytes 3538948
  0.6 4.4 %copy-start = (s32[1536]{0:T(1024)S(1)}, s32[1536]{0:T(1024)}, u32[]{:S(2)}) copy-start(s32[1536]{0:T(1024)} %param.11) | copy-start | bytes 18436
  0.7 4.4 %copy-start.1 = (s32[1536]{0:T(1024)S(1)}, s32[1536]{0:T(1024)}, u32[]{:S(2)}) copy-start(s32[1536]{0:T(1024)} %param.12) | copy-start | bytes 18436
  0.7 1.4 %copy-start.3 = (bf16[2,96,3072]{2,1,0:T(8,128)(2,1)S(1)}, bf16[2,96,3072]{2,1,0:T(8,128)(2,1)}, u32[]{:S(2)}) copy-start(bf16[2,96,3072]{2,1,0:T(8,128)(2,1)} %sec_hbm.7) | copy-start | bytes 3538948
  2.0 3.0 %copy-start.4 = (bf16[2,96,3072]{2,1,0:T(8,128)(2,1)S(1)}, bf16[2,96,3072]{2,1,0:T(8,128)(2,1)}, u32[]{:S(2)}) copy-start(bf16[2,96,3072]{2,1,0:T(8,128)(2,1)} %sec_hbm.7) | copy-start | bytes 3538948
  2.0 3.0 %copy-start.5 = (bf16[8,24576]{1,0:T(8,128)(2,1)S(1)}, bf16[8,24576]{1,0:T(8,128)(2,1)}, u32[]{:S(2)}) copy-start(bf16[8,24576]{1,0:T(8,128)(2,1)} %taps_hbm.3) | copy-start | bytes 1179652
  2.0 3.0 %copy-start.6 = (s32[24576]{0:T(1024)S(1)}, s32[24576]{0:T(1024)}, u32[]{:S(2)}) copy-start(s32[24576]{0:T(1024)} %param.13) | copy-start | bytes 294916
  2.0 3.0 %copy-start.8 = (bf16[992,256]{1,0:T(8,128)(2,1)S(1)}, bf16[992,256]{1,0:T(8,128)(2,1)}, u32[]{:S(2)}) copy-start(bf16[992,256]{1,0:T(8,128)(2,1)} %constant.39.clone.table_hbm) | copy-start | bytes 1523716
  4.2 6.9 %collective-permute-start = (bf16[2,64,3072]{2,1,0:T(8,128)(2,1)S(1)}, bf16[2,64,3072]{2,1,0:T(8,128)(2,1)S(1)}, u32[]{:S(2)}, u32[]{:S(2)}) collective-permute-start(bf16[2,64,3072]{2,1,0:T(8,128)(2,1)S(1)} %get-tuple-element.13), channel_id=1, source_target_pairs={{0,8},{16,24},{32,40},{48,56},{64,72},{80,88},{96,104},{112,120},{... | collective-permute-start | bytes 2359304 | tf_op jit(solution)/shard_map/ppermute | solution.py:836
  4.3 6.8 %collective-permute-start.1 = (bf16[2,64,3072]{2,1,0:T(8,128)(2,1)S(1)}, bf16[2,64,3072]{2,1,0:T(8,128)(2,1)S(1)}, u32[]{:S(2)}, u32[]{:S(2)}) collective-permute-start(bf16[2,64,3072]{2,1,0:T(8,128)(2,1)S(1)} %get-tuple-element.14), channel_id=1, source_target_pairs={{8,16},{24,32},{40,48},{56,64},{72,80},{88,96},{104,112},{16,8},{3... | collective-permute-start | bytes 2359304 | tf_op jit(solution)/shard_map/ppermute | solution.py:836
  11.0 1.4 %copy-start.9 = (f32[192,3072]{1,0:T(8,128)}, f32[192,3072]{1,0:T(8,128)S(1)}, u32[]{:S(2)}) copy-start(f32[192,3072]{1,0:T(8,128)S(1)} %get-tuple-element.20.sum_hbm) | copy-start | bytes 7077892
  11.1 1.6 %copy-start.10 = (bf16[1024,384]{1,0:T(8,128)(2,1)}, bf16[1024,384]{1,0:T(8,128)(2,1)S(1)}, u32[]{:S(2)}) copy-start(bf16[1024,384]{1,0:T(8,128)(2,1)S(1)} %get-tuple-element.21.pick_hbm) | copy-start | bytes 2359300
  11.1 3.9 %copy-start.7 = (s32[2,1,96]{2,1,0:T(1,128)S(1)}, s32[2,1,96]{2,1,0:T(1,128)}, u32[]{:S(2)}) copy-start(s32[2,1,96]{2,1,0:T(1,128)} %param.10) | copy-start | bytes 2308
  12.7 8.0 %collective-permute-start.2 = (bf16[2,288,128]{2,1,0:T(8,128)(2,1)S(1)}, bf16[2,288,128]{2,1,0:T(8,128)(2,1)S(1)}, u32[]{:S(2)}, u32[]{:S(2)}) collective-permute-start(bf16[2,288,128]{2,1,0:T(8,128)(2,1)S(1)} %get-tuple-element.15.sent_mate_ref), channel_id=1, source_target_pairs={{0,1},{2,3},{4,5},{6,7},{1,0},{3,2},{5,4},{7,6},{8,9},{10,11},{12,... | collective-permute-start | bytes 442376 | tf_op jit(solution)/shard_map/ppermute | solution.py:836
  14.3 6.4 %collective-permute-start.3 = (bf16[2,288,128]{2,1,0:T(8,128)(2,1)S(1)}, bf16[2,288,128]{2,1,0:T(8,128)(2,1)S(1)}, u32[]{:S(2)}, u32[]{:S(2)}) collective-permute-start(bf16[2,288,128]{2,1,0:T(8,128)(2,1)S(1)} %get-tuple-element.16.sent_other_ref), channel_id=1, source_target_pairs={{1,2},{3,4},{5,6},{2,1},{4,3},{6,5},{9,10},{11,12},{13,14},{10,9},... | collective-permute-start | bytes 442376 | tf_op jit(solution)/shard_map/ppermute | solution.py:836
  27.5 61.5 %all-to-all-start = ((bf16[128,8,1536]{2,1,0:T(8,128)(2,1)}), bf16[128,8,1536]{2,1,0:T(8,128)(2,1)S(1)}, u32[]{:S(2)}, u32[]{:S(2)}) async-start(bf16[128,8,1536]{2,1,0:T(8,128)(2,1)} %bitcast.20), calls=%async_computation | async-start | bytes 6291456 | tf_op jit(solution)/shard_map/all_to_all | solution.py:875

commit v7 on v6

--- a/solution.py
+++ b/solution.py
@@ -292,7 +292,7 @@
     )(sec)
 
 
-def edges_kernel(ref_hbm, sec_hbm, near_ref, far_ref, mate_ref, other_ref, sems):
+def edges_kernel(ref_hbm, sec_hbm, far_ref, near_ref, mate_ref, other_ref, sems):
     odd_rows = lax.axis_index("az") & 1
     odd = lax.axis_index("rg") & 1
     own = CHIP_LEN + MARGIN
@@ -331,7 +331,7 @@
             flops=4 * 10**9, bytes_accessed=4 * 10**6, transcendentals=0
         ),
         name="rg_edges",
-    )(ref, sec, near, far)
+    )(ref, sec, far, near)
 
 
 def side_by_side(half, pairs):
@@ -445,8 +445,8 @@
 def inner_kernel(
     off_ref,
     sec_hbm,
+    far_ref,
     near_ref,
-    far_ref,
     table_hbm,
     spec_ref,
     tot_ref,
@@ -540,7 +540,7 @@
             flops=6 * 10**9, bytes_accessed=20 * 10**6, transcendentals=0
         ),
         name="inner_pairs",
-    )(off, sec, near, far, table, spectra)
+    )(off, sec, far, near, table, spectra)
 
 
 def finish_kernel(
@@ -835,7 +835,8 @@
         pairs = [(i, i + 1) for i in range(first, count - 1, 2)]
         return lax.ppermute(block, axis, pairs + [(j, i) for i, j in pairs])
 
-    return swap(mate, 0), swap(other, 1)
+    from_other = swap(other, 1)
+    return swap(mate, 0), from_other
 
 
 def per_device(

time: 91.7 us -> 90.9 us (level)
    all_to_all x1, starting transfers between devices: 20.5 us -> 16.9 us  [per_device(): arrived = lax.all_to_all(packed, BOTH, 0, 0, tiled=True)]
    ppermute x4, starting transfers between devices: 3.03 us -> 5.91 us  [swap(): return lax.ppermute(block, axis, pairs + [(j, i) for i, j in pairs])]
where the time goes in v7:
time: 90.9 us; the launch traced here: 90.7 us
  waiting for transfers between devices  36.4 us (40%)
  Pallas kernels  23.3 us (26%)
  starting transfers between devices  22.8 us (25%)
  other arithmetic  4.43 us (5%)
  local copies, waits for them, and re-layouts  2.94 us (3%)
    all_to_all x1, waiting for transfers between devices, per_device(): arrived = lax.all_to_all(packed, BOTH, 0, 0, tiled=True)  36.4 us
    all_to_all x1, starting transfers between devices, per_device(): arrived = lax.all_to_all(packed, BOTH, 0, 0, tiled=True)  16.9 us
    pallas_call x1, Pallas kernels, finish(): pl.pallas_call(finish_kernel, out_shape=(jax.ShapeDtypeStruct((2, 128), F...  6.8 us
    pallas_call x1, Pallas kernels, own_side(): pl.pallas_call(own_kernel, out_shape=(jax.ShapeDtypeStruct((2 * LINES, CO...  5.99 us
    ppermute x4, starting transfers between devices, swap(): return lax.ppermute(block, axis, pairs + [(j, i) for i, j in pairs])  5.91 us
    pallas_call x1, Pallas kernels, inner_pairs(): pl.pallas_call(inner_kernel, out_shape=(sums, sums), in_specs=[smem, hbm,...  5.71 us
    reduce_sum x1, other arithmetic, owner_table(): rank = jnp.sum(before.astype(jnp.int32), axis=1)  4.11 us
    unnamed x22, local copies, waits for them, and re-layouts  2.85 us
  transfers between devices with their start and end apart: 5, of which 1 were waited for; matrix products, arithmetic and copies ran while one was open for 5% of the time, Pallas kernels for 13%

profile of v7, /device:TPU:0, one launch (start us, length us, event | category | flops | bytes accessed | tf_op | source)
XLA Modules:
  0.0 90.7 jit_solution(6602001662674668618)
XLA Ops:
  0.6 0.0 copy-start.2
  0.6 0.0 copy-start
  0.7 0.0 copy-start.1
  0.7 0.0 copy-start.3
  0.7 1.4 %copy-done.3 = bf16[2,96,3072]{2,1,0:T(8,128)(2,1)S(1)} copy-done((bf16[2,96,3072]{2,1,0:T(8,128)(2,1)S(1)}, bf16[2,96,3072]{2,1,0:T(8,128)(2,1)}, u32[]{:S(2)}) %copy-start.3) | copy-done | bytes 1179672
  2.0 2.1 %rims.1 = (bf16[2,64,3072]{2,1,0:T(8,128)(2,1)S(1)}, bf16[2,64,3072]{2,1,0:T(8,128)(2,1)S(1)}) custom-call(bf16[2,96,3072]{2,1,0:T(8,128)(2,1)S(1)} %copy-done.3), custom_call_target="tpu_custom_call" | custom-call | flops 4000000000 | bytes 4000000 | tf_op jit(solution)/shard_map/rims/pallas_call | solution.py:281
  4.2 0.7 collective-permute-start
  4.9 3.1 %collective-permute-start.1 = (bf16[2,64,3072]{2,1,0:T(8,128)(2,1)S(1)}, bf16[2,64,3072]{2,1,0:T(8,128)(2,1)S(1)}, u32[]{:S(2)}, u32[]{:S(2)}) collective-permute-start(bf16[2,64,3072]{2,1,0:T(8,128)(2,1)S(1)} %get-tuple-element.14), channel_id=1, source_target_pairs={{0,8},{16,24},{32,40},{48,56},{64,72},{80,88},{96,104},{112,120},{... | collective-permute-start | bytes 2359304 | tf_op jit(solution)/shard_map/ppermute | solution.py:836
  7.9 0.0 copy-done.2
  8.0 0.0 copy-done.5
  8.0 0.0 copy-done.6
  8.0 0.0 copy-done.8
  8.0 6.0 %own_side.1 = (f32[192,3072]{1,0:T(8,128)S(1)}, bf16[1024,384]{1,0:T(8,128)(2,1)S(1)}, f32[3072,256]{1,0:T(8,128)S(1)}) custom-call(bf16[192,3072]{1,0:T(8,128)(2,1)S(1)} %bitcast.14, s32[192,128]{1,0:T(8,128)S(1)} %bitcast.15, bf16[8,24576]{1,0:T(8,128)(2,1)S(1)} %copy-done.5, s32[12,128]{1,0:T(8,128)S(1)} %bitcast.12, s32[12,128]{1,0:T(8,128)S(1)} %bitcast.13, ...), custom_call_target="tpu_custom_call" | custom-call | flops 2000000000 | bytes 6000000 | tf_op jit(solution)/shard_map/own_side/pallas_call | solution.py:234
  14.0 0.0 copy-start.7
  14.0 0.0 collective-permute-done.far_ref
  14.0 0.0 collective-permute-done.1.near_ref
  14.0 0.1 rg_edges.1
  14.2 1.2 %copy-done.9 = f32[192,3072]{1,0:T(8,128)} copy-done((f32[192,3072]{1,0:T(8,128)}, f32[192,3072]{1,0:T(8,128)S(1)}, u32[]{:S(2)}) %copy-start.9) | copy-done | bytes 2359320
  15.4 0.2 copy-done.10
  15.6 1.5 %collective-permute-start.2 = (bf16[2,288,128]{2,1,0:T(8,128)(2,1)S(1)}, bf16[2,288,128]{2,1,0:T(8,128)(2,1)S(1)}, u32[]{:S(2)}, u32[]{:S(2)}) collective-permute-start(bf16[2,288,128]{2,1,0:T(8,128)(2,1)S(1)} %get-tuple-element.15.sent_mate_ref), channel_id=1, source_target_pairs={{0,1},{2,3},{4,5},{6,7},{1,0},{3,2},{5,4},{7,6},{8,9},{10,11},{12,... | collective-permute-start | bytes 442376 | tf_op jit(solution)/shard_map/ppermute | solution.py:836
  17.1 0.7 collective-permute-start.3
  17.8 5.7 %inner_pairs.1 = (f32[48,128]{1,0:T(8,128)S(1)}, f32[48,128]{1,0:T(8,128)S(1)}) custom-call(s32[2,96]{1,0:T(2,128)S(1)} %bitcast.17, bf16[2,96,3072]{2,1,0:T(8,128)(2,1)S(1)} %copy-done.4, bf16[2,64,3072]{2,1,0:T(8,128)(2,1)S(1)} %collective-permute-done.far_ref, bf16[2,64,3072]{2,1,0:T(8,128)(2,1)S(1)} %collective-permute-done.1.near_ref, ...), custom_call_target="tpu_custom_call" | custom-call | flops 6000000000 | bytes 20000000 | tf_op jit(solution)/shard_map/inner_pairs/pallas_call | solution.py:525
  23.5 0.0 collective-permute-done.2.got_mate_ref
  23.5 0.0 collective-permute-done.3.got_other_ref
  23.5 6.8 %finish.1 = (f32[2,128]{1,0:T(2,128)}, bf16[1024,1536]{1,0:T(8,128)(2,1)}) custom-call(s32[2,96]{1,0:T(2,128)S(1)} %bitcast.18, s32[2,96]{1,0:T(2,128)S(1)} %bitcast.19, bf16[2,288,128]{2,1,0:T(8,128)(2,1)S(1)} %get-tuple-element.15.sent_mate_ref, bf16[2,288,128]{2,1,0:T(8,128)(2,1)S(1)} %get-tuple-element.16.sent_other_ref, ...), custom_call_target="tpu_custom_call" | custom-call | flops 2000000000 | bytes 10000000 | tf_op jit(solution)/shard_map/finish/pallas_call | solution.py:743
  30.3 16.9 %all-to-all-start = ((bf16[128,8,1536]{2,1,0:T(8,128)(2,1)}), bf16[128,8,1536]{2,1,0:T(8,128)(2,1)S(1)}, u32[]{:S(2)}, u32[]{:S(2)}) async-start(bf16[128,8,1536]{2,1,0:T(8,128)(2,1)} %bitcast.20), calls=%async_computation | async-start | bytes 6291456 | tf_op jit(solution)/shard_map/all_to_all | solution.py:876
  47.2 4.1 %convert_reduce_fusion.1 = (s32[1536]{0:T(1024)S(1)}, s32[1536]{0:T(1024)S(1)}) fusion(pred[1536]{0:T(1024)(128)(4,1)S(1)} %broadcast_compare_fusion, s32[1536]{0:T(1024)S(1)} %add_select_fusion), kind=kLoop, calls=%fused_computation.1 | loop fusion | flops 18871296 | bytes 19968 | tf_op jit(solution)/shard_map/reduce_sum | solution.py:815
  51.4 0.2 select_reduce_fusion
  51.5 0.1 eq.81
  51.6 0.1 and_convert_fusion.pick_ref
  51.8 36.4 %all-to-all-done = bf16[128,8,1536]{2,1,0:T(8,128)(2,1)S(1)} async-done(((bf16[128,8,1536]{2,1,0:T(8,128)(2,1)}), bf16[128,8,1536]{2,1,0:T(8,128)(2,1)S(1)}, u32[]{:S(2)}, u32[]{:S(2)}) %all-to-all-start) | async-done | bytes 3145760 | tf_op jit(solution)/shard_map/all_to_all | solution.py:876
  88.2 2.5 %place_lines.1 = bf16[2,32,24576]{2,1,0:T(8,128)(2,1)} custom-call(bf16[128,128]{1,0:T(8,128)(2,1)S(1)} %and_convert_fusion.pick_ref, bf16[16,8,8,1536]{3,2,1,0:T(8,128)(2,1)S(1)} %bitcast.11), custom_call_target="tpu_custom_call" | custom-call | flops 1000000000 | bytes 8000000 | tf_op jit(solution)/shard_map/place_lines/pallas_call | solution.py:793
  (18 shorter events, 0.1 us)
Async XLA Ops:
  0.6 7.3 %copy-start.2 = (bf16[2,96,3072]{2,1,0:T(8,128)(2,1)S(1)}, bf16[2,96,3072]{2,1,0:T(8,128)(2,1)}, u32[]{:S(2)}) copy-start(bf16[2,96,3072]{2,1,0:T(8,128)(2,1)} %ref_hbm.3) | copy-start | bytes 3538948
  0.6 7.3 %copy-start = (s32[1536]{0:T(1024)S(1)}, s32[1536]{0:T(1024)}, u32[]{:S(2)}) copy-start(s32[1536]{0:T(1024)} %param.11) | copy-start | bytes 18436
  0.7 7.3 %copy-start.1 = (s32[1536]{0:T(1024)S(1)}, s32[1536]{0:T(1024)}, u32[]{:S(2)}) copy-start(s32[1536]{0:T(1024)} %param.12) | copy-start | bytes 18436
  0.7 1.4 %copy-start.3 = (bf16[2,96,3072]{2,1,0:T(8,128)(2,1)S(1)}, bf16[2,96,3072]{2,1,0:T(8,128)(2,1)}, u32[]{:S(2)}) copy-start(bf16[2,96,3072]{2,1,0:T(8,128)(2,1)} %sec_hbm.7) | copy-start | bytes 3538948
  2.0 5.9 %copy-start.4 = (bf16[2,96,3072]{2,1,0:T(8,128)(2,1)S(1)}, bf16[2,96,3072]{2,1,0:T(8,128)(2,1)}, u32[]{:S(2)}) copy-start(bf16[2,96,3072]{2,1,0:T(8,128)(2,1)} %sec_hbm.7) | copy-start | bytes 3538948
  2.0 5.9 %copy-start.5 = (bf16[8,24576]{1,0:T(8,128)(2,1)S(1)}, bf16[8,24576]{1,0:T(8,128)(2,1)}, u32[]{:S(2)}) copy-start(bf16[8,24576]{1,0:T(8,128)(2,1)} %taps_hbm.3) | copy-start | bytes 1179652
  2.0 5.9 %copy-start.6 = (s32[24576]{0:T(1024)S(1)}, s32[24576]{0:T(1024)}, u32[]{:S(2)}) copy-start(s32[24576]{0:T(1024)} %param.13) | copy-start | bytes 294916
  2.0 5.9 %copy-start.8 = (bf16[992,256]{1,0:T(8,128)(2,1)S(1)}, bf16[992,256]{1,0:T(8,128)(2,1)}, u32[]{:S(2)}) copy-start(bf16[992,256]{1,0:T(8,128)(2,1)} %constant.39.clone.table_hbm) | copy-start | bytes 1523716
  4.2 9.8 %collective-permute-start = (bf16[2,64,3072]{2,1,0:T(8,128)(2,1)S(1)}, bf16[2,64,3072]{2,1,0:T(8,128)(2,1)S(1)}, u32[]{:S(2)}, u32[]{:S(2)}) collective-permute-start(bf16[2,64,3072]{2,1,0:T(8,128)(2,1)S(1)} %get-tuple-element.13), channel_id=1, source_target_pairs={{8,16},{24,32},{40,48},{56,64},{72,80},{88,96},{104,112},{16,8},{3... | collective-permute-start | bytes 2359304 | tf_op jit(solution)/shard_map/ppermute | solution.py:836
  4.9 9.1 %collective-permute-start.1 = (bf16[2,64,3072]{2,1,0:T(8,128)(2,1)S(1)}, bf16[2,64,3072]{2,1,0:T(8,128)(2,1)S(1)}, u32[]{:S(2)}, u32[]{:S(2)}) collective-permute-start(bf16[2,64,3072]{2,1,0:T(8,128)(2,1)S(1)} %get-tuple-element.14), channel_id=1, source_target_pairs={{0,8},{16,24},{32,40},{48,56},{64,72},{80,88},{96,104},{112,120},{... | collective-permute-start | bytes 2359304 | tf_op jit(solution)/shard_map/ppermute | solution.py:836
  14.0 1.4 %copy-start.9 = (f32[192,3072]{1,0:T(8,128)}, f32[192,3072]{1,0:T(8,128)S(1)}, u32[]{:S(2)}) copy-start(f32[192,3072]{1,0:T(8,128)S(1)} %get-tuple-element.20.sum_hbm) | copy-start | bytes 7077892
  14.0 1.6 %copy-start.10 = (bf16[1024,384]{1,0:T(8,128)(2,1)}, bf16[1024,384]{1,0:T(8,128)(2,1)S(1)}, u32[]{:S(2)}) copy-start(bf16[1024,384]{1,0:T(8,128)(2,1)S(1)} %get-tuple-element.21.pick_hbm) | copy-start | bytes 2359300
  14.0 3.8 %copy-start.7 = (s32[2,1,96]{2,1,0:T(1,128)S(1)}, s32[2,1,96]{2,1,0:T(1,128)}, u32[]{:S(2)}) copy-start(s32[2,1,96]{2,1,0:T(1,128)} %param.10) | copy-start | bytes 2308
  15.6 7.9 %collective-permute-start.2 = (bf16[2,288,128]{2,1,0:T(8,128)(2,1)S(1)}, bf16[2,288,128]{2,1,0:T(8,128)(2,1)S(1)}, u32[]{:S(2)}, u32[]{:S(2)}) collective-permute-start(bf16[2,288,128]{2,1,0:T(8,128)(2,1)S(1)} %get-tuple-element.15.sent_mate_ref), channel_id=1, source_target_pairs={{0,1},{2,3},{4,5},{6,7},{1,0},{3,2},{5,4},{7,6},{8,9},{10,11},{12,... | collective-permute-start | bytes 442376 | tf_op jit(solution)/shard_map/ppermute | solution.py:836
  17.1 6.4 %collective-permute-start.3 = (bf16[2,288,128]{2,1,0:T(8,128)(2,1)S(1)}, bf16[2,288,128]{2,1,0:T(8,128)(2,1)S(1)}, u32[]{:S(2)}, u32[]{:S(2)}) collective-permute-start(bf16[2,288,128]{2,1,0:T(8,128)(2,1)S(1)} %get-tuple-element.16.sent_other_ref), channel_id=1, source_target_pairs={{1,2},{3,4},{5,6},{2,1},{4,3},{6,5},{9,10},{11,12},{13,14},{10,9},... | collective-permute-start | bytes 442376 | tf_op jit(solution)/shard_map/ppermute | solution.py:836
  30.3 57.8 %all-to-all-start = ((bf16[128,8,1536]{2,1,0:T(8,128)(2,1)}), bf16[128,8,1536]{2,1,0:T(8,128)(2,1)S(1)}, u32[]{:S(2)}, u32[]{:S(2)}) async-start(bf16[128,8,1536]{2,1,0:T(8,128)(2,1)} %bitcast.20), calls=%async_computation | async-start | bytes 6291456 | tf_op jit(solution)/shard_map/all_to_all | solution.py:876

commit v8 on v7

--- a/solution.py
+++ b/solution.py
@@ -34,7 +34,7 @@
 WIDTH = HALF * 128
 LINE_SPAN = 256
 SCRATCH_BLOCKS = BLOCKS + 3
-GROUP = 24
+GROUP = 48
 BAND_ROWS = 64
 PLACED = 4
 TABLE = (992, 256)
@@ -374,15 +374,15 @@
         def block(at):
             return rcols_ref[:, pl.ds(pl.multiple_of(at * 128, 128), 128)].astype(F32)
 
-        for member in range(4):
-            first = step * 4 + member
+        for member in range(12):
+            first = step * 12 + member
             near, here, far = block(first), block(first + 1), block(first + 2)
             to = pl.multiple_of(first * 256, 256)
             chips_ref[:, pl.ds(to, 128)] = even_pair(near, here)
             chips_ref[:, pl.ds(pl.multiple_of(to + 128, 128), 128)] = odd_pair(here, far)
         return carry
 
-    lax.fori_loop(0, PAIRS // 8, cut, 0)
+    lax.fori_loop(0, PAIRS // 24, cut, 0)
     first_pass(table_ref, chips_ref, half_ref)
 
     for step in range(PAIRS // GROUP):
@@ -465,8 +465,8 @@
         scols_ref[block] = none
 
     def widen_rims(step, carry):
-        for member in range(4):
-            block = step * 4 + member
+        for member in range(12):
+            block = step * 12 + member
             at = pl.ds(pl.multiple_of(block * 128, 128), 128)
             for part in range(2):
                 for rows_ref, low in ((near_ref, 1 - odd), (far_ref, odd)):
@@ -476,31 +476,31 @@
                     )
         return carry
 
-    lax.fori_loop(0, BLOCKS // 4, widen_rims, 0)
+    lax.fori_loop(0, BLOCKS // 12, widen_rims, 0)
     for copy in fetch:
         copy.wait()
 
     def widen(step, carry):
-        for member in range(4):
-            block = step * 4 + member
+        for member in range(12):
+            block = step * 12 + member
             at = pl.ds(pl.multiple_of(block * 128, 128), 128)
             for part in range(2):
                 own = part * ROWS + MARGIN
                 scols_ref[block + 1, own : own + LINES, :] = sec_ref[part, :, at].astype(F32)
         return carry
 
-    lax.fori_loop(0, BLOCKS // 4, widen, 0)
+    lax.fori_loop(0, BLOCKS // 12, widen, 0)
 
     def cut(step, carry):
-        for member in range(8):
-            pair = step * 8 + member
+        for member in range(16):
+            pair = step * 16 + member
             to = pl.ds(pl.multiple_of(pair * 128, 128), 128)
             re, im = cut_pair(off_ref, scols_ref, pair, 0)
             chips_ref[0:CHIP_LEN, to] = re
             chips_ref[CHIP_LEN : 2 * CHIP_LEN, to] = im
         return carry
 
-    lax.fori_loop(0, PAIRS // 8, cut, 0)
+    lax.fori_loop(0, PAIRS // 16, cut, 0)
     first_pass(table_ref, chips_ref, half_ref)
 
     def correlate(step, carry):

time: 90.9 us -> 90.2 us (level)
  Pallas kernels: 23.3 us -> 22.2 us
  transfers between devices with their start and end apart: 5 -> 5, of which waited for: 1 -> 1; matrix products, arithmetic and copies ran while one was open for 5% -> 5% of each run, Pallas kernels for 13% -> 12%
where the time goes in v8:
time: 90.2 us; the launch traced here: 90 us
  waiting for transfers between devices  36.4 us (40%)
  starting transfers between devices  23.1 us (26%)
  Pallas kernels  22.2 us (25%)
  other arithmetic  4.43 us (5%)
  local copies, waits for them, and re-layouts  2.94 us (3%)
    all_to_all x1, waiting for transfers between devices, per_device(): arrived = lax.all_to_all(packed, BOTH, 0, 0, tiled=True)  36.4 us
    all_to_all x1, starting transfers between devices, per_device(): arrived = lax.all_to_all(packed, BOTH, 0, 0, tiled=True)  17.2 us
    pallas_call x1, Pallas kernels, finish(): pl.pallas_call(finish_kernel, out_shape=(jax.ShapeDtypeStruct((2, 128), F...  6.8 us
    ppermute x4, starting transfers between devices, swap(): return lax.ppermute(block, axis, pairs + [(j, i) for i, j in pairs])  5.91 us
    pallas_call x1, Pallas kernels, own_side(): pl.pallas_call(own_kernel, out_shape=(jax.ShapeDtypeStruct((2 * LINES, CO...  5.68 us
    pallas_call x1, Pallas kernels, inner_pairs(): pl.pallas_call(inner_kernel, out_shape=(sums, sums), in_specs=[smem, hbm,...  4.95 us
    reduce_sum x1, other arithmetic, owner_table(): rank = jnp.sum(before.astype(jnp.int32), axis=1)  4.11 us
    unnamed x22, local copies, waits for them, and re-layouts  2.85 us
  transfers between devices with their start and end apart: 5, of which 1 were waited for; matrix products, arithmetic and copies ran while one was open for 5% of the time, Pallas kernels for 12%

profile of v8, /device:TPU:0, one launch (start us, length us, event | category | flops | bytes accessed | tf_op | source)
XLA Modules:
  0.0 90.0 jit_solution(8508170293244970794)
XLA Ops:
  0.6 0.0 copy-start.2
  0.7 0.0 copy-start.3
  0.7 1.4 %copy-done.3 = bf16[2,96,3072]{2,1,0:T(8,128)(2,1)S(1)} copy-done((bf16[2,96,3072]{2,1,0:T(8,128)(2,1)S(1)}, bf16[2,96,3072]{2,1,0:T(8,128)(2,1)}, u32[]{:S(2)}) %copy-start.3) | copy-done | bytes 1179672
  2.0 2.1 %rims.1 = (bf16[2,64,3072]{2,1,0:T(8,128)(2,1)S(1)}, bf16[2,64,3072]{2,1,0:T(8,128)(2,1)S(1)}) custom-call(bf16[2,96,3072]{2,1,0:T(8,128)(2,1)S(1)} %copy-done.3), custom_call_target="tpu_custom_call" | custom-call | flops 4000000000 | bytes 4000000 | tf_op jit(solution)/shard_map/rims/pallas_call | solution.py:281
  4.2 0.7 collective-permute-start
  4.9 3.1 %collective-permute-start.1 = (bf16[2,64,3072]{2,1,0:T(8,128)(2,1)S(1)}, bf16[2,64,3072]{2,1,0:T(8,128)(2,1)S(1)}, u32[]{:S(2)}, u32[]{:S(2)}) collective-permute-start(bf16[2,64,3072]{2,1,0:T(8,128)(2,1)S(1)} %get-tuple-element.14), channel_id=1, source_target_pairs={{0,8},{16,24},{32,40},{48,56},{64,72},{80,88},{96,104},{112,120},{... | collective-permute-start | bytes 2359304 | tf_op jit(solution)/shard_map/ppermute | solution.py:836
  7.9 0.0 copy-done.2
  8.0 0.0 copy-done.5
  8.0 0.0 copy-done.6
  8.0 0.0 copy-done.8
  8.0 5.7 %own_side.1 = (f32[192,3072]{1,0:T(8,128)S(1)}, bf16[1024,384]{1,0:T(8,128)(2,1)S(1)}, f32[3072,256]{1,0:T(8,128)S(1)}) custom-call(bf16[192,3072]{1,0:T(8,128)(2,1)S(1)} %bitcast.14, s32[192,128]{1,0:T(8,128)S(1)} %bitcast.15, bf16[8,24576]{1,0:T(8,128)(2,1)S(1)} %copy-done.5, s32[12,128]{1,0:T(8,128)S(1)} %bitcast.12, s32[12,128]{1,0:T(8,128)S(1)} %bitcast.13, ...), custom_call_target="tpu_custom_call" | custom-call | flops 2000000000 | bytes 6000000 | tf_op jit(solution)/shard_map/own_side/pallas_call | solution.py:234
  13.7 0.0 copy-start.9
  13.7 0.0 copy-start.10
  13.7 0.0 copy-start.7
  13.7 0.0 collective-permute-done.far_ref
  13.7 0.0 collective-permute-done.1.near_ref
  13.7 0.1 rg_edges.1
  13.9 1.2 %copy-done.9 = f32[192,3072]{1,0:T(8,128)} copy-done((f32[192,3072]{1,0:T(8,128)}, f32[192,3072]{1,0:T(8,128)S(1)}, u32[]{:S(2)}) %copy-start.9) | copy-done | bytes 2359320
  15.1 0.2 copy-done.10
  15.3 1.5 %collective-permute-start.2 = (bf16[2,288,128]{2,1,0:T(8,128)(2,1)S(1)}, bf16[2,288,128]{2,1,0:T(8,128)(2,1)S(1)}, u32[]{:S(2)}, u32[]{:S(2)}) collective-permute-start(bf16[2,288,128]{2,1,0:T(8,128)(2,1)S(1)} %get-tuple-element.15.sent_mate_ref), channel_id=1, source_target_pairs={{0,1},{2,3},{4,5},{6,7},{1,0},{3,2},{5,4},{7,6},{8,9},{10,11},{12,... | collective-permute-start | bytes 442376 | tf_op jit(solution)/shard_map/ppermute | solution.py:836
  16.8 0.7 collective-permute-start.3
  17.5 5.0 %inner_pairs.1 = (f32[48,128]{1,0:T(8,128)S(1)}, f32[48,128]{1,0:T(8,128)S(1)}) custom-call(s32[2,96]{1,0:T(2,128)S(1)} %bitcast.17, bf16[2,96,3072]{2,1,0:T(8,128)(2,1)S(1)} %copy-done.4, bf16[2,64,3072]{2,1,0:T(8,128)(2,1)S(1)} %collective-permute-done.far_ref, bf16[2,64,3072]{2,1,0:T(8,128)(2,1)S(1)} %collective-permute-done.1.near_ref, ...), custom_call_target="tpu_custom_call" | custom-call | flops 6000000000 | bytes 20000000 | tf_op jit(solution)/shard_map/inner_pairs/pallas_call | solution.py:525
  22.5 0.0 collective-permute-done.2.got_mate_ref
  22.5 0.0 collective-permute-done.3.got_other_ref
  22.5 6.8 %finish.1 = (f32[2,128]{1,0:T(2,128)}, bf16[1024,1536]{1,0:T(8,128)(2,1)}) custom-call(s32[2,96]{1,0:T(2,128)S(1)} %bitcast.18, s32[2,96]{1,0:T(2,128)S(1)} %bitcast.19, bf16[2,288,128]{2,1,0:T(8,128)(2,1)S(1)} %get-tuple-element.15.sent_mate_ref, bf16[2,288,128]{2,1,0:T(8,128)(2,1)S(1)} %get-tuple-element.16.sent_other_ref, ...), custom_call_target="tpu_custom_call" | custom-call | flops 2000000000 | bytes 10000000 | tf_op jit(solution)/shard_map/finish/pallas_call | solution.py:743
  29.3 17.2 %all-to-all-start = ((bf16[128,8,1536]{2,1,0:T(8,128)(2,1)}), bf16[128,8,1536]{2,1,0:T(8,128)(2,1)S(1)}, u32[]{:S(2)}, u32[]{:S(2)}) async-start(bf16[128,8,1536]{2,1,0:T(8,128)(2,1)} %bitcast.20), calls=%async_computation | async-start | bytes 6291456 | tf_op jit(solution)/shard_map/all_to_all | solution.py:876
  46.5 4.1 %convert_reduce_fusion.1 = (s32[1536]{0:T(1024)S(1)}, s32[1536]{0:T(1024)S(1)}) fusion(pred[1536]{0:T(1024)(128)(4,1)S(1)} %broadcast_compare_fusion, s32[1536]{0:T(1024)S(1)} %add_select_fusion), kind=kLoop, calls=%fused_computation.1 | loop fusion | flops 18871296 | bytes 19968 | tf_op jit(solution)/shard_map/reduce_sum | solution.py:815
  50.6 0.2 select_reduce_fusion
  50.8 0.1 eq.81
  50.9 0.1 and_convert_fusion.pick_ref
  51.0 36.4 %all-to-all-done = bf16[128,8,1536]{2,1,0:T(8,128)(2,1)S(1)} async-done(((bf16[128,8,1536]{2,1,0:T(8,128)(2,1)}), bf16[128,8,1536]{2,1,0:T(8,128)(2,1)S(1)}, u32[]{:S(2)}, u32[]{:S(2)}) %all-to-all-start) | async-done | bytes 3145760 | tf_op jit(solution)/shard_map/all_to_all | solution.py:876
  87.4 2.5 %place_lines.1 = bf16[2,32,24576]{2,1,0:T(8,128)(2,1)} custom-call(bf16[128,128]{1,0:T(8,128)(2,1)S(1)} %and_convert_fusion.pick_ref, bf16[16,8,8,1536]{3,2,1,0:T(8,128)(2,1)S(1)} %bitcast.11), custom_call_target="tpu_custom_call" | custom-call | flops 1000000000 | bytes 8000000 | tf_op jit(solution)/shard_map/place_lines/pallas_call | solution.py:793
  (18 shorter events, 0.1 us)
Async XLA Ops:
  0.6 7.3 %copy-start.2 = (bf16[2,96,3072]{2,1,0:T(8,128)(2,1)S(1)}, bf16[2,96,3072]{2,1,0:T(8,128)(2,1)}, u32[]{:S(2)}) copy-start(bf16[2,96,3072]{2,1,0:T(8,128)(2,1)} %ref_hbm.3) | copy-start | bytes 3538948
  0.6 7.3 %copy-start = (s32[1536]{0:T(1024)S(1)}, s32[1536]{0:T(1024)}, u32[]{:S(2)}) copy-start(s32[1536]{0:T(1024)} %param.11) | copy-start | bytes 18436
  0.7 7.3 %copy-start.1 = (s32[1536]{0:T(1024)S(1)}, s32[1536]{0:T(1024)}, u32[]{:S(2)}) copy-start(s32[1536]{0:T(1024)} %param.12) | copy-start | bytes 18436
  0.7 1.4 %copy-start.3 = (bf16[2,96,3072]{2,1,0:T(8,128)(2,1)S(1)}, bf16[2,96,3072]{2,1,0:T(8,128)(2,1)}, u32[]{:S(2)}) copy-start(bf16[2,96,3072]{2,1,0:T(8,128)(2,1)} %sec_hbm.7) | copy-start | bytes 3538948
  2.0 5.9 %copy-start.4 = (bf16[2,96,3072]{2,1,0:T(8,128)(2,1)S(1)}, bf16[2,96,3072]{2,1,0:T(8,128)(2,1)}, u32[]{:S(2)}) copy-start(bf16[2,96,3072]{2,1,0:T(8,128)(2,1)} %sec_hbm.7) | copy-start | bytes 3538948
  2.0 5.9 %copy-start.5 = (bf16[8,24576]{1,0:T(8,128)(2,1)S(1)}, bf16[8,24576]{1,0:T(8,128)(2,1)}, u32[]{:S(2)}) copy-start(bf16[8,24576]{1,0:T(8,128)(2,1)} %taps_hbm.3) | copy-start | bytes 1179652
  2.0 5.9 %copy-start.6 = (s32[24576]{0:T(1024)S(1)}, s32[24576]{0:T(1024)}, u32[]{:S(2)}) copy-start(s32[24576]{0:T(1024)} %param.13) | copy-start | bytes 294916
  2.0 5.9 %copy-start.8 = (bf16[992,256]{1,0:T(8,128)(2,1)S(1)}, bf16[992,256]{1,0:T(8,128)(2,1)}, u32[]{:S(2)}) copy-start(bf16[992,256]{1,0:T(8,128)(2,1)} %constant.39.clone.table_hbm) | copy-start | bytes 1523716
  4.2 9.5 %collective-permute-start = (bf16[2,64,3072]{2,1,0:T(8,128)(2,1)S(1)}, bf16[2,64,3072]{2,1,0:T(8,128)(2,1)S(1)}, u32[]{:S(2)}, u32[]{:S(2)}) collective-permute-start(bf16[2,64,3072]{2,1,0:T(8,128)(2,1)S(1)} %get-tuple-element.13), channel_id=1, source_target_pairs={{8,16},{24,32},{40,48},{56,64},{72,80},{88,96},{104,112},{16,8},{3... | collective-permute-start | bytes 2359304 | tf_op jit(solution)/shard_map/ppermute | solution.py:836
  4.9 8.8 %collective-permute-start.1 = (bf16[2,64,3072]{2,1,0:T(8,128)(2,1)S(1)}, bf16[2,64,3072]{2,1,0:T(8,128)(2,1)S(1)}, u32[]{:S(2)}, u32[]{:S(2)}) collective-permute-start(bf16[2,64,3072]{2,1,0:T(8,128)(2,1)S(1)} %get-tuple-element.14), channel_id=1, source_target_pairs={{0,8},{16,24},{32,40},{48,56},{64,72},{80,88},{96,104},{112,120},{... | collective-permute-start | bytes 2359304 | tf_op jit(solution)/shard_map/ppermute | solution.py:836
  13.7 1.4 %copy-start.9 = (f32[192,3072]{1,0:T(8,128)}, f32[192,3072]{1,0:T(8,128)S(1)}, u32[]{:S(2)}) copy-start(f32[192,3072]{1,0:T(8,128)S(1)} %get-tuple-element.20.sum_hbm) | copy-start | bytes 7077892
  13.7 1.6 %copy-start.10 = (bf16[1024,384]{1,0:T(8,128)(2,1)}, bf16[1024,384]{1,0:T(8,128)(2,1)S(1)}, u32[]{:S(2)}) copy-start(bf16[1024,384]{1,0:T(8,128)(2,1)S(1)} %get-tuple-element.21.pick_hbm) | copy-start | bytes 2359300
  13.7 3.8 %copy-start.7 = (s32[2,1,96]{2,1,0:T(1,128)S(1)}, s32[2,1,96]{2,1,0:T(1,128)}, u32[]{:S(2)}) copy-start(s32[2,1,96]{2,1,0:T(1,128)} %param.10) | copy-start | bytes 2308
  15.3 7.1 %collective-permute-start.2 = (bf16[2,288,128]{2,1,0:T(8,128)(2,1)S(1)}, bf16[2,288,128]{2,1,0:T(8,128)(2,1)S(1)}, u32[]{:S(2)}, u32[]{:S(2)}) collective-permute-start(bf16[2,288,128]{2,1,0:T(8,128)(2,1)S(1)} %get-tuple-element.15.sent_mate_ref), channel_id=1, source_target_pairs={{0,1},{2,3},{4,5},{6,7},{1,0},{3,2},{5,4},{7,6},{8,9},{10,11},{12,... | collective-permute-start | bytes 442376 | tf_op jit(solution)/shard_map/ppermute | solution.py:836
  16.8 5.7 %collective-permute-start.3 = (bf16[2,288,128]{2,1,0:T(8,128)(2,1)S(1)}, bf16[2,288,128]{2,1,0:T(8,128)(2,1)S(1)}, u32[]{:S(2)}, u32[]{:S(2)}) collective-permute-start(bf16[2,288,128]{2,1,0:T(8,128)(2,1)S(1)} %get-tuple-element.16.sent_other_ref), channel_id=1, source_target_pairs={{1,2},{3,4},{5,6},{2,1},{4,3},{6,5},{9,10},{11,12},{13,14},{10,9},... | collective-permute-start | bytes 442376 | tf_op jit(solution)/shard_map/ppermute | solution.py:836
  29.3 58.2 %all-to-all-start = ((bf16[128,8,1536]{2,1,0:T(8,128)(2,1)}), bf16[128,8,1536]{2,1,0:T(8,128)(2,1)S(1)}, u32[]{:S(2)}, u32[]{:S(2)}) async-start(bf16[128,8,1536]{2,1,0:T(8,128)(2,1)} %bitcast.20), calls=%async_computation | async-start | bytes 6291456 | tf_op jit(solution)/shard_map/all_to_all | solution.py:876

commit v9 on v8

--- a/solution.py
+++ b/solution.py
@@ -259,21 +259,12 @@
     )(sec, starts, taps, src, own, ref, table)
 
 
-def rims_kernel(sec_hbm, mate_ref, other_ref, sems):
+def rims_kernel(sec_ref, mate_ref, other_ref):
     odd = lax.axis_index("az") & 1
-    pairs = []
     for to_ref, at in ((other_ref, odd), (mate_ref, 1 - odd)):
-        first = at * (LINES - MARGIN)
+        rows = pl.ds(pl.multiple_of(at * (LINES - MARGIN), 32), MARGIN)
         for part in range(2):
-            for row in range(0, MARGIN, 32):
-                pairs.append(
-                    (
-                        sec_hbm.at[part, pl.ds(pl.multiple_of(first + row, 16), 32), :],
-                        to_ref.at[part, row : row + 32, :],
-                    )
-                )
-    for copy in begin(sems, *pairs):
-        copy.wait()
+            to_ref[part] = sec_ref[part, rows, :]
 
 
 def rims(sec):
@@ -281,9 +272,8 @@
     return pl.pallas_call(
         rims_kernel,
         out_shape=(rows, rows),
-        in_specs=[hbm],
-        out_specs=(hbm, hbm),
-        scratch_shapes=[pltpu.SemaphoreType.DMA((8,))],
+        in_specs=[vmem],
+        out_specs=(vmem, vmem),
         compiler_params=pltpu.CompilerParams(vmem_limit_bytes=RIM_VMEM),
         cost_estimate=pl.CostEstimate(
             flops=4 * 10**9, bytes_accessed=4 * 10**6, transcendentals=0

time: 90.2 us -> 88.3 us (0.979)
  Pallas kernels: 22.2 us -> 20.2 us
    pallas_call x1, Pallas kernels: 2.13 us -> 0.12 us  [rims(): pl.pallas_call(rims_kernel, out_shape=(rows, rows), in_specs=[vmem], out_...]
where the time goes in v9:
time: 88.3 us; the launch traced here: 88.1 us
  waiting for transfers between devices  36.4 us (41%)
  starting transfers between devices  23.2 us (26%)
  Pallas kernels  20.2 us (23%)
  other arithmetic  4.43 us (5%)
  local copies, waits for them, and re-layouts  2.94 us (3%)
    all_to_all x1, waiting for transfers between devices, per_device(): arrived = lax.all_to_all(packed, BOTH, 0, 0, tiled=True)  36.4 us
    all_to_all x1, starting transfers between devices, per_device(): arrived = lax.all_to_all(packed, BOTH, 0, 0, tiled=True)  17.1 us
    pallas_call x1, Pallas kernels, finish(): pl.pallas_call(finish_kernel, out_shape=(jax.ShapeDtypeStruct((2, 128), F...  6.8 us
    ppermute x4, starting transfers between devices, swap(): return lax.ppermute(block, axis, pairs + [(j, i) for i, j in pairs])  6.04 us
    pallas_call x1, Pallas kernels, own_side(): pl.pallas_call(own_kernel, out_shape=(jax.ShapeDtypeStruct((2 * LINES, CO...  5.68 us
    pallas_call x1, Pallas kernels, inner_pairs(): pl.pallas_call(inner_kernel, out_shape=(sums, sums), in_specs=[smem, hbm,...  4.96 us
    reduce_sum x1, other arithmetic, owner_table(): rank = jnp.sum(before.astype(jnp.int32), axis=1)  4.11 us
    unnamed x22, local copies, waits for them, and re-layouts  2.85 us
  transfers between devices with their start and end apart: 5, of which 1 were waited for; matrix products, arithmetic and copies ran while one was open for 5% of the time, Pallas kernels for 12%

profile of v9, /device:TPU:0, one launch (start us, length us, event | category | flops | bytes accessed | tf_op | source)
XLA Modules:
  0.0 88.1 jit_solution(17352733539949270846)
XLA Ops:
  0.6 0.0 copy-start.2
  0.6 0.0 copy-start
  0.7 0.0 copy-start.1
  0.7 0.0 copy-start.3
  0.7 1.4 %copy-done.3 = bf16[2,96,3072]{2,1,0:T(8,128)(2,1)S(1)} copy-done((bf16[2,96,3072]{2,1,0:T(8,128)(2,1)S(1)}, bf16[2,96,3072]{2,1,0:T(8,128)(2,1)}, u32[]{:S(2)}) %copy-start.3) | copy-done | bytes 1179672
  2.0 0.1 rims.1
  2.2 0.8 collective-permute-start
  3.0 3.1 %collective-permute-start.1 = (bf16[2,64,3072]{2,1,0:T(8,128)(2,1)S(1)}, bf16[2,64,3072]{2,1,0:T(8,128)(2,1)S(1)}, u32[]{:S(2)}, u32[]{:S(2)}) collective-permute-start(bf16[2,64,3072]{2,1,0:T(8,128)(2,1)S(1)} %get-tuple-element.14), channel_id=1, source_target_pairs={{0,8},{16,24},{32,40},{48,56},{64,72},{80,88},{96,104},{112,120},{... | collective-permute-start | bytes 2359304 | tf_op jit(solution)/shard_map/ppermute | solution.py:826
  6.1 0.0 copy-done.2
  6.1 0.0 copy-done.5
  6.1 0.0 copy-done.6
  6.1 0.0 copy-done.8
  6.1 5.7 %own_side.1 = (f32[192,3072]{1,0:T(8,128)S(1)}, bf16[1024,384]{1,0:T(8,128)(2,1)S(1)}, f32[3072,256]{1,0:T(8,128)S(1)}) custom-call(bf16[192,3072]{1,0:T(8,128)(2,1)S(1)} %bitcast.14, s32[192,128]{1,0:T(8,128)S(1)} %bitcast.15, bf16[8,24576]{1,0:T(8,128)(2,1)S(1)} %copy-done.5, s32[12,128]{1,0:T(8,128)S(1)} %bitcast.12, s32[12,128]{1,0:T(8,128)S(1)} %bitcast.13, ...), custom_call_target="tpu_custom_call" | custom-call | flops 2000000000 | bytes 6000000 | tf_op jit(solution)/shard_map/own_side/pallas_call | solution.py:234
  11.8 0.0 copy-start.7
  11.8 0.0 collective-permute-done.far_ref
  11.8 0.0 collective-permute-done.1.near_ref
  11.9 0.1 rg_edges.1
  12.0 1.2 %copy-done.9 = f32[192,3072]{1,0:T(8,128)} copy-done((f32[192,3072]{1,0:T(8,128)}, f32[192,3072]{1,0:T(8,128)S(1)}, u32[]{:S(2)}) %copy-start.9) | copy-done | bytes 2359320
  13.2 0.2 copy-done.10
  13.5 1.5 %collective-permute-start.2 = (bf16[2,288,128]{2,1,0:T(8,128)(2,1)S(1)}, bf16[2,288,128]{2,1,0:T(8,128)(2,1)S(1)}, u32[]{:S(2)}, u32[]{:S(2)}) collective-permute-start(bf16[2,288,128]{2,1,0:T(8,128)(2,1)S(1)} %get-tuple-element.15.sent_mate_ref), channel_id=1, source_target_pairs={{0,1},{2,3},{4,5},{6,7},{1,0},{3,2},{5,4},{7,6},{8,9},{10,11},{12,... | collective-permute-start | bytes 442376 | tf_op jit(solution)/shard_map/ppermute | solution.py:826
  14.9 0.7 collective-permute-start.3
  15.6 5.0 %inner_pairs.1 = (f32[48,128]{1,0:T(8,128)S(1)}, f32[48,128]{1,0:T(8,128)S(1)}) custom-call(s32[2,96]{1,0:T(2,128)S(1)} %bitcast.17, bf16[2,96,3072]{2,1,0:T(8,128)(2,1)S(1)} %copy-done.4, bf16[2,64,3072]{2,1,0:T(8,128)(2,1)S(1)} %collective-permute-done.far_ref, bf16[2,64,3072]{2,1,0:T(8,128)(2,1)S(1)} %collective-permute-done.1.near_ref, ...), custom_call_target="tpu_custom_call" | custom-call | flops 6000000000 | bytes 20000000 | tf_op jit(solution)/shard_map/inner_pairs/pallas_call | solution.py:515
  20.6 0.0 collective-permute-done.2.got_mate_ref
  20.6 0.0 collective-permute-done.3.got_other_ref
  20.6 6.8 %finish.1 = (f32[2,128]{1,0:T(2,128)}, bf16[1024,1536]{1,0:T(8,128)(2,1)}) custom-call(s32[2,96]{1,0:T(2,128)S(1)} %bitcast.18, s32[2,96]{1,0:T(2,128)S(1)} %bitcast.19, bf16[2,288,128]{2,1,0:T(8,128)(2,1)S(1)} %get-tuple-element.15.sent_mate_ref, bf16[2,288,128]{2,1,0:T(8,128)(2,1)S(1)} %get-tuple-element.16.sent_other_ref, ...), custom_call_target="tpu_custom_call" | custom-call | flops 2000000000 | bytes 10000000 | tf_op jit(solution)/shard_map/finish/pallas_call | solution.py:733
  27.4 17.1 %all-to-all-start = ((bf16[128,8,1536]{2,1,0:T(8,128)(2,1)}), bf16[128,8,1536]{2,1,0:T(8,128)(2,1)S(1)}, u32[]{:S(2)}, u32[]{:S(2)}) async-start(bf16[128,8,1536]{2,1,0:T(8,128)(2,1)} %bitcast.20), calls=%async_computation | async-start | bytes 6291456 | tf_op jit(solution)/shard_map/all_to_all | solution.py:866
  44.6 4.1 %convert_reduce_fusion.1 = (s32[1536]{0:T(1024)S(1)}, s32[1536]{0:T(1024)S(1)}) fusion(pred[1536]{0:T(1024)(128)(4,1)S(1)} %broadcast_compare_fusion, s32[1536]{0:T(1024)S(1)} %add_select_fusion), kind=kLoop, calls=%fused_computation.1 | loop fusion | flops 18871296 | bytes 19968 | tf_op jit(solution)/shard_map/reduce_sum | solution.py:805
  48.7 0.2 select_reduce_fusion
  48.9 0.1 eq.81
  49.0 0.1 and_convert_fusion.pick_ref
  49.1 36.4 %all-to-all-done = bf16[128,8,1536]{2,1,0:T(8,128)(2,1)S(1)} async-done(((bf16[128,8,1536]{2,1,0:T(8,128)(2,1)}), bf16[128,8,1536]{2,1,0:T(8,128)(2,1)S(1)}, u32[]{:S(2)}, u32[]{:S(2)}) %all-to-all-start) | async-done | bytes 3145760 | tf_op jit(solution)/shard_map/all_to_all | solution.py:866
  85.6 2.5 %place_lines.1 = bf16[2,32,24576]{2,1,0:T(8,128)(2,1)} custom-call(bf16[128,128]{1,0:T(8,128)(2,1)S(1)} %and_convert_fusion.pick_ref, bf16[16,8,8,1536]{3,2,1,0:T(8,128)(2,1)S(1)} %bitcast.11), custom_call_target="tpu_custom_call" | custom-call | flops 1000000000 | bytes 8000000 | tf_op jit(solution)/shard_map/place_lines/pallas_call | solution.py:783
  (18 shorter events, 0.1 us)
Async XLA Ops:
  0.6 5.4 %copy-start.2 = (bf16[2,96,3072]{2,1,0:T(8,128)(2,1)S(1)}, bf16[2,96,3072]{2,1,0:T(8,128)(2,1)}, u32[]{:S(2)}) copy-start(bf16[2,96,3072]{2,1,0:T(8,128)(2,1)} %ref_hbm.3) | copy-start | bytes 3538948
  0.6 5.4 %copy-start = (s32[1536]{0:T(1024)S(1)}, s32[1536]{0:T(1024)}, u32[]{:S(2)}) copy-start(s32[1536]{0:T(1024)} %param.11) | copy-start | bytes 18436
  0.7 5.4 %copy-start.1 = (s32[1536]{0:T(1024)S(1)}, s32[1536]{0:T(1024)}, u32[]{:S(2)}) copy-start(s32[1536]{0:T(1024)} %param.12) | copy-start | bytes 18436
  0.7 1.4 %copy-start.3 = (bf16[2,96,3072]{2,1,0:T(8,128)(2,1)S(1)}, bf16[2,96,3072]{2,1,0:T(8,128)(2,1)}, u32[]{:S(2)}) copy-start(bf16[2,96,3072]{2,1,0:T(8,128)(2,1)} %sec_hbm.5) | copy-start | bytes 3538948
  2.0 4.0 %copy-start.4 = (bf16[2,96,3072]{2,1,0:T(8,128)(2,1)S(1)}, bf16[2,96,3072]{2,1,0:T(8,128)(2,1)}, u32[]{:S(2)}) copy-start(bf16[2,96,3072]{2,1,0:T(8,128)(2,1)} %sec_hbm.5) | copy-start | bytes 3538948
  2.0 4.1 %copy-start.5 = (bf16[8,24576]{1,0:T(8,128)(2,1)S(1)}, bf16[8,24576]{1,0:T(8,128)(2,1)}, u32[]{:S(2)}) copy-start(bf16[8,24576]{1,0:T(8,128)(2,1)} %taps_hbm.3) | copy-start | bytes 1179652
  2.0 4.1 %copy-start.6 = (s32[24576]{0:T(1024)S(1)}, s32[24576]{0:T(1024)}, u32[]{:S(2)}) copy-start(s32[24576]{0:T(1024)} %param.13) | copy-start | bytes 294916
  2.0 4.1 %copy-start.8 = (bf16[992,256]{1,0:T(8,128)(2,1)S(1)}, bf16[992,256]{1,0:T(8,128)(2,1)}, u32[]{:S(2)}) copy-start(bf16[992,256]{1,0:T(8,128)(2,1)} %constant.39.clone.table_hbm) | copy-start | bytes 1523716
  2.2 9.7 %collective-permute-start = (bf16[2,64,3072]{2,1,0:T(8,128)(2,1)S(1)}, bf16[2,64,3072]{2,1,0:T(8,128)(2,1)S(1)}, u32[]{:S(2)}, u32[]{:S(2)}) collective-permute-start(bf16[2,64,3072]{2,1,0:T(8,128)(2,1)S(1)} %get-tuple-element.13), channel_id=1, source_target_pairs={{8,16},{24,32},{40,48},{56,64},{72,80},{88,96},{104,112},{16,8},{3... | collective-permute-start | bytes 2359304 | tf_op jit(solution)/shard_map/ppermute | solution.py:826
  3.0 8.8 %collective-permute-start.1 = (bf16[2,64,3072]{2,1,0:T(8,128)(2,1)S(1)}, bf16[2,64,3072]{2,1,0:T(8,128)(2,1)S(1)}, u32[]{:S(2)}, u32[]{:S(2)}) collective-permute-start(bf16[2,64,3072]{2,1,0:T(8,128)(2,1)S(1)} %get-tuple-element.14), channel_id=1, source_target_pairs={{0,8},{16,24},{32,40},{48,56},{64,72},{80,88},{96,104},{112,120},{... | collective-permute-start | bytes 2359304 | tf_op jit(solution)/shard_map/ppermute | solution.py:826
  11.8 1.4 %copy-start.9 = (f32[192,3072]{1,0:T(8,128)}, f32[192,3072]{1,0:T(8,128)S(1)}, u32[]{:S(2)}) copy-start(f32[192,3072]{1,0:T(8,128)S(1)} %get-tuple-element.20.sum_hbm) | copy-start | bytes 7077892
  11.8 1.6 %copy-start.10 = (bf16[1024,384]{1,0:T(8,128)(2,1)}, bf16[1024,384]{1,0:T(8,128)(2,1)S(1)}, u32[]{:S(2)}) copy-start(bf16[1024,384]{1,0:T(8,128)(2,1)S(1)} %get-tuple-element.21.pick_hbm) | copy-start | bytes 2359300
  11.8 3.8 %copy-start.7 = (s32[2,1,96]{2,1,0:T(1,128)S(1)}, s32[2,1,96]{2,1,0:T(1,128)}, u32[]{:S(2)}) copy-start(s32[2,1,96]{2,1,0:T(1,128)} %param.10) | copy-start | bytes 2308
  13.5 7.1 %collective-permute-start.2 = (bf16[2,288,128]{2,1,0:T(8,128)(2,1)S(1)}, bf16[2,288,128]{2,1,0:T(8,128)(2,1)S(1)}, u32[]{:S(2)}, u32[]{:S(2)}) collective-permute-start(bf16[2,288,128]{2,1,0:T(8,128)(2,1)S(1)} %get-tuple-element.15.sent_mate_ref), channel_id=1, source_target_pairs={{0,1},{2,3},{4,5},{6,7},{1,0},{3,2},{5,4},{7,6},{8,9},{10,11},{12,... | collective-permute-start | bytes 442376 | tf_op jit(solution)/shard_map/ppermute | solution.py:826
  14.9 5.7 %collective-permute-start.3 = (bf16[2,288,128]{2,1,0:T(8,128)(2,1)S(1)}, bf16[2,288,128]{2,1,0:T(8,128)(2,1)S(1)}, u32[]{:S(2)}, u32[]{:S(2)}) collective-permute-start(bf16[2,288,128]{2,1,0:T(8,128)(2,1)S(1)} %get-tuple-element.16.sent_other_ref), channel_id=1, source_target_pairs={{1,2},{3,4},{5,6},{2,1},{4,3},{6,5},{9,10},{11,12},{13,14},{10,9},... | collective-permute-start | bytes 442376 | tf_op jit(solution)/shard_map/ppermute | solution.py:826
  27.4 58.1 %all-to-all-start = ((bf16[128,8,1536]{2,1,0:T(8,128)(2,1)}), bf16[128,8,1536]{2,1,0:T(8,128)(2,1)S(1)}, u32[]{:S(2)}, u32[]{:S(2)}) async-start(bf16[128,8,1536]{2,1,0:T(8,128)(2,1)} %bitcast.20), calls=%async_computation | async-start | bytes 6291456 | tf_op jit(solution)/shard_map/all_to_all | solution.py:866
